TPU v7x, 128 devices: a whole 4x4x4 slice. The times are simulated.
128 devices in a mesh: seq: 16 (over x, y), head: 8 (over z, core).
Axes of the slice: x: 4, y: 4, z: 4, core: 2. Of those that a mesh axis runs over, the one named last changes fastest.
Arguments:
- node_input: bfloat16 [49152, 1024], P(('seq', 'head')), may hold values from -13 to 13
- w_query: bfloat16 [1024, 1024], P(None, 'head'), may hold values from -0.1875 to 0.1875
- w_key: bfloat16 [1024, 1024], P(None, 'head'), may hold values from -0.1875 to 0.1875
- w_value: bfloat16 [1024, 1024], P(None, 'head'), may hold values from -0.1875 to 0.1875
- grad_context: bfloat16 [49152, 1024], P(('seq', 'head')), may hold values from -6 to 6
- key_blocks: int32 [384, 4], P('seq'), may hold values from 0 to 383, as said below
- counts: int32 [384], P('seq'), may hold values from 1 to 4
Outputs:
- grad_input: bfloat16 [49152, 1024], P(('seq', 'head'))
- grad_wq: float32 [1024, 1024], P('seq', 'head')
- grad_wk: float32 [1024, 1024], P('seq', 'head')
- grad_wv: float32 [1024, 1024], P('seq', 'head')
Inputs may be any that keep to these rules, and one draw needn't show every extreme that they name: `key_blocks`: entry 0 of the list of block b is b itself. Block g is owned by seq index g // 24. Among entries 1 to 3 of the lists of the 24 blocks of one seq index, at most 7 name blocks of any one owner; in every draw one owner is named exactly 7 times by every seq index. Entries may repeat.
All inputs are finite; a program needn't handle non-finite values.
Results may differ from a plain program's by a relative error of at most 0.006.
The roundings to bfloat16 on the way count: a program that leaves them out, or rounds other values in their place, can miss the bound.
Values may be sent and summed in bfloat16 or wider, within the bound.
No kernel may reach another device: no remote copies, remote signals or barrier semaphores. Data moves between devices by JAX's collectives and lax.ppermute only.
A program may use at most 128 MiB of HBM per device.

v0:
```python
from functools import partial

import jax
import jax.numpy as jnp
from jax import lax
from jax.sharding import PartitionSpec as P

HDIM = 64
BLOCK = 128
KB = 4


tiles_per_step = 4


def attend_group(tile_group, softmax_scale):
    query_tiles, grad_tiles, key_heads, value_heads, valid_entry = tile_group
    keep_mask = valid_entry[:, None, None, :, None]
    scores = (
        jnp.einsum("bqhd,bjkhd->bhqjk", query_tiles, key_heads, preferred_element_type=jnp.float32)
        * softmax_scale
    )
    row_max = jnp.max(jnp.where(keep_mask, scores, -1e30), axis=(3, 4), keepdims=True)
    unnorm = jnp.where(keep_mask, jnp.exp(scores - row_max), 0.0)
    row_total = jnp.sum(unnorm, axis=(3, 4), keepdims=True)
    probs = unnorm / row_total
    grad_probs = jnp.einsum(
        "bqhd,bjkhd->bhqjk", grad_tiles, value_heads, preferred_element_type=jnp.float32
    )
    delta_rows = jnp.sum(probs * grad_probs, axis=(3, 4), keepdims=True)
    grad_scores = (probs * (grad_probs - delta_rows) * softmax_scale).astype(jnp.bfloat16)
    probs_low = probs.astype(jnp.bfloat16)
    grad_query = jnp.einsum(
        "bhqjk,bjkhd->bqhd", grad_scores, key_heads, preferred_element_type=jnp.float32
    ).astype(jnp.bfloat16)
    part_keys = jnp.einsum(
        "bhqjk,bqhd->bjkhd", grad_scores, query_tiles, preferred_element_type=jnp.float32
    )
    part_values = jnp.einsum(
        "bhqjk,bqhd->bjkhd", probs_low, grad_tiles, preferred_element_type=jnp.float32
    )
    return (grad_query, part_keys, part_values)


def shards(node_input, w_query, w_key, w_value, grad_context, key_blocks, counts):
    n_seq = lax.axis_size("seq")
    gathered = lax.all_gather(node_input, "head", axis=0, tiled=True)
    queries = jnp.dot(gathered, w_query, preferred_element_type=jnp.float32).astype(jnp.bfloat16)
    keys_here = jnp.dot(gathered, w_key, preferred_element_type=jnp.float32).astype(jnp.bfloat16)
    values_here = jnp.dot(gathered, w_value, preferred_element_type=jnp.float32).astype(
        jnp.bfloat16
    )
    upstream = lax.all_to_all(grad_context, "head", split_axis=1, concat_axis=0, tiled=True)
    node_rows = gathered.shape[0]
    head_cols = w_query.shape[1]
    heads_here = head_cols // HDIM
    blocks = node_rows // BLOCK
    softmax_scale = HDIM ** (-0.5)
    capacity = max(2, 3 * blocks * (KB - 1) // (2 * n_seq) + 1)
    slot_count = n_seq * capacity
    remote = key_blocks[:, 1:].reshape(-1)
    owner_of = remote // blocks
    inner_block = remote % blocks
    member = (owner_of[:, None] == jnp.arange(n_seq, dtype=jnp.int32)[None, :]).astype(jnp.int32)
    rank_in = jnp.sum((jnp.cumsum(member, axis=0) - 1) * member, axis=1)
    slot_index = owner_of * capacity + rank_in
    requests = jnp.zeros((slot_count,), jnp.int32).at[slot_index].set(inner_block)
    asked_blocks = lax.all_to_all(requests, "seq", split_axis=0, concat_axis=0, tiled=True)
    key_tiles = keys_here.reshape(blocks, BLOCK, head_cols)
    value_tiles = values_here.reshape(blocks, BLOCK, head_cols)
    served_keys = key_tiles[asked_blocks]
    served_values = value_tiles[asked_blocks]
    fetched_keys, fetched_values = (
        lax.all_to_all(served_keys, "seq", split_axis=0, concat_axis=0, tiled=True),
        lax.all_to_all(served_values, "seq", split_axis=0, concat_axis=0, tiled=True),
    )
    key_set = jnp.concatenate(
        [key_tiles[:, None], fetched_keys[slot_index].reshape(blocks, KB - 1, BLOCK, head_cols)],
        axis=1,
    )
    value_set = jnp.concatenate(
        [
            value_tiles[:, None],
            fetched_values[slot_index].reshape(blocks, KB - 1, BLOCK, head_cols),
        ],
        axis=1,
    )
    valid_entry = jnp.arange(KB, dtype=jnp.int32)[None, :] < counts[:, None]
    step_total = blocks // tiles_per_step

    def grouped(tensor):
        return tensor.reshape((step_total, tiles_per_step) + tensor.shape[1:])

    group_inputs = (
        grouped(queries.reshape(blocks, BLOCK, heads_here, HDIM)),
        grouped(upstream.reshape(blocks, BLOCK, heads_here, HDIM)),
        grouped(key_set.reshape(blocks, KB, BLOCK, heads_here, HDIM)),
        grouped(value_set.reshape(blocks, KB, BLOCK, heads_here, HDIM)),
        grouped(valid_entry),
    )
    results = lax.map(partial(attend_group, softmax_scale=softmax_scale), group_inputs)
    grad_query = results[0].reshape(node_rows, head_cols)
    part_keys = results[1].reshape(blocks, KB, BLOCK, head_cols)
    part_values = results[2].reshape(blocks, KB, BLOCK, head_cols)
    base_keys = part_keys[:, 0].reshape(blocks, BLOCK * head_cols)
    base_values = part_values[:, 0].reshape(blocks, BLOCK * head_cols)
    far_keys = part_keys[:, 1:].reshape(-1, BLOCK, head_cols).astype(jnp.bfloat16)
    far_values = part_values[:, 1:].reshape(-1, BLOCK, head_cols).astype(jnp.bfloat16)
    send_keys = jnp.zeros((slot_count, BLOCK, head_cols), jnp.bfloat16).at[slot_index].set(far_keys)
    send_values = (
        jnp.zeros((slot_count, BLOCK, head_cols), jnp.bfloat16).at[slot_index].set(far_values)
    )
    slot_keys, slot_values = (
        lax.all_to_all(send_keys, "seq", split_axis=0, concat_axis=0, tiled=True),
        lax.all_to_all(send_values, "seq", split_axis=0, concat_axis=0, tiled=True),
    )
    owner_map = (asked_blocks[None, :] == jnp.arange(blocks, dtype=jnp.int32)[:, None]).astype(
        jnp.float32
    )
    added_keys = jnp.dot(
        owner_map,
        slot_keys.reshape(slot_count, -1).astype(jnp.float32),
        precision=lax.Precision.HIGHEST,
    )
    added_values = jnp.dot(
        owner_map,
        slot_values.reshape(slot_count, -1).astype(jnp.float32),
        precision=lax.Precision.HIGHEST,
    )
    grad_key = (base_keys + added_keys).reshape(node_rows, head_cols).astype(jnp.bfloat16)
    grad_value = (base_values + added_values).reshape(node_rows, head_cols).astype(jnp.bfloat16)
    contract = (((0,), (0,)), ((), ()))
    term_query = lax.dot_general(gathered, grad_query, contract, preferred_element_type=jnp.float32)
    term_key = lax.dot_general(gathered, grad_key, contract, preferred_element_type=jnp.float32)
    term_value = lax.dot_general(gathered, grad_value, contract, preferred_element_type=jnp.float32)
    weight_grads = lax.psum_scatter(
        jnp.concatenate([term_query, term_key, term_value], axis=1),
        "seq",
        scatter_dimension=0,
        tiled=True,
    )
    grad_wq = weight_grads[:, :head_cols]
    grad_wk = weight_grads[:, head_cols : 2 * head_cols]
    grad_wv = weight_grads[:, 2 * head_cols :]
    contract = (((1,), (1,)), ((), ()))
    summed = lax.dot_general(grad_query, w_query, contract, preferred_element_type=jnp.float32)
    summed = summed + lax.dot_general(grad_key, w_key, contract, preferred_element_type=jnp.float32)
    summed = summed + lax.dot_general(
        grad_value, w_value, contract, preferred_element_type=jnp.float32
    )
    grad_input = lax.psum_scatter(summed, "head", scatter_dimension=0, tiled=True).astype(
        jnp.bfloat16
    )
    return (grad_input, grad_wq, grad_wk, grad_wv)


def solution(mesh):
    placed = (
        P(("seq", "head"), None),
        P(None, "head"),
        P(None, "head"),
        P(None, "head"),
        P(("seq", "head"), None),
        P("seq", None),
        P("seq"),
    )
    return jax.shard_map(
        shards,
        mesh=mesh,
        in_specs=placed,
        out_specs=(P(("seq", "head"), None), P("seq", "head"), P("seq", "head"), P("seq", "head")),
        check_vma=False,
    )
```

profile of v0, /device:TPU:1, one launch (start us, length us, event | category | flops | bytes accessed | tf_op | source)
XLA Modules:
  0.0 553.4 jit_solution(14402435967929532808)
XLA Ops:
  12.1 7.6 %all-to-all-start = ((s32[16,7,1]{1,2,0:T(1,128)}), s32[16,7,1]{1,2,0:T(1,128)S(1)}, u32[]{:S(2)}, u32[]{:S(2)}) async-start(s32[16,7,1]{1,2,0:T(1,128)} %bitcast.24), calls=%async_computation | async-start | bytes 16384 | tf_op jit(solution)/shard_map/all_to_all | solution.py:68
  26.0 7.4 %all-to-all-start.2 = ((bf16[384,8,128]{0,2,1:T(8,128)(2,1)}), bf16[384,8,128]{0,2,1:T(8,128)(2,1)S(1)}, u32[]{:S(2)}, u32[]{:S(2)}) async-start(bf16[384,8,128]{0,2,1:T(8,128)(2,1)} %bitcast.27), calls=%async_computation.2 | async-start | bytes 1572864 | tf_op jit(solution)/shard_map/all_to_all | solution.py:53
  34.8 28.2 %all-gather.2.cloned.1.call-done = bf16[3072,1024]{1,0:T(8,128)(2,1)} async-done(((bf16[384,1024]{1,0:T(8,128)(2,1)}), bf16[3072,1024]{1,0:T(8,128)(2,1)}) %all-gather.2.cloned.1.call-update) | async-done | bytes 6291472 | tf_op jit(solution)/shard_map/all_gather | solution.py:47
  63.0 4.6 convolution_convert_fusion.2
  70.5 6.7 %all-to-all-start.1 = ((bf16[112,128,128]{2,1,0:T(8,128)(2,1)}), bf16[112,128,128]{2,1,0:T(8,128)(2,1)}, u32[]{:S(2)}, u32[]{:S(2)}) async-start(bf16[112,128,128]{2,1,0:T(8,128)(2,1)} %gather_fusion), calls=%async_computation.1 | async-start | bytes 7340032 | tf_op jit(solution)/shard_map/all_to_all | solution.py:74
  77.2 4.6 convolution_convert_fusion
  84.7 42.5 %all-to-all-done.1 = bf16[112,128,128]{2,1,0:T(8,128)(2,1)} async-done(((bf16[112,128,128]{2,1,0:T(8,128)(2,1)}), bf16[112,128,128]{2,1,0:T(8,128)(2,1)}, u32[]{:S(2)}, u32[]{:S(2)}) %all-to-all-start.1) | async-done | bytes 3670048 | tf_op jit(solution)/shard_map/all_to_all | solution.py:74
  127.2 12.0 %all-to-all-start.3 = ((bf16[112,128,128]{2,1,0:T(8,128)(2,1)}), bf16[112,128,128]{2,1,0:T(8,128)(2,1)}, u32[]{:S(2)}, u32[]{:S(2)}) async-start(bf16[112,128,128]{2,1,0:T(8,128)(2,1)} %gather_fusion.2), calls=%async_computation.3 | async-start | bytes 7340032 | tf_op jit(solution)/shard_map/all_to_all | solution.py:75
  148.5 4.6 convolution_convert_fusion.1
  161.9 23.5 %all-to-all-done.3 = bf16[112,128,128]{2,1,0:T(8,128)(2,1)} async-done(((bf16[112,128,128]{2,1,0:T(8,128)(2,1)}), bf16[112,128,128]{2,1,0:T(8,128)(2,1)}, u32[]{:S(2)}, u32[]{:S(2)}) %all-to-all-start.3) | async-done | bytes 3670048 | tf_op jit(solution)/shard_map/all_to_all | solution.py:75
  195.2 62.4 %while.14 = (s32[]{:T(128)}, bf16[6,4,128,2,64]{2,1,0,4,3:T(4,128)(2,1)}, f32[6,4,4,128,2,64]{3,5,4,2,1,0:T(8,128)}, f32[6,4,4,128,2,64]{3,5,4,2,1,0:T(8,128)}, ...) while((s32[]{:T(128)}, ...), condition=%wide.region_7.8_spmd, body=%wide.region_3.7_spmd.sunk | while | flops 349238272 | bytes 26918608 | solution.py:101
  267.6 10.9 %scatter_fusion.1 = bf16[112,128,128]{2,1,0:T(8,128)(2,1)} fusion(bf16[112,128,128]{2,1,0:T(8,128)(2,1)} %broadcast.148.clone.1, s32[72]{0:T(128)S(1)} %fusion.26, bf16[72,128,128]{2,1,0:T(8,128)(2,1)S(1)} %bitcast.156), kind=kCustom, calls=%fused_computation.6 | custom fusion | bytes 7078176 | tf_op jit(solution)/shard_map/scatter | solution.py:111
  278.4 4.8 all-to-all-start.5
  293.3 10.9 %scatter_fusion = bf16[112,128,128]{2,1,0:T(8,128)(2,1)} fusion(bf16[112,128,128]{2,1,0:T(8,128)(2,1)} %broadcast.148.clone, s32[72]{0:T(128)S(1)} %fusion.26, bf16[72,128,128]{2,1,0:T(8,128)(2,1)S(1)} %bitcast.155), kind=kCustom, calls=%fused_computation.5 | custom fusion | bytes 7078176 | tf_op jit(solution)/shard_map/scatter | solution.py:109
  304.2 21.1 %all-to-all-done.5 = bf16[112,128,128]{2,1,0:T(8,128)(2,1)} async-done(((bf16[112,128,128]{2,1,0:T(8,128)(2,1)}), bf16[112,128,128]{2,1,0:T(8,128)(2,1)}, u32[]{:S(2)}, u32[]{:S(2)}) %all-to-all-start.5) | async-done | bytes 3670048 | tf_op jit(solution)/shard_map/all_to_all | solution.py:115
  325.3 9.2 %all-to-all-start.4 = ((bf16[112,128,128]{2,1,0:T(8,128)(2,1)}), bf16[112,128,128]{2,1,0:T(8,128)(2,1)}, u32[]{:S(2)}, u32[]{:S(2)}) async-start(bf16[112,128,128]{2,1,0:T(8,128)(2,1)} %scatter_fusion), calls=%async_computation.4 | async-start | bytes 7340032 | tf_op jit(solution)/shard_map/all_to_all | solution.py:114
  342.9 4.7 convolution_bitcast_fusion.5
  347.6 4.8 fusion.16
  353.7 21.6 %all-to-all-done.4 = bf16[112,128,128]{2,1,0:T(8,128)(2,1)} async-done(((bf16[112,128,128]{2,1,0:T(8,128)(2,1)}), bf16[112,128,128]{2,1,0:T(8,128)(2,1)}, u32[]{:S(2)}, u32[]{:S(2)}) %all-to-all-start.4) | async-done | bytes 3670048 | tf_op jit(solution)/shard_map/all_to_all | solution.py:114
  375.3 6.3 %fusion.15 = bf16[24,16384]{1,0:T(8,128)(2,1)} fusion(bf16[14,8,128,128]{3,2,1,0:T(8,128)(2,1)} %bitcast.49, f32[3,8,128,128]{3,2,1,0:T(8,128)} %bitcast.159, s32[112]{0:T(128)S(1)} %eq.33), kind=kOutput, calls=%fused_computation.40 | convolution fusion | flops 88869504 | bytes 6029760 | tf_op jit(solution)/shard_map/dot_general | solution.py:120
  393.4 6.3 %fusion.32 = f32[3072,1024]{1,0:T(8,128)} fusion(bf16[3072,128]{1,0:T(8,128)(2,1)S(1)} %copy-done.2, bf16[1024,128]{1,0:T(8,128)(2,1)S(1)} %copy-done.8), kind=kOutput, calls=%fused_computation.84 | convolution fusion | flops 805306368 | bytes 13631488 | tf_op jit(solution)/shard_map/dot_general | solution.py:147
  399.7 11.4 %add_add_fusion = f32[3072,1024]{1,0:T(8,128)} fusion(f32[3072,1024]{1,0:T(8,128)S(1)} %fusion.31, f32[3072,1024]{1,0:T(8,128)} %fusion.32, bf16[3072,128]{1,0:T(8,128)(2,1)S(1)} %copy-done.3, bf16[1024,128]{1,0:T(8,128)(2,1)S(1)} %copy-done.10), kind=kOutput, calls=%fused_computation.42 | convolution fusion | flops 811597824 | bytes 38797312 | tf_op jit(solution)/shard_map/dot_general | solution.py:148
  411.1 57.6 %reduce-scatter.7.cloned.1.call-done = f32[64,384]{1,0:T(8,128)} async-done(((f32[1024,384]{1,0:T(8,128)}), f32[64,384]{1,0:T(8,128)}) %reduce-scatter.7.cloned.1.call-update) | async-done | bytes 98320
  470.2 73.9 %reduce-scatter.5.cloned.1.call-done = f32[384,1024]{1,0:T(8,128)} async-done(((f32[3072,1024]{1,0:T(8,128)}), f32[384,1024]{1,0:T(8,128)}) %reduce-scatter.5.cloned.1.call-update) | async-done | bytes 1572880 | tf_op jit(solution)/shard_map/reduce_scatter | solution.py:151
  (169 shorter events, 153.4 us)
Async XLA Ops:
  7.2 141.3 %copy-start = (bf16[1024,128]{1,0:T(8,128)(2,1)S(1)}, bf16[1024,128]{1,0:T(8,128)(2,1)}, u32[]{:S(2)}) copy-start(bf16[1024,128]{1,0:T(8,128)(2,1)} %param.10) | copy-start | bytes 786436
  7.2 55.8 %copy-start.7 = (bf16[1024,128]{1,0:T(8,128)(2,1)S(1)}, bf16[1024,128]{1,0:T(8,128)(2,1)}, u32[]{:S(2)}) copy-start(bf16[1024,128]{1,0:T(8,128)(2,1)} %param.11) | copy-start | bytes 786436
  7.2 55.8 %all-gather.2.cloned.1.call-start = ((), (), s32[]{:S(2)}) async-start(), calls=%async_computation.8 | async-start | bytes 7077888 | tf_op jit(solution)/shard_map/all_gather | solution.py:47
  12.1 13.9 %all-to-all-start = ((s32[16,7,1]{1,2,0:T(1,128)}), s32[16,7,1]{1,2,0:T(1,128)S(1)}, u32[]{:S(2)}, u32[]{:S(2)}) async-start(s32[16,7,1]{1,2,0:T(1,128)} %bitcast.24), calls=%async_computation | async-start | bytes 16384 | tf_op jit(solution)/shard_map/all_to_all | solution.py:68
  26.0 44.5 %all-to-all-start.2 = ((bf16[384,8,128]{0,2,1:T(8,128)(2,1)}), bf16[384,8,128]{0,2,1:T(8,128)(2,1)S(1)}, u32[]{:S(2)}, u32[]{:S(2)}) async-start(bf16[384,8,128]{0,2,1:T(8,128)(2,1)} %bitcast.27), calls=%async_computation.2 | async-start | bytes 1572864 | tf_op jit(solution)/shard_map/all_to_all | solution.py:53
  70.5 6.7 %copy-start.9 = (bf16[1024,128]{1,0:T(8,128)(2,1)S(1)}, bf16[1024,128]{1,0:T(8,128)(2,1)}, u32[]{:S(2)}) copy-start(bf16[1024,128]{1,0:T(8,128)(2,1)} %param.12) | copy-start | bytes 786436
  70.5 56.7 %all-to-all-start.1 = ((bf16[112,128,128]{2,1,0:T(8,128)(2,1)}), bf16[112,128,128]{2,1,0:T(8,128)(2,1)}, u32[]{:S(2)}, u32[]{:S(2)}) async-start(bf16[112,128,128]{2,1,0:T(8,128)(2,1)} %gather_fusion), calls=%async_computation.1 | async-start | bytes 7340032 | tf_op jit(solution)/shard_map/all_to_all | solution.py:74
  84.7 54.6 %copy-start.11 = (s32[24]{0:T(128)S(1)}, s32[24]{0:T(128)}, u32[]{:S(2)}) copy-start(s32[24]{0:T(128)} %param.15) | copy-start | bytes 292
  127.2 58.1 %all-to-all-start.3 = ((bf16[112,128,128]{2,1,0:T(8,128)(2,1)}), bf16[112,128,128]{2,1,0:T(8,128)(2,1)}, u32[]{:S(2)}, u32[]{:S(2)}) async-start(bf16[112,128,128]{2,1,0:T(8,128)(2,1)} %gather_fusion.2), calls=%async_computation.3 | async-start | bytes 7340032 | tf_op jit(solution)/shard_map/all_to_all | solution.py:75
  143.4 2.6 copy-start.4
  278.4 46.8 %all-to-all-start.5 = ((bf16[112,128,128]{2,1,0:T(8,128)(2,1)}), bf16[112,128,128]{2,1,0:T(8,128)(2,1)}, u32[]{:S(2)}, u32[]{:S(2)}) async-start(bf16[112,128,128]{2,1,0:T(8,128)(2,1)} %scatter_fusion.1), calls=%async_computation.5 | async-start | bytes 7340032 | tf_op jit(solution)/shard_map/all_to_all | solution.py:115
  325.3 50.0 %all-to-all-start.4 = ((bf16[112,128,128]{2,1,0:T(8,128)(2,1)}), bf16[112,128,128]{2,1,0:T(8,128)(2,1)}, u32[]{:S(2)}, u32[]{:S(2)}) async-start(bf16[112,128,128]{2,1,0:T(8,128)(2,1)} %scatter_fusion), calls=%async_computation.4 | async-start | bytes 7340032 | tf_op jit(solution)/shard_map/all_to_all | solution.py:114
  334.5 134.2 %reduce-scatter.7.cloned.1.call-start = ((), (), s32[]{:S(2)}) async-start(), calls=%async_computation.10 | async-start | bytes 1671168
  342.9 4.7 copy-start.5
  375.3 12.7 %slice-start = ((s8[6291456]{0:T(1024)(128)(4,1)}), s8[2097152]{0:T(1024)(128)(4,1)S(1)}, s32[]{:S(2)}) async-start(s8[6291456]{0:T(1024)(128)(4,1)} %bitcast.151), calls=%async_computation.11 | async-start | bytes 4194304
  383.8 4.2 slice-start.1
  383.8 4.4 copy-start.1
  388.3 1.0 copy-start.6
  391.2 2.2 copy-start.2
  391.2 2.2 copy-start.8
  391.2 152.9 %reduce-scatter.5.cloned.1.call-start = ((), (), s32[]{:S(2)}) async-start(), calls=%async_computation.9 | async-start | bytes 14155776 | tf_op jit(solution)/shard_map/reduce_scatter | solution.py:151
  393.3 6.3 %copy-start.3 = (bf16[3072,128]{1,0:T(8,128)(2,1)S(1)}, bf16[3072,128]{1,0:T(8,128)(2,1)}, u32[]{:S(2)}) copy-start(bf16[3072,128]{1,0:T(8,128)(2,1)} %convert_element_type.59) | copy-start | bytes 2359300
  393.4 6.3 %copy-start.10 = (bf16[1024,128]{1,0:T(8,128)(2,1)S(1)}, bf16[1024,128]{1,0:T(8,128)(2,1)}, u32[]{:S(2)}) copy-start(bf16[1024,128]{1,0:T(8,128)(2,1)} %param.12) | copy-start | bytes 786436
Sparse Core Ops, SparseCore 0:
  9.7 53.2 all-gather.1
  391.3 77.4 reduce-scatter.6
  471.2 72.8 reduce-scatter.4
where the time goes:
time: 561 us; the launch traced here: 553 us
  waiting for transfers between devices  273 us (49%)
  local copies, waits for them, and re-layouts  111 us (20%)
  matrix products  89.9 us (16%)
  starting transfers between devices  48.4 us (9%)
  other arithmetic  16.6 us (3%)
  between operations  14.6 us (3%)
    reduce_scatter x1, waiting for transfers between devices, shards(): lax.psum_scatter(summed, 'head', scatter_dimension=0, tiled=True)  73.9 us
    unnamed x4, waiting for transfers between devices  58.3 us
    all_to_all x1, waiting for transfers between devices, shards(): lax.all_to_all(served_keys, 'seq', split_axis=0, concat_axis=0, tiled=True)  42.5 us
    all_gather x1, waiting for transfers between devices, shards(): gathered = lax.all_gather(node_input, 'head', axis=0, tiled=True)  28.2 us
    all_to_all x1, waiting for transfers between devices, shards(): lax.all_to_all(served_values, 'seq', split_axis=0, concat_axis=0, tiled=T...  23.5 us
    scatter x2, local copies, waits for them, and re-layouts, shards(): jnp.zeros((slot_count, BLOCK, head_cols), jnp.bfloat16).at[slot_index]  21.8 us
    all_to_all x1, waiting for transfers between devices, shards(): lax.all_to_all(send_keys, 'seq', split_axis=0, concat_axis=0, tiled=True)  21.6 us
    all_to_all x1, waiting for transfers between devices, shards(): lax.all_to_all(send_values, 'seq', split_axis=0, concat_axis=0, tiled=True)  21.1 us
  transfers between devices with their start and end apart: 9, of which 8 were waited for; matrix products, arithmetic and copies ran while one was open for 19% of the time, Pallas kernels for 0%

commit v1 on v0

v1 whole, which is shorter than its diff:
```python
import functools

import jax
import jax.numpy as jnp
from jax import lax
from jax.experimental import pallas as pl
from jax.experimental.pallas import tpu as pltpu
from jax.sharding import PartitionSpec as P

HDIM = 64
BLOCK = 128
KB = 4
BF16 = jnp.bfloat16
F32 = jnp.float32
SCALE = HDIM ** (-0.5)
GROUP = 4
VMEM_LIMIT = 48 * 1024 * 1024
VMEM = pl.BlockSpec(memory_space=pltpu.VMEM)
SMEM = pl.BlockSpec(memory_space=pltpu.SMEM)
NT = (((1,), (1,)), ((), ()))
TN = (((0,), (0,)), ((), ()))


def params():
    return pltpu.CompilerParams(vmem_limit_bytes=VMEM_LIMIT)


def cost(flops, moved):
    return pl.CostEstimate(flops=int(flops), bytes_accessed=int(moved), transcendentals=0)


def head_mask(width):
    heads = width // HDIM
    row_head = jnp.arange(heads * BLOCK)[:, None] // BLOCK
    col_head = jnp.arange(width)[None, :] // HDIM
    return (row_head == col_head).astype(BF16)


def by_head(tile, mask_ref):
    heads = mask_ref.shape[0] // BLOCK
    return jnp.concatenate([tile] * heads, axis=0) * mask_ref[...]


def listed(meta_ref, order_ref, total):
    def scan(i, n):
        wanted = meta_ref[i] >= 0

        @pl.when(wanted)
        def _():
            order_ref[n] = i

        return n + wanted.astype(jnp.int32)

    return lax.fori_loop(0, total, scan, 0)


def row_stats(key_heads, value_heads, query, grad):
    heads = key_heads.shape[0] // BLOCK
    scores = lax.dot_general(key_heads, query, NT, preferred_element_type=F32)
    grad_probs = lax.dot_general(value_heads, grad, NT, preferred_element_type=F32)
    scores = scores.reshape(heads, BLOCK, BLOCK)
    grad_probs = grad_probs.reshape(heads, BLOCK, BLOCK)
    top = jnp.max(scores, axis=1, keepdims=True)
    unnorm = jnp.exp((scores - top) * SCALE)
    total = jnp.sum(unnorm, axis=1)
    weighted = jnp.sum(unnorm * grad_probs, axis=1)
    return top[:, 0] * SCALE + jnp.log(total), weighted / total


def slot_rows(ref, slot, per):
    return ref[slot // per, pl.ds(lax.rem(slot, per) * BLOCK, BLOCK), :]


def remote_stats_kernel(per, meta_ref, query_ref, grad_ref, key_ref, value_ref, mask_ref, out_ref, order_ref):
    total = meta_ref.shape[0]
    heads = mask_ref.shape[0] // BLOCK
    out_ref[...] = jnp.zeros_like(out_ref)
    n = listed(meta_ref, order_ref, total)

    def step(g, carry):
        for u in range(GROUP):
            slot = order_ref[jnp.minimum(g * GROUP + u, n - 1)]
            block = meta_ref[slot]
            lse, delta = row_stats(
                by_head(key_ref[block], mask_ref),
                by_head(value_ref[block], mask_ref),
                slot_rows(query_ref, slot, per),
                slot_rows(grad_ref, slot, per),
            )
            out_ref[slot, 0:heads] = lse
            out_ref[slot, heads : 2 * heads] = delta
        return carry

    lax.fori_loop(0, pl.cdiv(n, GROUP), step, 0)


def own_stats_kernel(query_ref, grad_ref, key_ref, value_ref, mask_ref, out_ref):
    heads = mask_ref.shape[0] // BLOCK
    blocks = query_ref.shape[0]

    def step(g, carry):
        for u in range(GROUP):
            b = g * GROUP + u
            lse, delta = row_stats(
                by_head(key_ref[b], mask_ref),
                by_head(value_ref[b], mask_ref),
                query_ref[b],
                grad_ref[b],
            )
            out_ref[b, 0:heads] = lse
            out_ref[b, heads : 2 * heads] = delta
        return carry

    lax.fori_loop(0, blocks // GROUP, step, 0)


def merge_kernel(slot_ref, count_ref, own_ref, far_ref, row_ref, back_ref, lse_ref, delta_ref):
    blocks = own_ref.shape[0]
    heads = own_ref.shape[1] // 2
    back_ref[...] = jnp.zeros_like(back_ref)
    for b in range(blocks):
        for j in range(KB - 1):
            live = count_ref[b] > j + 1
            stats = far_ref[slot_ref[b * (KB - 1) + j]]
            lse_ref[j, b] = jnp.where(live, stats[:heads], -1e30)
            delta_ref[j, b] = jnp.where(live, stats[heads:], 0.0)
    own = own_ref[...]
    lses = [own[:, :heads]] + [lse_ref[j] for j in range(KB - 1)]
    deltas = [own[:, heads:]] + [delta_ref[j] for j in range(KB - 1)]
    top = functools.reduce(jnp.maximum, lses)
    weights = [jnp.exp(v - top) for v in lses]
    total = sum(weights)
    row_ref[:, :heads] = top + jnp.log(total)
    row_ref[:, heads:] = sum(w * d for w, d in zip(weights, deltas)) / total
    for b in range(blocks):
        for j in range(KB - 1):
            back_ref[slot_ref[b * (KB - 1) + j]] = row_ref[b]


def entry_grads(key_heads, value_heads, query, grad, stats):
    heads = key_heads.shape[0] // BLOCK
    scores = lax.dot_general(key_heads, query, NT, preferred_element_type=F32)
    grad_probs = lax.dot_general(value_heads, grad, NT, preferred_element_type=F32)
    scores = scores.reshape(heads, BLOCK, BLOCK)
    grad_probs = grad_probs.reshape(heads, BLOCK, BLOCK)
    probs = jnp.exp(scores * SCALE - stats[:heads][:, None, :])
    grad_scores = probs * (grad_probs - stats[heads:][:, None, :]) * SCALE
    flat = (heads * BLOCK, BLOCK)
    return probs.astype(BF16).reshape(flat), grad_scores.astype(BF16).reshape(flat)


def pick_heads(stacked):
    width = stacked.shape[1]
    heads = width // HDIM
    col_head = lax.broadcasted_iota(jnp.int32, (BLOCK, width), 1) // HDIM
    picked = stacked[:BLOCK]
    for h in range(1, heads):
        picked = jnp.where(col_head == h, stacked[h * BLOCK : (h + 1) * BLOCK], picked)
    return picked


def far_query_kernel(per, meta_ref, query_ref, grad_ref, stats_ref, key_ref, value_ref, mask_ref, out_ref, order_ref):
    total = meta_ref.shape[0]
    n = listed(meta_ref, order_ref, total)

    def step(g, carry):
        for u in range(GROUP):
            slot = order_ref[jnp.minimum(g * GROUP + u, n - 1)]
            block = meta_ref[slot]
            key_heads = by_head(key_ref[block], mask_ref)
            _, grad_scores = entry_grads(
                key_heads,
                by_head(value_ref[block], mask_ref),
                slot_rows(query_ref, slot, per),
                slot_rows(grad_ref, slot, per),
                stats_ref[slot],
            )
            term = lax.dot_general(grad_scores, key_heads, TN, preferred_element_type=F32)
            out_ref[slot] = term.astype(BF16)
        return carry

    lax.fori_loop(0, pl.cdiv(n, GROUP), step, 0)


def key_value_kernel(
    per,
    meta_ref,
    far_query_ref,
    far_grad_ref,
    far_stats_ref,
    query_ref,
    grad_ref,
    stats_ref,
    key_ref,
    value_ref,
    mask_ref,
    own_term_ref,
    key_out_ref,
    value_out_ref,
    order_ref,
    key_sum,
    value_sum,
):
    blocks = query_ref.shape[0]
    total = meta_ref.shape[0]

    def own(g, carry):
        for u in range(GROUP):
            b = g * GROUP + u
            key_heads = by_head(key_ref[b], mask_ref)
            query = query_ref[b]
            grad = grad_ref[b]
            probs, grad_scores = entry_grads(
                key_heads, by_head(value_ref[b], mask_ref), query, grad, stats_ref[b]
            )
            own_term_ref[b] = lax.dot_general(grad_scores, key_heads, TN, preferred_element_type=F32)
            key_sum[b] = pick_heads(jnp.dot(grad_scores, query, preferred_element_type=F32))
            value_sum[b] = pick_heads(jnp.dot(probs, grad, preferred_element_type=F32))
        return carry

    lax.fori_loop(0, blocks // GROUP, own, 0)
    n = listed(meta_ref, order_ref, total)

    def far(g, carry):
        for u in range(GROUP):
            at = g * GROUP + u
            slot = order_ref[jnp.minimum(at, n - 1)]
            block = meta_ref[slot]
            query = slot_rows(far_query_ref, slot, per)
            grad = slot_rows(far_grad_ref, slot, per)
            probs, grad_scores = entry_grads(
                by_head(key_ref[block], mask_ref),
                by_head(value_ref[block], mask_ref),
                query,
                grad,
                far_stats_ref[slot],
            )
            keep = at < n
            key_term = pick_heads(jnp.dot(grad_scores, query, preferred_element_type=F32))
            value_term = pick_heads(jnp.dot(probs, grad, preferred_element_type=F32))
            key_sum[block] += jnp.where(keep, key_term, 0.0)
            value_sum[block] += jnp.where(keep, value_term, 0.0)
        return carry

    lax.fori_loop(0, pl.cdiv(n, GROUP), far, 0)
    key_out_ref[...] = key_sum[...].astype(BF16)
    value_out_ref[...] = value_sum[...].astype(BF16)


def query_sum_kernel(slot_ref, count_ref, own_ref, far_ref, out_ref):
    blocks = own_ref.shape[0]

    def step(b, carry):
        total = own_ref[b]
        for j in range(KB - 1):
            term = far_ref[slot_ref[b * (KB - 1) + j]].astype(F32)
            total = total + jnp.where(count_ref[b] > j + 1, term, 0.0)
        out_ref[b] = total.astype(BF16)
        return carry

    lax.fori_loop(0, blocks, step, 0)


def pack_kernel(per, peers_step, source_ref, tile_ref, out_ref):
    first = pl.program_id(0) * peers_step
    for p in range(peers_step):
        for r in range(per):
            out_ref[p, r * BLOCK : (r + 1) * BLOCK, :] = tile_ref[source_ref[(first + p) * per + r]]


def pack_meta_kernel(per, peers_step, source_ref, tile_ref, meta_ref, out_ref):
    pack_kernel(per, peers_step, source_ref, tile_ref, out_ref)
    out_ref[:, per * BLOCK :, :] = meta_ref[...]


def pack(tiles, source, meta, n_seq, per):
    blocks, _, cols = tiles.shape
    peers_step = 4
    extra = 0 if meta is None else meta.shape[1]
    rows = per * BLOCK + extra
    in_specs = [pl.BlockSpec((blocks, BLOCK, cols), lambda i, s: (0, 0, 0))]
    operands = [tiles]
    if meta is not None:
        in_specs.append(pl.BlockSpec((peers_step, extra, cols), lambda i, s: (i, 0, 0)))
        operands.append(meta)
    return pl.pallas_call(
        functools.partial(pack_kernel if meta is None else pack_meta_kernel, per, peers_step),
        grid_spec=pltpu.PrefetchScalarGridSpec(
            num_scalar_prefetch=1,
            grid=(n_seq // peers_step,),
            in_specs=in_specs,
            out_specs=pl.BlockSpec((peers_step, rows, cols), lambda i, s: (i, 0, 0)),
        ),
        out_shape=jax.ShapeDtypeStruct((n_seq, rows, cols), BF16),
        compiler_params=params(),
        cost_estimate=cost(0, 2 * 2 * n_seq * rows * cols),
    )(source, *operands)


def seq_exchange(x):
    return lax.all_to_all(x, "seq", split_axis=0, concat_axis=0, tiled=True)


def head_exchange(x):
    n_head = lax.axis_size("head")
    me = lax.axis_index("head")
    parts = x.reshape(n_head, x.shape[0] // n_head, x.shape[1])
    out = []
    for shift in range(n_head):
        chunk = lax.dynamic_index_in_dim(parts, lax.rem(me + shift, n_head), 0, keepdims=False)
        if shift:
            chunk = lax.ppermute(chunk, "head", [(h, (h + shift) % n_head) for h in range(n_head)])
        out.append(chunk)
    return jnp.concatenate(out, axis=1)


def shards(node_input, w_query, w_key, w_value, grad_context, key_blocks, counts):
    n_seq = lax.axis_size("seq")
    n_head = lax.axis_size("head")
    me = lax.axis_index("head")
    cols = w_query.shape[1]
    heads = cols // HDIM
    blocks = key_blocks.shape[0]
    nodes = blocks * BLOCK
    per = max(2, 3 * blocks * (KB - 1) // (2 * n_seq) + 1)
    slots = n_seq * per
    mask = head_mask(cols)

    remote = key_blocks[:, 1:].reshape(-1)
    entries = remote.shape[0]
    owner = remote // blocks
    inner = remote % blocks
    numbers = jnp.arange(entries, dtype=jnp.int32)
    live = (numbers % (KB - 1)) + 1 < counts[numbers // (KB - 1)]
    before = (owner[:, None] == owner[None, :]) & (numbers[None, :] < numbers[:, None])
    slot_of = owner * per + jnp.sum(before.astype(jnp.int32), axis=1)
    taken = slot_of[None, :] == jnp.arange(slots, dtype=jnp.int32)[:, None]
    source = jnp.sum(jnp.where(taken, numbers[None, :] // (KB - 1), 0), axis=1)
    asked = jnp.sum(jnp.where(taken & live[None, :], inner[None, :] + 1, 0), axis=1) - 1
    meta = jnp.broadcast_to(
        jnp.pad(asked.reshape(n_seq, per), ((0, 0), (0, 16 - per)))[:, :, None], (n_seq, 16, cols)
    ).astype(BF16)

    upstream = lax.all_to_all(grad_context, "head", split_axis=1, concat_axis=0, tiled=True)
    grad_tiles = upstream.reshape(blocks, BLOCK, cols)
    far_grads = seq_exchange(pack(grad_tiles, source, meta, n_seq, per))
    far_meta = far_grads[:, per * BLOCK : per * BLOCK + per, 0].astype(jnp.int32).reshape(-1)

    gathered = lax.all_gather(node_input, "head", axis=0, tiled=True)
    queries = jnp.dot(gathered, w_query, preferred_element_type=F32).astype(BF16)
    query_tiles = queries.reshape(blocks, BLOCK, cols)
    far_queries = seq_exchange(pack(query_tiles, source, None, n_seq, per))
    keys = jnp.dot(gathered, w_key, preferred_element_type=F32).astype(BF16)
    values = jnp.dot(gathered, w_value, preferred_element_type=F32).astype(BF16)
    key_tiles = keys.reshape(blocks, BLOCK, cols)
    value_tiles = values.reshape(blocks, BLOCK, cols)

    w_all = jnp.concatenate([w_query, w_key, w_value], axis=0)
    w_all, _ = lax.optimization_barrier((w_all, gathered))
    w_all = lax.all_gather(w_all, "head", axis=0)
    turn = lax.rem(me - jnp.arange(n_head, dtype=jnp.int32) + n_head, n_head)
    w_all = w_all[turn].reshape(n_head, 3, w_query.shape[0], cols)
    w_all = w_all.transpose(1, 2, 0, 3).reshape(3, w_query.shape[0], n_head * cols)

    unit_flops = 2 * heads * BLOCK * BLOCK * cols
    tile_bytes = 2 * BLOCK * cols
    stats_shape = jax.ShapeDtypeStruct((slots, 2 * heads, BLOCK), F32)
    own_stats = pl.pallas_call(
        own_stats_kernel,
        out_shape=jax.ShapeDtypeStruct((blocks, 2 * heads, BLOCK), F32),
        in_specs=[VMEM] * 5,
        out_specs=VMEM,
        compiler_params=params(),
        cost_estimate=cost(2 * blocks * unit_flops, 4 * blocks * tile_bytes),
    )(query_tiles, grad_tiles, key_tiles, value_tiles, mask)
    far_stats = pl.pallas_call(
        functools.partial(remote_stats_kernel, per),
        out_shape=stats_shape,
        in_specs=[SMEM] + [VMEM] * 5,
        out_specs=VMEM,
        scratch_shapes=[pltpu.SMEM((slots,), jnp.int32)],
        compiler_params=params(),
        cost_estimate=cost(2 * slots * unit_flops, 2 * slots * tile_bytes),
    )(far_meta, far_queries, far_grads, key_tiles, value_tiles, mask)
    row_stats_all, back = pl.pallas_call(
        merge_kernel,
        out_shape=(jax.ShapeDtypeStruct((blocks, 2 * heads, BLOCK), F32), stats_shape),
        in_specs=[SMEM, SMEM, VMEM, VMEM],
        out_specs=(VMEM, VMEM),
        scratch_shapes=[pltpu.VMEM((KB - 1, blocks, heads, BLOCK), F32)] * 2,
        compiler_params=params(),
        cost_estimate=cost(0, 2 * 2 * slots * 4 * heads * BLOCK),
    )(slot_of, counts, own_stats, seq_exchange(far_stats))
    back = seq_exchange(back)

    far_terms = pl.pallas_call(
        functools.partial(far_query_kernel, per),
        out_shape=jax.ShapeDtypeStruct((slots, BLOCK, cols), BF16),
        in_specs=[SMEM] + [VMEM] * 6,
        out_specs=VMEM,
        scratch_shapes=[pltpu.SMEM((slots,), jnp.int32)],
        compiler_params=params(),
        cost_estimate=cost(3 * slots * unit_flops, 3 * slots * tile_bytes),
    )(far_meta, far_queries, far_grads, back, key_tiles, value_tiles, mask)
    back_terms = seq_exchange(far_terms)

    tile_shape = (blocks, BLOCK, cols)
    own_terms, grad_keys, grad_values = pl.pallas_call(
        functools.partial(key_value_kernel, per),
        out_shape=(
            jax.ShapeDtypeStruct(tile_shape, F32),
            jax.ShapeDtypeStruct(tile_shape, BF16),
            jax.ShapeDtypeStruct(tile_shape, BF16),
        ),
        in_specs=[SMEM] + [VMEM] * 9,
        out_specs=(VMEM,) * 3,
        scratch_shapes=[
            pltpu.SMEM((slots,), jnp.int32),
            pltpu.VMEM(tile_shape, F32),
            pltpu.VMEM(tile_shape, F32),
        ],
        compiler_params=params(),
        cost_estimate=cost(5 * slots * unit_flops, 3 * slots * tile_bytes),
    )(far_meta, far_queries, far_grads, back, query_tiles, grad_tiles, row_stats_all, key_tiles, value_tiles, mask)

    contract_rows = (((0,), (0,)), ((), ()))
    contract_cols = (((1,), (1,)), ((), ()))
    grad_key_value = jnp.concatenate(
        [grad_keys.reshape(nodes, cols), grad_values.reshape(nodes, cols)], axis=1
    )
    term_key_value = lax.dot_general(gathered, grad_key_value, contract_rows, preferred_element_type=F32)
    rows = head_exchange(grad_key_value).reshape(-1, n_head, 2, cols)
    rows_key = rows[:, :, 0].reshape(-1, n_head * cols)
    rows_value = rows[:, :, 1].reshape(-1, n_head * cols)
    summed = lax.dot_general(rows_key, w_all[1], contract_cols, preferred_element_type=F32)
    summed = summed + lax.dot_general(rows_value, w_all[2], contract_cols, preferred_element_type=F32)

    grad_query = pl.pallas_call(
        query_sum_kernel,
        out_shape=jax.ShapeDtypeStruct(tile_shape, BF16),
        in_specs=[SMEM, SMEM, VMEM, VMEM],
        out_specs=VMEM,
        compiler_params=params(),
        cost_estimate=cost(0, slots * tile_bytes),
    )(slot_of, counts, own_terms, back_terms).reshape(nodes, cols)
    term_query = lax.dot_general(gathered, grad_query, contract_rows, preferred_element_type=F32)
    weight_terms = jnp.concatenate([term_query, term_key_value], axis=1).astype(BF16)
    weight_terms = seq_exchange(weight_terms.reshape(n_seq, -1, 3 * cols))
    weight_grads = jnp.sum(weight_terms.astype(F32), axis=0)
    rows_query = head_exchange(grad_query)
    summed = summed + lax.dot_general(rows_query, w_all[0], contract_cols, preferred_element_type=F32)
    return (
        summed.astype(BF16),
        weight_grads[:, :cols],
        weight_grads[:, cols : 2 * cols],
        weight_grads[:, 2 * cols :],
    )


def solution(mesh):
    placed = (
        P(("seq", "head"), None),
        P(None, "head"),
        P(None, "head"),
        P(None, "head"),
        P(("seq", "head"), None),
        P("seq", None),
        P("seq"),
    )
    return jax.shard_map(
        shards,
        mesh=mesh,
        in_specs=placed,
        out_specs=(P(("seq", "head"), None), P("seq", "head"), P("seq", "head"), P("seq", "head")),
        check_vma=False,
    )
```

time: 561 us -> 342 us (0.61)
  waiting for transfers between devices: 273 us -> 91.4 us
  matrix products: 89.9 us -> 29.3 us
  local copies, waits for them, and re-layouts: 111 us -> 64.1 us
  Pallas kernels: 0 us -> 45.6 us
  starting transfers between devices: 48.4 us -> 79.7 us
  other arithmetic: 16.6 us -> 4.67 us
  blocking collectives: 0 us -> 10.5 us
    reduce_scatter x1 -> x0, waiting for transfers between devices: 73.9 us -> none  [shards(): lax.psum_scatter(summed, 'head', scatter_dimension=0, tiled=True)]
    dot_general x41 -> x8, matrix products: 89.9 us -> 29.3 us  [the longest x1 4.69 us: shards(): keys = jnp.dot(gathered, w_key, preferred_element_type=F32).astype(BF16)]
    unnamed x4 -> x2, waiting for transfers between devices: 58.3 us -> 0.7 us
    all_to_all x5, waiting for transfers between devices: 113 us -> 59.4 us  [seq_exchange(): return lax.all_to_all(x, 'seq', split_axis=0, concat_axis=0, tiled=True)]
    pallas_call x0 -> x8, Pallas kernels: none -> 45.6 us  [the longest x1 19.1 us: shards(): pl.pallas_call(functools.partial(key_value_kernel, per), out_shape=(jax.S...]
    ppermute x0 -> x14, starting transfers between devices: none -> 24.1 us  [head_exchange(): lax.ppermute(chunk, 'head', [(h, (h + shift) % n_head) for h in range(n_h...]
    scatter x3 -> x0, local copies, waits for them, and re-layouts: 22.6 us -> none  [the longest x2 21.8 us: shards(): jnp.zeros((slot_count, BLOCK, head_cols), jnp.bfloat16).at[slot_index]]
    unnamed x30 -> x56, local copies, waits for them, and re-layouts: 4.23 us -> 18.4 us
  transfers between devices with their start and end apart: 9 -> 22, of which waited for: 8 -> 7; matrix products, arithmetic and copies ran while one was open for 19% -> 18% of each run, Pallas kernels for 0% -> 13%
where the time goes in v1:
time: 342 us; the launch traced here: 340 us
  waiting for transfers between devices  91.4 us (27%)
  starting transfers between devices  79.7 us (23%)
  local copies, waits for them, and re-layouts  64.1 us (19%)
  Pallas kernels  45.6 us (13%)
  matrix products  29.3 us (9%)
  between operations  14.6 us (4%)
  blocking collectives  10.5 us (3%)
  other arithmetic  4.67 us (1%)
    all_to_all x5, waiting for transfers between devices, seq_exchange(): return lax.all_to_all(x, 'seq', split_axis=0, concat_axis=0, tiled=True)  59.4 us
    all_to_all x5, starting transfers between devices, seq_exchange(): return lax.all_to_all(x, 'seq', split_axis=0, concat_axis=0, tiled=True)  48.7 us
    ppermute x14, starting transfers between devices, head_exchange(): lax.ppermute(chunk, 'head', [(h, (h + shift) % n_head) for h in range(n_h...  24.1 us
    pallas_call x1, Pallas kernels, shards(): pl.pallas_call(functools.partial(key_value_kernel, per), out_shape=(jax.S...  19.1 us
    unnamed x56, local copies, waits for them, and re-layouts  18.4 us
    all_gather x1, waiting for transfers between devices, shards(): gathered = lax.all_gather(node_input, 'head', axis=0, tiled=True)  15.9 us
    pallas_call x1, Pallas kernels, shards(): pl.pallas_call(functools.partial(far_query_kernel, per), out_shape=jax.Sh...  11.9 us
    all_to_all x1, waiting for transfers between devices, shards(): lax.all_to_all(grad_context, 'head', split_axis=1, concat_axis=0, tiled=T...  10.7 us
  transfers between devices with their start and end apart: 22, of which 7 were waited for; matrix products, arithmetic and copies ran while one was open for 18% of the time, Pallas kernels for 13%

profile of v1, /device:TPU:1, one launch (start us, length us, event | category | flops | bytes accessed | tf_op | source)
XLA Modules:
  0.0 339.9 jit_solution(1946980260659182282)
XLA Ops:
  9.3 6.8 %all-to-all-start = ((bf16[384,8,128]{2,0,1:T(8,128)(2,1)}), bf16[384,8,128]{2,0,1:T(8,128)(2,1)S(1)}, u32[]{:S(2)}, u32[]{:S(2)}) async-start(bf16[384,8,128]{2,0,1:T(8,128)(2,1)} %copy_bitcast_fusion), calls=%async_computation | async-start | bytes 1572864 | tf_op jit(solution)/shard_map/all_to_all | solution.py:344
  18.5 10.7 %all-to-all-done = bf16[384,8,128]{2,0,1:T(8,128)(2,1)S(1)} async-done(((bf16[384,8,128]{2,0,1:T(8,128)(2,1)}), bf16[384,8,128]{2,0,1:T(8,128)(2,1)S(1)}, u32[]{:S(2)}, u32[]{:S(2)}) %all-to-all-start) | async-done | bytes 786464 | tf_op jit(solution)/shard_map/all_to_all | solution.py:344
  32.0 7.2 %all-to-all-start.1 = ((bf16[16,912,128]{2,1,0:T(8,128)(2,1)}), bf16[16,912,128]{2,1,0:T(8,128)(2,1)}, u32[]{:S(2)}, u32[]{:S(2)}) async-start(bf16[16,912,128]{2,1,0:T(8,128)(2,1)} %copy-done.3), calls=%async_computation.1 | async-start | bytes 7471104 | tf_op jit(solution)/shard_map/all_to_all | solution.py:301
  40.2 15.9 %all-gather.4.cloned.1.call-done = bf16[3072,1024]{1,0:T(8,128)(2,1)} async-done(((bf16[384,1024]{1,0:T(8,128)(2,1)}), bf16[3072,1024]{1,0:T(8,128)(2,1)}) %all-gather.4.cloned.1.call-update) | async-done | bytes 6291472 | tf_op jit(solution)/shard_map/all_gather | solution.py:349
  56.1 4.6 %convolution_convert_fusion.2 = bf16[3072,128]{1,0:T(8,128)(2,1)S(1)} fusion(bf16[3072,1024]{1,0:T(8,128)(2,1)} %all-gather.4.cloned.1.call-done, bf16[1024,128]{1,0:T(8,128)(2,1)S(1)} %copy-done.16), kind=kOutput, calls=%fused_computation.4 | convolution fusion | flops 805699584 | bytes 7340032 | tf_op jit(solution)/shard_map/dot_general | solution.py:350
  63.4 22.0 %all-to-all-done.1.grad_ref.far_grad_ref = bf16[16,912,128]{2,1,0:T(8,128)(2,1)} async-done(((bf16[16,912,128]{2,1,0:T(8,128)(2,1)}), bf16[16,912,128]{2,1,0:T(8,128)(2,1)}, u32[]{:S(2)}, u32[]{:S(2)}) %all-to-all-start.1) | async-done | bytes 3735584 | tf_op jit(solution)/shard_map/all_to_all | solution.py:301
  85.4 4.5 %all-to-all-start.2 = ((bf16[16,896,128]{2,1,0:T(8,128)(2,1)}), bf16[16,896,128]{2,1,0:T(8,128)(2,1)}, u32[]{:S(2)}, u32[]{:S(2)}) async-start(bf16[16,896,128]{2,1,0:T(8,128)(2,1)} %copy-done.4), calls=%async_computation.2 | async-start | bytes 7340032 | tf_op jit(solution)/shard_map/all_to_all | solution.py:301
  91.2 4.7 %convolution_convert_fusion.1 = bf16[3072,128]{1,0:T(8,128)(2,1)S(1)} fusion(bf16[3072,1024]{1,0:T(8,128)(2,1)} %all-gather.4.cloned.1.call-done, bf16[1024,128]{1,0:T(8,128)(2,1)S(1)} %copy-done.17), kind=kOutput, calls=%fused_computation.3 | convolution fusion | flops 805699584 | bytes 7340032 | tf_op jit(solution)/shard_map/dot_general | solution.py:353
  96.0 4.7 %convolution_convert_fusion = bf16[3072,128]{1,0:T(8,128)(2,1)S(1)} fusion(bf16[3072,1024]{1,0:T(8,128)(2,1)} %all-gather.4.cloned.1.call-done, bf16[1024,128]{1,0:T(8,128)(2,1)S(1)} %copy-done.19), kind=kOutput, calls=%fused_computation.2 | convolution fusion | flops 805699584 | bytes 7340032 | tf_op jit(solution)/shard_map/dot_general | solution.py:354
  100.6 32.4 %all-to-all-done.2.query_ref.far_query_ref = bf16[16,896,128]{2,1,0:T(8,128)(2,1)} async-done(((bf16[16,896,128]{2,1,0:T(8,128)(2,1)}), bf16[16,896,128]{2,1,0:T(8,128)(2,1)}, u32[]{:S(2)}, u32[]{:S(2)}) %all-to-all-start.2) | async-done | bytes 3670048 | tf_op jit(solution)/shard_map/all_to_all | solution.py:301
  133.0 7.1 %shard_map.105 = f32[112,4,128]{2,1,0:T(4,128)S(1)} custom-call(s32[112]{0:T(128)S(1)} %reshape.332.meta_ref, bf16[16,896,128]{2,1,0:T(8,128)(2,1)} %all-to-all-done.2.query_ref.far_query_ref, bf16[16,912,128]{2,1,0:T(8,128)(2,1)} %all-to-all-done.1.grad_ref.far_grad_ref, bf16[24,128,128]{2,1,0:T(8,128)(2,1)S(1)} %bitcast.88, ...), custom_call_target="tpu_custom_call" | custom-call | flops 1879048192 | bytes 7340032 | tf_op jit(solution)/shard_map/pallas_call | solution.py:376
  140.8 10.2 %all-to-all-start.3 = ((f32[112,4,128]{2,1,0:T(4,128)}), f32[112,4,128]{2,1,0:T(4,128)S(1)}, u32[]{:S(2)}, u32[]{:S(2)}) async-start(f32[112,4,128]{2,1,0:T(4,128)} %copy-done.9), calls=%async_computation.3 | async-start | bytes 458752 | tf_op jit(solution)/shard_map/all_to_all | solution.py:301
  153.2 5.0 %all-to-all-done.3.far_ref = f32[112,4,128]{2,1,0:T(4,128)S(1)} async-done(((f32[112,4,128]{2,1,0:T(4,128)}), f32[112,4,128]{2,1,0:T(4,128)S(1)}, u32[]{:S(2)}, u32[]{:S(2)}) %all-to-all-start.3) | async-done | bytes 229408 | tf_op jit(solution)/shard_map/all_to_all | solution.py:301
  159.0 10.5 %all_to_all.46.far_stats_ref.stats_ref = f32[112,4,128]{2,1,0:T(4,128)S(1)} all-to-all(f32[112,4,128]{2,1,0:T(4,128)S(1)} %get-tuple-element.10), channel_id=1, replica_groups=mesh['seq'=16,'head'=8] {'seq'}, dimensions={0} | all-to-all | bytes 458752 | tf_op jit(solution)/shard_map/all_to_all | solution.py:301
  169.6 11.9 %shard_map.108 = bf16[112,128,128]{2,1,0:T(8,128)(2,1)S(1)} custom-call(s32[112]{0:T(128)S(1)} %reshape.332.meta_ref, bf16[16,896,128]{2,1,0:T(8,128)(2,1)} %all-to-all-done.2.query_ref.far_query_ref, bf16[16,912,128]{2,1,0:T(8,128)(2,1)} %all-to-all-done.1.grad_ref.far_grad_ref, f32[112,4,128]{2,1,0:T(4,128)S(1)} %all_to_all.46.far_stats_ref.stats_ref, ...), custom_call_target="tpu_custom_call" | custom-call | flops 2818572288 | bytes 11010048 | tf_op jit(solution)/shard_map/pallas_call | solution.py:396
  183.2 12.8 %all-to-all-start.5 = ((bf16[112,128,128]{2,1,0:T(8,128)(2,1)}), bf16[112,128,128]{2,1,0:T(8,128)(2,1)}, u32[]{:S(2)}, u32[]{:S(2)}) async-start(bf16[112,128,128]{2,1,0:T(8,128)(2,1)} %copy-done.5), calls=%async_computation.5 | async-start | bytes 7340032 | tf_op jit(solution)/shard_map/all_to_all | solution.py:301
  196.1 19.1 %shard_map.107 = (f32[24,128,128]{2,1,0:T(8,128)}, bf16[24,128,128]{2,1,0:T(8,128)(2,1)S(1)}, bf16[24,128,128]{2,1,0:T(8,128)(2,1)S(1)}) custom-call(s32[112]{0:T(128)S(1)} %reshape.332.meta_ref, bf16[16,896,128]{2,1,0:T(8,128)(2,1)} %all-to-all-done.2.query_ref.far_query_ref, bf16[16,912,128]{2,1,0:T(8,128)(2,1)} %all-to-all-done.1.grad_ref.far_grad_ref, ...), custom_call_target="tpu_custom_call" | custom-call | flops 4697620480 | bytes 11010048 | tf_op jit(solution)/shard_map/pallas_call | solution.py:408
  219.9 5.7 %collective-permute-start.4 = (bf16[384,256]{1,0:T(8,128)(2,1)}, bf16[384,256]{1,0:T(8,128)(2,1)}, u32[]{:S(2)}, u32[]{:S(2)}) collective-permute-start(bf16[384,256]{1,0:T(8,128)(2,1)} %bitcast.18), channel_id=1, source_target_pairs={{0,5},{1,6},{2,7},{3,0},{4,1},{5,2},{6,3},{7,4},{8,13},{9,14},{10,... | collective-permute-start | bytes 589832 | tf_op jit(solution)/shard_map/ppermute | solution.py:312
  229.4 5.6 %collective-permute-start.1 = (bf16[384,256]{1,0:T(8,128)(2,1)}, bf16[384,256]{1,0:T(8,128)(2,1)}, u32[]{:S(2)}, u32[]{:S(2)}) collective-permute-start(bf16[384,256]{1,0:T(8,128)(2,1)} %bitcast.12), channel_id=1, source_target_pairs={{0,2},{1,3},{2,4},{3,5},{4,6},{5,7},{6,0},{7,1},{8,10},{9,11},{10,... | collective-permute-start | bytes 589832 | tf_op jit(solution)/shard_map/ppermute | solution.py:312
  243.2 4.6 %fusion.7 = bf16[1024,256]{0,1:T(8,128)(2,1)S(1)} fusion(bf16[3072,1024]{1,0:T(8,128)(2,1)} %all-gather.4.cloned.1.call-done, bf16[3072,128]{1,0:T(8,128)(2,1)S(1)} %bitcast.102, bf16[3072,128]{1,0:T(8,128)(2,1)S(1)} %bitcast.100), kind=kOutput, calls=%fused_computation.28 | convolution fusion | flops 1614020608 | bytes 8388608 | tf_op jit(solution)/shard_map/dot_general | solution.py:431
  271.1 14.0 %all-to-all-start.6 = ((bf16[16,64,384]{2,1,0:T(8,128)(2,1)}), bf16[16,64,384]{2,1,0:T(8,128)(2,1)S(1)}, u32[]{:S(2)}, u32[]{:S(2)}) async-start(bf16[16,64,384]{2,1,0:T(8,128)(2,1)} %pad_maximum_fusion.1), calls=%async_computation.6 | async-start | bytes 1572864 | tf_op jit(solution)/shard_map/all_to_all | solution.py:301
  303.9 6.8 %gather_fusion.1 = bf16[8,3072,128]{2,1,0:T(8,128)(2,1)} fusion(bf16[8,3072,128]{2,1,0:T(8,128)(2,1)} %bitcast.107, s32[1024]{0:T(1024)S(1)} %pad_clamp_fusion), kind=kCustom, calls=%fused_computation.1 | custom fusion | bytes 12582944 | tf_op jit(solution)/shard_map/gather | solution.py:362
  310.7 5.4 %fusion.28 = (bf16[1,1024,8,128]{3,1,0,2:T(8,128)(2,1)}, bf16[1,1024,8,128]{3,1,0,2:T(8,128)(2,1)S(1)}, bf16[1,1024,8,128]{3,1,0,2:T(8,128)(2,1)}) fusion(bf16[3,1024,8,128]{3,1,0,2:T(8,128)(2,1)} %bitcast.103), kind=kLoop, calls=%fused_computation.111 | loop fusion | bytes 12582912 | tf_op jit(solution)/shard_map/slice | solution.py:451
  321.6 3.9 %copy.85 = bf16[1,1024,8,128]{1,3,2,0:T(8,128)(2,1)} copy(bf16[1,1024,8,128]{3,1,0,2:T(8,128)(2,1)} %get-tuple-element.18) | data formatting | bytes 4194304 | tf_op jit(solution)/shard_map/slice | solution.py:451
  (156 shorter events, 89.2 us)
Async XLA Ops:
  7.2 48.9 %all-gather.4.cloned.1.call-start = ((), (), s32[]{:S(2)}) async-start(), calls=%async_computation.7 | async-start | bytes 7077888 | tf_op jit(solution)/shard_map/all_gather | solution.py:349
  9.3 19.9 %all-to-all-start = ((bf16[384,8,128]{2,0,1:T(8,128)(2,1)}), bf16[384,8,128]{2,0,1:T(8,128)(2,1)S(1)}, u32[]{:S(2)}, u32[]{:S(2)}) async-start(bf16[384,8,128]{2,0,1:T(8,128)(2,1)} %copy_bitcast_fusion), calls=%async_computation | async-start | bytes 1572864 | tf_op jit(solution)/shard_map/all_to_all | solution.py:344
  32.0 53.4 %all-to-all-start.1 = ((bf16[16,912,128]{2,1,0:T(8,128)(2,1)}), bf16[16,912,128]{2,1,0:T(8,128)(2,1)}, u32[]{:S(2)}, u32[]{:S(2)}) async-start(bf16[16,912,128]{2,1,0:T(8,128)(2,1)} %copy-done.3), calls=%async_computation.1 | async-start | bytes 7471104 | tf_op jit(solution)/shard_map/all_to_all | solution.py:301
  39.2 264.7 %all-gather.6.cloned.1.call-start = ((), (), s32[]{:S(2)}) async-start(), calls=%async_computation.8 | async-start | bytes 7077888 | tf_op jit(solution)/shard_map/all_gather | solution.py:360
  60.7 90.3 %copy-start.6 = (bf16[3072,128]{1,0:T(8,128)(2,1)}, bf16[3072,128]{1,0:T(8,128)(2,1)S(1)}, u32[]{:S(2)}) copy-start(bf16[3072,128]{1,0:T(8,128)(2,1)S(1)} %convolution_convert_fusion.2) | copy-start | bytes 2359300
  85.4 47.7 %all-to-all-start.2 = ((bf16[16,896,128]{2,1,0:T(8,128)(2,1)}), bf16[16,896,128]{2,1,0:T(8,128)(2,1)}, u32[]{:S(2)}, u32[]{:S(2)}) async-start(bf16[16,896,128]{2,1,0:T(8,128)(2,1)} %copy-done.4), calls=%async_computation.2 | async-start | bytes 7340032 | tf_op jit(solution)/shard_map/all_to_all | solution.py:301
  140.8 17.4 %all-to-all-start.3 = ((f32[112,4,128]{2,1,0:T(4,128)}), f32[112,4,128]{2,1,0:T(4,128)S(1)}, u32[]{:S(2)}, u32[]{:S(2)}) async-start(f32[112,4,128]{2,1,0:T(4,128)} %copy-done.9), calls=%async_computation.3 | async-start | bytes 458752 | tf_op jit(solution)/shard_map/all_to_all | solution.py:301
  183.2 80.0 %all-to-all-start.5 = ((bf16[112,128,128]{2,1,0:T(8,128)(2,1)}), bf16[112,128,128]{2,1,0:T(8,128)(2,1)}, u32[]{:S(2)}, u32[]{:S(2)}) async-start(bf16[112,128,128]{2,1,0:T(8,128)(2,1)} %copy-done.5), calls=%async_computation.5 | async-start | bytes 7340032 | tf_op jit(solution)/shard_map/all_to_all | solution.py:301
  219.9 20.9 %collective-permute-start.4 = (bf16[384,256]{1,0:T(8,128)(2,1)}, bf16[384,256]{1,0:T(8,128)(2,1)}, u32[]{:S(2)}, u32[]{:S(2)}) collective-permute-start(bf16[384,256]{1,0:T(8,128)(2,1)} %bitcast.18), channel_id=1, source_target_pairs={{0,5},{1,6},{2,7},{3,0},{4,1},{5,2},{6,3},{7,4},{8,13},{9,14},{10,... | collective-permute-start | bytes 589832 | tf_op jit(solution)/shard_map/ppermute | solution.py:312
  226.4 16.7 %copy-start.11 = (bf16[24,128,128]{2,1,0:T(8,128)(2,1)S(1)}, bf16[24,128,128]{2,1,0:T(8,128)(2,1)}, u32[]{:S(2)}) copy-start(bf16[24,128,128]{2,1,0:T(8,128)(2,1)} %copy-done.10) | copy-start | bytes 2359300
  227.6 14.7 %collective-permute-start = (bf16[384,256]{1,0:T(8,128)(2,1)S(1)}, bf16[384,256]{1,0:T(8,128)(2,1)S(1)}, u32[]{:S(2)}, u32[]{:S(2)}) collective-permute-start(bf16[384,256]{1,0:T(8,128)(2,1)S(1)} %bitcast.120), channel_id=1, source_target_pairs={{0,1},{1,2},{2,3},{3,4},{4,5},{5,6},{6,7},{7,0},{8,9},{9,10},{10,1... | collective-permute-start | bytes 589832 | tf_op jit(solution)/shard_map/ppermute | solution.py:312
  229.4 20.6 %collective-permute-start.1 = (bf16[384,256]{1,0:T(8,128)(2,1)}, bf16[384,256]{1,0:T(8,128)(2,1)}, u32[]{:S(2)}, u32[]{:S(2)}) collective-permute-start(bf16[384,256]{1,0:T(8,128)(2,1)} %bitcast.12), channel_id=1, source_target_pairs={{0,2},{1,3},{2,4},{3,5},{4,6},{5,7},{6,0},{7,1},{8,10},{9,11},{10,... | collective-permute-start | bytes 589832 | tf_op jit(solution)/shard_map/ppermute | solution.py:312
  235.8 15.2 %collective-permute-start.2 = (bf16[384,256]{1,0:T(8,128)(2,1)}, bf16[384,256]{1,0:T(8,128)(2,1)}, u32[]{:S(2)}, u32[]{:S(2)}) collective-permute-start(bf16[384,256]{1,0:T(8,128)(2,1)} %bitcast.14), channel_id=1, source_target_pairs={{0,3},{1,4},{2,5},{3,6},{4,7},{5,0},{6,1},{7,2},{8,11},{9,12},{10,... | collective-permute-start | bytes 589832 | tf_op jit(solution)/shard_map/ppermute | solution.py:312
  239.1 13.0 %collective-permute-start.3 = (bf16[384,256]{1,0:T(8,128)(2,1)}, bf16[384,256]{1,0:T(8,128)(2,1)}, u32[]{:S(2)}, u32[]{:S(2)}) collective-permute-start(bf16[384,256]{1,0:T(8,128)(2,1)} %bitcast.16), channel_id=1, source_target_pairs={{0,4},{1,5},{2,6},{3,7},{4,0},{5,1},{6,2},{7,3},{8,12},{9,13},{10,... | collective-permute-start | bytes 589832 | tf_op jit(solution)/shard_map/ppermute | solution.py:312
  240.8 12.5 %collective-permute-start.5 = (bf16[384,256]{1,0:T(8,128)(2,1)}, bf16[384,256]{1,0:T(8,128)(2,1)}, u32[]{:S(2)}, u32[]{:S(2)}) collective-permute-start(bf16[384,256]{1,0:T(8,128)(2,1)} %bitcast.20), channel_id=1, source_target_pairs={{0,6},{1,7},{2,0},{3,1},{4,2},{5,3},{6,4},{7,5},{8,14},{9,15},{10,... | collective-permute-start | bytes 589832 | tf_op jit(solution)/shard_map/ppermute | solution.py:312
  242.3 12.1 %collective-permute-start.6 = (bf16[384,256]{1,0:T(8,128)(2,1)}, bf16[384,256]{1,0:T(8,128)(2,1)}, u32[]{:S(2)}, u32[]{:S(2)}) collective-permute-start(bf16[384,256]{1,0:T(8,128)(2,1)} %bitcast.22), channel_id=1, source_target_pairs={{0,7},{1,0},{2,1},{3,2},{4,3},{5,4},{6,5},{7,6},{8,15},{9,8},{10,9... | collective-permute-start | bytes 589832 | tf_op jit(solution)/shard_map/ppermute | solution.py:312
  271.1 32.0 %all-to-all-start.6 = ((bf16[16,64,384]{2,1,0:T(8,128)(2,1)}), bf16[16,64,384]{2,1,0:T(8,128)(2,1)S(1)}, u32[]{:S(2)}, u32[]{:S(2)}) async-start(bf16[16,64,384]{2,1,0:T(8,128)(2,1)} %pad_maximum_fusion.1), calls=%async_computation.6 | async-start | bytes 1572864 | tf_op jit(solution)/shard_map/all_to_all | solution.py:301
  285.2 8.6 %collective-permute-start.7 = (bf16[384,128]{1,0:T(8,128)(2,1)S(1)}, bf16[384,128]{1,0:T(8,128)(2,1)S(1)}, u32[]{:S(2)}, u32[]{:S(2)}) collective-permute-start(bf16[384,128]{1,0:T(8,128)(2,1)S(1)} %get-tuple-element.37), channel_id=1, source_target_pairs={{0,1},{1,2},{2,3},{3,4},{4,5},{5,6},{6,7},{7,0},{8,9},{9,10},{10,1... | collective-permute-start | bytes 294920 | tf_op jit(solution)/shard_map/ppermute | solution.py:312
  286.4 12.0 %collective-permute-start.8 = (bf16[384,128]{1,0:T(8,128)(2,1)S(1)}, bf16[384,128]{1,0:T(8,128)(2,1)S(1)}, u32[]{:S(2)}, u32[]{:S(2)}) collective-permute-start(bf16[384,128]{1,0:T(8,128)(2,1)S(1)} %get-tuple-element.36), channel_id=1, source_target_pairs={{0,2},{1,3},{2,4},{3,5},{4,6},{5,7},{6,0},{7,1},{8,10},{9,11},{10,... | collective-permute-start | bytes 294920 | tf_op jit(solution)/shard_map/ppermute | solution.py:312
  286.4 12.6 %collective-permute-start.9 = (bf16[384,128]{1,0:T(8,128)(2,1)S(1)}, bf16[384,128]{1,0:T(8,128)(2,1)S(1)}, u32[]{:S(2)}, u32[]{:S(2)}) collective-permute-start(bf16[384,128]{1,0:T(8,128)(2,1)S(1)} %get-tuple-element.35), channel_id=1, source_target_pairs={{0,3},{1,4},{2,5},{3,6},{4,7},{5,0},{6,1},{7,2},{8,11},{9,12},{10,... | collective-permute-start | bytes 294920 | tf_op jit(solution)/shard_map/ppermute | solution.py:312
  288.2 11.5 %collective-permute-start.10 = (bf16[384,128]{1,0:T(8,128)(2,1)S(1)}, bf16[384,128]{1,0:T(8,128)(2,1)S(1)}, u32[]{:S(2)}, u32[]{:S(2)}) collective-permute-start(bf16[384,128]{1,0:T(8,128)(2,1)S(1)} %get-tuple-element.34), channel_id=1, source_target_pairs={{0,4},{1,5},{2,6},{3,7},{4,0},{5,1},{6,2},{7,3},{8,12},{9,13},{10,... | collective-permute-start | bytes 294920 | tf_op jit(solution)/shard_map/ppermute | solution.py:312
  290.5 9.8 %collective-permute-start.11 = (bf16[384,128]{1,0:T(8,128)(2,1)S(1)}, bf16[384,128]{1,0:T(8,128)(2,1)S(1)}, u32[]{:S(2)}, u32[]{:S(2)}) collective-permute-start(bf16[384,128]{1,0:T(8,128)(2,1)S(1)} %get-tuple-element.33), channel_id=1, source_target_pairs={{0,5},{1,6},{2,7},{3,0},{4,1},{5,2},{6,3},{7,4},{8,13},{9,14},{10,... | collective-permute-start | bytes 294920 | tf_op jit(solution)/shard_map/ppermute | solution.py:312
  293.8 7.2 %collective-permute-start.12 = (bf16[384,128]{1,0:T(8,128)(2,1)S(1)}, bf16[384,128]{1,0:T(8,128)(2,1)S(1)}, u32[]{:S(2)}, u32[]{:S(2)}) collective-permute-start(bf16[384,128]{1,0:T(8,128)(2,1)S(1)} %get-tuple-element.32), channel_id=1, source_target_pairs={{0,6},{1,7},{2,0},{3,1},{4,2},{5,3},{6,4},{7,5},{8,14},{9,15},{10,... | collective-permute-start | bytes 294920 | tf_op jit(solution)/shard_map/ppermute | solution.py:312
  298.4 4.0 %collective-permute-start.13 = (bf16[384,128]{1,0:T(8,128)(2,1)S(1)}, bf16[384,128]{1,0:T(8,128)(2,1)S(1)}, u32[]{:S(2)}, u32[]{:S(2)}) collective-permute-start(bf16[384,128]{1,0:T(8,128)(2,1)S(1)} %get-tuple-element.31), channel_id=1, source_target_pairs={{0,7},{1,0},{2,1},{3,2},{4,3},{5,4},{6,5},{7,6},{8,15},{9,8},{10,9... | collective-permute-start | bytes 294920 | tf_op jit(solution)/shard_map/ppermute | solution.py:312
  (19 other events, 76.6 us)
Sparse Core Ops, SparseCore 0:
  9.7 46.3 all-gather.3
  57.8 40.5 all-gather.5

commit v2 on v1

v2 whole, which is shorter than its diff:
```python
import functools

import jax
import jax.numpy as jnp
from jax import lax
from jax.experimental import pallas as pl
from jax.experimental.pallas import tpu as pltpu
from jax.sharding import PartitionSpec as P

HDIM = 64
BLOCK = 128
KB = 4
BF16 = jnp.bfloat16
F32 = jnp.float32
SCALE = HDIM ** (-0.5)
GROUP = 6
VMEM_LIMIT = 56 * 1024 * 1024
VMEM = pl.BlockSpec(memory_space=pltpu.VMEM)
SMEM = pl.BlockSpec(memory_space=pltpu.SMEM)
NT = (((1,), (1,)), ((), ()))
TN = (((0,), (0,)), ((), ()))


def params():
    return pltpu.CompilerParams(vmem_limit_bytes=VMEM_LIMIT)


def cost(flops, moved):
    return pl.CostEstimate(flops=int(flops), bytes_accessed=int(moved), transcendentals=0)


def head_mask(width, scale):
    heads = width // HDIM
    row_head = jnp.arange(heads * BLOCK)[:, None] // BLOCK
    col_head = jnp.arange(width)[None, :] // HDIM
    return jnp.where(row_head == col_head, scale, 0.0).astype(BF16)


def by_head(tile, mask_ref):
    heads = mask_ref.shape[0] // BLOCK
    return jnp.concatenate([tile] * heads, axis=0) * mask_ref[...]


def products(key_heads, value_heads, query, grad):
    heads = key_heads.shape[0] // BLOCK
    scores = lax.dot_general(key_heads, query, NT, preferred_element_type=F32)
    grad_probs = lax.dot_general(value_heads, grad, NT, preferred_element_type=F32)
    return scores.reshape(heads, BLOCK, BLOCK), grad_probs.reshape(heads, BLOCK, BLOCK)


def row_stats(scores, grad_probs):
    top = jnp.max(scores, axis=1, keepdims=True)
    unnorm = jnp.exp(scores - top)
    total = jnp.sum(unnorm, axis=1)
    weighted = jnp.sum(unnorm * grad_probs, axis=1)
    return top[:, 0] + jnp.log(total), weighted / total


def entry_grads(scores, grad_probs, stats):
    heads = scores.shape[0]
    probs = jnp.exp(scores - stats[:heads][:, None, :])
    grad_scores = probs * (grad_probs - stats[heads:][:, None, :])
    flat = (heads * BLOCK, BLOCK)
    return probs.astype(BF16).reshape(flat), grad_scores.astype(BF16).reshape(flat)


def group_of(blocks):
    return GROUP if blocks % GROUP == 0 else 1


def slot_rows(ref, slot, per):
    return ref[slot // per, pl.ds(lax.rem(slot, per) * BLOCK, BLOCK), :]


def remote_stats_kernel(
    per,
    count_ref,
    order_ref,
    meta_ref,
    query_ref,
    grad_ref,
    key_ref,
    value_ref,
    key_mask_ref,
    mask_ref,
    out_ref,
):
    heads = mask_ref.shape[0] // BLOCK
    out_ref[...] = jnp.zeros_like(out_ref)
    n = count_ref[0]

    def step(g, carry):
        picked = [order_ref[jnp.minimum(g * GROUP + u, n - 1)] for u in range(GROUP)]
        pairs = [
            products(
                by_head(key_ref[meta_ref[slot]], key_mask_ref),
                by_head(value_ref[meta_ref[slot]], mask_ref),
                slot_rows(query_ref, slot, per),
                slot_rows(grad_ref, slot, per),
            )
            for slot in picked
        ]
        for slot, pair in zip(picked, pairs):
            lse, delta = row_stats(*pair)
            out_ref[slot, 0:heads] = lse
            out_ref[slot, heads : 2 * heads] = delta
        return carry

    lax.fori_loop(0, pl.cdiv(n, GROUP), step, 0)


def own_stats_kernel(query_ref, grad_ref, key_ref, value_ref, key_mask_ref, mask_ref, out_ref):
    heads = mask_ref.shape[0] // BLOCK
    blocks = query_ref.shape[0]
    group = group_of(blocks)

    def step(g, carry):
        picked = [g * group + u for u in range(group)]
        pairs = [
            products(
                by_head(key_ref[b], key_mask_ref),
                by_head(value_ref[b], mask_ref),
                query_ref[b],
                grad_ref[b],
            )
            for b in picked
        ]
        for b, pair in zip(picked, pairs):
            lse, delta = row_stats(*pair)
            out_ref[b, 0:heads] = lse
            out_ref[b, heads : 2 * heads] = delta
        return carry

    lax.fori_loop(0, blocks // group, step, 0)


def merge_kernel(slot_ref, count_ref, own_ref, far_ref, row_ref, back_ref, lse_ref, delta_ref):
    blocks = own_ref.shape[0]
    heads = own_ref.shape[1] // 2
    back_ref[...] = jnp.zeros_like(back_ref)
    for b in range(blocks):
        for j in range(KB - 1):
            live = count_ref[b] > j + 1
            stats = far_ref[slot_ref[b * (KB - 1) + j]]
            lse_ref[j, b] = jnp.where(live, stats[:heads], -1e30)
            delta_ref[j, b] = jnp.where(live, stats[heads:], 0.0)
    own = own_ref[...]
    lses = [own[:, :heads]] + [lse_ref[j] for j in range(KB - 1)]
    deltas = [own[:, heads:]] + [delta_ref[j] for j in range(KB - 1)]
    top = functools.reduce(jnp.maximum, lses)
    weights = [jnp.exp(v - top) for v in lses]
    total = sum(weights)
    row_ref[:, :heads] = top + jnp.log(total)
    row_ref[:, heads:] = sum(w * d for w, d in zip(weights, deltas)) / total
    for b in range(blocks):
        for j in range(KB - 1):
            back_ref[slot_ref[b * (KB - 1) + j]] = row_ref[b]


def pick_heads(stacked):
    width = stacked.shape[1]
    heads = width // HDIM
    col_head = lax.broadcasted_iota(jnp.int32, (BLOCK, width), 1) // HDIM
    picked = stacked[:BLOCK]
    for h in range(1, heads):
        picked = jnp.where(col_head == h, stacked[h * BLOCK : (h + 1) * BLOCK], picked)
    return picked


def across_heads(tile, mask_ref):
    heads = mask_ref.shape[1] // BLOCK
    return jnp.concatenate([tile] * heads, axis=1) * mask_ref[...]


def far_query_kernel(
    per,
    count_ref,
    order_ref,
    meta_ref,
    query_ref,
    grad_ref,
    stats_ref,
    key_ref,
    value_ref,
    key_across_ref,
    key_mask_ref,
    mask_ref,
    across_mask_ref,
    out_ref,
):
    n = count_ref[0]

    def step(g, carry):
        picked = [order_ref[jnp.minimum(g * GROUP + u, n - 1)] for u in range(GROUP)]
        pairs = [
            products(
                by_head(key_ref[meta_ref[slot]], key_mask_ref),
                by_head(value_ref[meta_ref[slot]], mask_ref),
                slot_rows(query_ref, slot, per),
                slot_rows(grad_ref, slot, per),
            )
            for slot in picked
        ]
        grads = [entry_grads(*pair, stats_ref[slot])[1] for slot, pair in zip(picked, pairs)]
        for slot, grad_scores in zip(picked, grads):
            key_across = across_heads(key_across_ref[meta_ref[slot]], across_mask_ref)
            term = jnp.dot(key_across, grad_scores, preferred_element_type=F32)
            out_ref[slot] = term.astype(BF16)
        return carry

    lax.fori_loop(0, pl.cdiv(n, GROUP), step, 0)


def key_value_kernel(
    per,
    target_ref,
    count_ref,
    order_ref,
    meta_ref,
    far_query_ref,
    far_grad_ref,
    far_stats_ref,
    query_ref,
    grad_ref,
    stats_ref,
    key_ref,
    value_ref,
    key_across_ref,
    key_mask_ref,
    mask_ref,
    across_mask_ref,
    own_term_ref,
    out_ref,
    *rest,
):
    chunk_refs, (key_sum, value_sum) = rest[:-2], rest[-2:]
    blocks = query_ref.shape[0]
    width = query_ref.shape[2]
    group = group_of(blocks)

    def own(g, carry):
        picked = [g * group + u for u in range(group)]
        pairs = [
            products(
                by_head(key_ref[b], key_mask_ref),
                by_head(value_ref[b], mask_ref),
                query_ref[b],
                grad_ref[b],
            )
            for b in picked
        ]
        grads = [entry_grads(*pair, stats_ref[b]) for b, pair in zip(picked, pairs)]
        for b, (probs, grad_scores) in zip(picked, grads):
            key_across = across_heads(key_across_ref[b], across_mask_ref)
            own_term_ref[b] = jnp.dot(key_across, grad_scores, preferred_element_type=F32)
            key_sum[b] = pick_heads(jnp.dot(grad_scores, query_ref[b], preferred_element_type=F32))
            value_sum[b] = pick_heads(jnp.dot(probs, grad_ref[b], preferred_element_type=F32))
        return carry

    lax.fori_loop(0, blocks // group, own, 0)
    n = count_ref[0]

    def far(g, carry):
        places = [g * GROUP + u for u in range(GROUP)]
        picked = [order_ref[jnp.minimum(at, n - 1)] for at in places]
        tiles = [
            (slot_rows(far_query_ref, slot, per), slot_rows(far_grad_ref, slot, per)) for slot in picked
        ]
        pairs = [
            products(
                by_head(key_ref[meta_ref[slot]], key_mask_ref),
                by_head(value_ref[meta_ref[slot]], mask_ref),
                *tile,
            )
            for slot, tile in zip(picked, tiles)
        ]
        grads = [entry_grads(*pair, far_stats_ref[slot]) for slot, pair in zip(picked, pairs)]
        terms = [
            (
                pick_heads(jnp.dot(grad_scores, query, preferred_element_type=F32)),
                pick_heads(jnp.dot(probs, grad, preferred_element_type=F32)),
            )
            for (probs, grad_scores), (query, grad) in zip(grads, tiles)
        ]
        for at, slot, (key_term, value_term) in zip(places, picked, terms):
            block = meta_ref[slot]
            key_sum[block] += jnp.where(at < n, key_term, 0.0)
            value_sum[block] += jnp.where(at < n, value_term, 0.0)
        return carry

    lax.fori_loop(0, pl.cdiv(n, GROUP), far, 0)
    for b in range(blocks):
        rows = slice(b * BLOCK, (b + 1) * BLOCK)
        out_ref[rows, :width] = (key_sum[b] * SCALE).astype(BF16)
        out_ref[rows, width:] = value_sum[b].astype(BF16)
    copy_chunks(target_ref, out_ref, chunk_refs)


def copy_chunks(target_ref, out_ref, chunk_refs):
    for i, chunk_ref in enumerate(chunk_refs):
        rows = chunk_ref.shape[0]
        chunk_ref[...] = out_ref[pl.ds(pl.multiple_of(target_ref[i] * rows, BLOCK), rows), :]


def query_sum_kernel(target_ref, slot_ref, count_ref, own_ref, far_ref, out_ref, *chunk_refs):
    blocks = own_ref.shape[0]

    for b in range(blocks):
        total = own_ref[b]
        for j in range(KB - 1):
            term = far_ref[slot_ref[b * (KB - 1) + j]].astype(F32)
            total = total + jnp.where(count_ref[b] > j + 1, term, 0.0)
        out_ref[b * BLOCK : (b + 1) * BLOCK, :] = total.T.astype(BF16)
    copy_chunks(target_ref, out_ref, chunk_refs)


def rows_kernel(halves, first, width, *refs):
    n = len(halves)
    chunks = jnp.concatenate([ref[...] for ref in refs[:n]], axis=1)
    weight_refs = list(refs[n : n + sum(halves)])
    start_ref, out_ref = refs[-2:]
    depth = out_ref.shape[1] // 2
    sides = ([], [])
    for count in halves:
        pieces = [weight_refs.pop(0) for _ in range(count)]
        for half in range(2):
            if count == 2:
                sides[half].append(pieces[half][:, first : first + width])
            else:
                sides[half].append(pieces[0][half * depth : (half + 1) * depth, first : first + width])
    for half in range(2):
        columns = slice(half * depth, (half + 1) * depth)
        total = lax.dot_general(
            chunks, jnp.concatenate(sides[half], axis=1), NT, preferred_element_type=F32
        )
        if start_ref is not None:
            total = total + start_ref[:, columns]
        out_ref[:, columns] = total.astype(out_ref.dtype)


def first_rows_kernel(halves, first, width, *refs):
    rows_kernel(halves, first, width, *refs[:-1], None, refs[-1])


def project_kernel(places, source_ref, *refs):
    n = len(places)
    weight_ref, query_ref, key_ref, value_ref, out_ref = refs[n:]
    cols = query_ref.shape[1]
    for i, (index, half) in enumerate(places):
        rows = refs[i].shape[0]
        start = source_ref[index] * (rows if half is None else 2 * rows) + (half or 0) * rows
        span = pl.ds(pl.multiple_of(start, 64), rows)
        out_ref[span, :] = refs[i][...]
        result = jnp.dot(refs[i][...], weight_ref[...], preferred_element_type=F32)
        for j, ref in enumerate((query_ref, key_ref, value_ref)):
            ref[span, :] = result[:, j * cols : (j + 1) * cols].astype(BF16)


def pack_kernel(per, peers_step, source_ref, tile_ref, *rest):
    out_ref = rest[-1]
    first = pl.program_id(0) * peers_step
    for p in range(peers_step):
        for r in range(per):
            out_ref[p, r * BLOCK : (r + 1) * BLOCK, :] = tile_ref[source_ref[(first + p) * per + r]]
    if len(rest) == 2:
        out_ref[:, per * BLOCK :, :] = rest[0][...]


def pack(tiles, source, meta, n_seq, per):
    blocks, _, cols = tiles.shape
    peers_step = 4 if n_seq % 4 == 0 else 1
    extra = 0 if meta is None else meta.shape[1]
    rows = per * BLOCK + extra
    in_specs = [pl.BlockSpec((blocks, BLOCK, cols), lambda i, s: (0, 0, 0))]
    operands = [tiles]
    if meta is not None:
        in_specs.append(pl.BlockSpec((peers_step, extra, cols), lambda i, s: (i, 0, 0)))
        operands.append(meta)
    return pl.pallas_call(
        functools.partial(pack_kernel, per, peers_step),
        grid_spec=pltpu.PrefetchScalarGridSpec(
            num_scalar_prefetch=1,
            grid=(n_seq // peers_step,),
            in_specs=in_specs,
            out_specs=pl.BlockSpec((peers_step, rows, cols), lambda i, s: (i, 0, 0)),
        ),
        out_shape=jax.ShapeDtypeStruct((n_seq, rows, cols), BF16),
        compiler_params=params(),
        cost_estimate=cost(0, 2 * 2 * n_seq * rows * cols),
    )(source, *operands)


def seq_exchange(x):
    return lax.all_to_all(x, "seq", split_axis=0, concat_axis=0, tiled=True)


def head_pairs(step, swap):
    n_head = lax.axis_size("head")
    return [(h, (h + 2 * step) % n_head ^ swap) for h in range(n_head)]


def places_from(n_head):
    return [(step, swap) for step in range(n_head // 2) for swap in range(2)]


def head_gather(x):
    n_head = lax.axis_size("head")
    rounds = n_head // 2
    half = x.shape[0] // 2
    found = {0: [x]}
    up = down = x
    for step in range(1, rounds // 2 + 1):
        if 2 * step < rounds:
            up = lax.ppermute(up, "head", head_pairs(1, 0))
            down = lax.ppermute(down, "head", head_pairs(-1, 0))
            found[step], found[rounds - step] = [up], [down]
        else:
            found[step] = [
                lax.ppermute(up[:half], "head", head_pairs(1, 0)),
                lax.ppermute(down[half:], "head", head_pairs(-1, 0)),
            ]
    pieces = {}
    for step, blocks in found.items():
        pieces[step, 0] = blocks
        pieces[step, 1] = [lax.ppermute(b, "head", head_pairs(0, 1)) for b in blocks]
    return pieces


def head_send(chunks):
    order = places_from(lax.axis_size("head"))
    return [
        c if place == (0, 0) else lax.ppermute(c, "head", head_pairs(*place))
        for place, c in zip(order, chunks)
    ]


def shards(node_input, w_query, w_key, w_value, grad_context, key_blocks, counts):
    n_seq = lax.axis_size("seq")
    n_head = lax.axis_size("head")
    me = lax.axis_index("head")
    cols = w_query.shape[1]
    heads = cols // HDIM
    blocks = key_blocks.shape[0]
    nodes = blocks * BLOCK
    per = max(2, 3 * blocks * (KB - 1) // (2 * n_seq) + 1)
    slots = n_seq * per
    key_mask = head_mask(cols, SCALE)
    mask = head_mask(cols, 1.0)
    order = places_from(n_head)
    steps = jnp.array([p[0] for p in order], jnp.int32)
    swaps = jnp.array([p[1] for p in order], jnp.int32)
    targets = (lax.rem(me // 2 + steps, n_head // 2) * 2) + (lax.rem(me, 2) + swaps) % 2
    sources = (lax.rem(me // 2 - steps + n_head // 2, n_head // 2) * 2) + (lax.rem(me, 2) + swaps) % 2

    remote = key_blocks[:, 1:].reshape(-1)
    entries = remote.shape[0]
    owner = remote // blocks
    inner = remote % blocks
    numbers = jnp.arange(entries, dtype=jnp.int32)
    live = (numbers % (KB - 1)) + 1 < counts[numbers // (KB - 1)]
    before = (owner[:, None] == owner[None, :]) & (numbers[None, :] < numbers[:, None])
    slot_of = owner * per + jnp.sum(before.astype(jnp.int32), axis=1)
    taken = slot_of[None, :] == jnp.arange(slots, dtype=jnp.int32)[:, None]
    source = jnp.sum(jnp.where(taken, numbers[None, :] // (KB - 1), 0), axis=1)
    asked = jnp.sum(jnp.where(taken & live[None, :], inner[None, :] + 1, 0), axis=1) - 1
    meta = jnp.broadcast_to(
        jnp.pad(asked.reshape(n_seq, per), ((0, 0), (0, 16 - per)))[:, :, None], (n_seq, 16, cols)
    ).astype(BF16)

    upstream = lax.all_to_all(grad_context, "head", split_axis=1, concat_axis=0, tiled=True)
    grad_tiles = upstream.reshape(blocks, BLOCK, cols)
    far_grads = seq_exchange(pack(grad_tiles, source, meta, n_seq, per))
    far_meta = far_grads[:, per * BLOCK : per * BLOCK + per, 0].astype(jnp.int32).reshape(-1)
    slot_numbers = jnp.arange(slots, dtype=jnp.int32)
    wanted = far_meta >= 0
    ahead = wanted[None, :] & (slot_numbers[None, :] < slot_numbers[:, None])
    rank = jnp.where(wanted, jnp.sum(ahead.astype(jnp.int32), axis=1), slots)
    far_order = jnp.sum(
        jnp.where(rank[None, :] == slot_numbers[:, None], slot_numbers[None, :], 0), axis=1
    )
    far_count = jnp.sum(wanted.astype(jnp.int32)).reshape(1)
    far_list = (far_count, far_order, far_meta)

    found = head_gather(node_input)
    places, pieces = [], []
    for i, place in enumerate(order):
        for half, piece in enumerate(found[place]):
            places.append((i, None if len(found[place]) == 1 else half))
            pieces.append(piece)
    w_all = jnp.concatenate([w_query, w_key, w_value], axis=1)
    queries, keys, values, gathered = pl.pallas_call(
        functools.partial(project_kernel, places),
        out_shape=(jax.ShapeDtypeStruct((nodes, cols), BF16),) * 3
        + (jax.ShapeDtypeStruct((nodes, node_input.shape[1]), BF16),),
        in_specs=[SMEM] + [VMEM] * (len(pieces) + 1),
        out_specs=(VMEM,) * 4,
        compiler_params=params(),
        cost_estimate=cost(6 * nodes * node_input.shape[1] * cols, 4 * nodes * node_input.shape[1]),
    )(sources, *pieces, w_all)
    query_tiles = queries.reshape(blocks, BLOCK, cols)
    far_queries = seq_exchange(pack(query_tiles, source, None, n_seq, per))
    key_tiles = keys.reshape(blocks, BLOCK, cols)
    value_tiles = values.reshape(blocks, BLOCK, cols)

    w_all, _ = lax.optimization_barrier((w_all, queries))
    found = head_gather(w_all)
    halves = [len(found[place]) for place in order]
    w_pieces = [piece for place in order for piece in found[place]]
    far_queries, *w_pieces = lax.optimization_barrier((far_queries, *w_pieces))
    key_across = keys.reshape(blocks, BLOCK, cols).transpose(0, 2, 1)
    across_mask = key_mask.T

    unit_flops = 2 * heads * BLOCK * BLOCK * cols
    tile_bytes = 2 * BLOCK * cols
    stats_shape = jax.ShapeDtypeStruct((slots, 2 * heads, BLOCK), F32)
    own_stats = pl.pallas_call(
        own_stats_kernel,
        out_shape=jax.ShapeDtypeStruct((blocks, 2 * heads, BLOCK), F32),
        in_specs=[VMEM] * 6,
        out_specs=VMEM,
        compiler_params=params(),
        cost_estimate=cost(2 * blocks * unit_flops, 4 * blocks * tile_bytes),
    )(query_tiles, grad_tiles, key_tiles, value_tiles, key_mask, mask)
    far_stats = pl.pallas_call(
        functools.partial(remote_stats_kernel, per),
        out_shape=stats_shape,
        in_specs=[SMEM] * 3 + [VMEM] * 6,
        out_specs=VMEM,
        compiler_params=params(),
        cost_estimate=cost(2 * slots * unit_flops, 2 * slots * tile_bytes),
    )(*far_list, far_queries, far_grads, key_tiles, value_tiles, key_mask, mask)
    row_stats_all, back = pl.pallas_call(
        merge_kernel,
        out_shape=(jax.ShapeDtypeStruct((blocks, 2 * heads, BLOCK), F32), stats_shape),
        in_specs=[SMEM, SMEM, VMEM, VMEM],
        out_specs=(VMEM, VMEM),
        scratch_shapes=[pltpu.VMEM((KB - 1, blocks, heads, BLOCK), F32)] * 2,
        compiler_params=params(),
        cost_estimate=cost(0, 2 * 2 * slots * 4 * heads * BLOCK),
    )(slot_of, counts, own_stats, seq_exchange(far_stats))
    back = seq_exchange(back)

    far_terms = pl.pallas_call(
        functools.partial(far_query_kernel, per),
        out_shape=jax.ShapeDtypeStruct((slots, cols, BLOCK), BF16),
        in_specs=[SMEM] * 3 + [VMEM] * 9,
        out_specs=VMEM,
        compiler_params=params(),
        cost_estimate=cost(3 * slots * unit_flops, 3 * slots * tile_bytes),
    )(
        *far_list,
        far_queries,
        far_grads,
        back,
        key_tiles,
        value_tiles,
        key_across,
        key_mask,
        mask,
        across_mask,
    )
    back_terms = seq_exchange(far_terms)

    rows = nodes // n_head
    tile_shape = (blocks, BLOCK, cols)
    own_terms, grad_key_value, *chunks = pl.pallas_call(
        functools.partial(key_value_kernel, per),
        out_shape=(
            jax.ShapeDtypeStruct((blocks, cols, BLOCK), F32),
            jax.ShapeDtypeStruct((nodes, 2 * cols), BF16),
        )
        + (jax.ShapeDtypeStruct((rows, 2 * cols), BF16),) * n_head,
        in_specs=[SMEM] * 4 + [VMEM] * 12,
        out_specs=(VMEM,) * (2 + n_head),
        scratch_shapes=[
            pltpu.VMEM(tile_shape, F32),
            pltpu.VMEM(tile_shape, F32),
        ],
        compiler_params=params(),
        cost_estimate=cost(5 * slots * unit_flops, 3 * slots * tile_bytes),
    )(
        targets,
        *far_list,
        far_queries,
        far_grads,
        back,
        query_tiles,
        grad_tiles,
        row_stats_all,
        key_tiles,
        value_tiles,
        key_across,
        key_mask,
        mask,
        across_mask,
    )

    contract_rows = (((0,), (0,)), ((), ()))
    chunks = head_send(chunks)
    term_key_value = lax.dot_general(gathered, grad_key_value, contract_rows, preferred_element_type=F32)
    width = w_query.shape[0]
    summed = pl.pallas_call(
        functools.partial(first_rows_kernel, halves, cols, 2 * cols),
        out_shape=jax.ShapeDtypeStruct((rows, width), F32),
        in_specs=[VMEM] * (len(chunks) + len(w_pieces)),
        out_specs=VMEM,
        compiler_params=params(),
        cost_estimate=cost(2 * rows * width * 2 * cols * n_head, 2 * width * 3 * cols * n_head),
    )(*chunks, *w_pieces)

    back_terms, summed = lax.optimization_barrier((back_terms, summed))
    grad_query, *chunks = pl.pallas_call(
        query_sum_kernel,
        out_shape=(jax.ShapeDtypeStruct((nodes, cols), BF16),)
        + (jax.ShapeDtypeStruct((rows, cols), BF16),) * n_head,
        in_specs=[SMEM] * 3 + [VMEM] * 2,
        out_specs=(VMEM,) * (1 + n_head),
        compiler_params=params(),
        cost_estimate=cost(0, slots * tile_bytes),
    )(targets, slot_of, counts, own_terms, back_terms)
    term_query = lax.dot_general(gathered, grad_query, contract_rows, preferred_element_type=F32)
    weight_terms = jnp.concatenate([term_query, term_key_value], axis=1).astype(BF16)
    weight_terms = seq_exchange(weight_terms.reshape(n_seq, -1, 3 * cols))
    weight_grads = jnp.sum(weight_terms.astype(F32), axis=0)
    chunks = head_send(chunks)
    grad_input = pl.pallas_call(
        functools.partial(rows_kernel, halves, 0, cols),
        grid=(1,),
        out_shape=jax.ShapeDtypeStruct((rows, width), BF16),
        in_specs=[VMEM] * n_head
        + [pl.BlockSpec((p.shape[0], cols), lambda i: (0, 0)) for p in w_pieces]
        + [VMEM],
        out_specs=VMEM,
        compiler_params=params(),
        cost_estimate=cost(2 * rows * width * cols * n_head, 2 * width * cols * n_head),
    )(*chunks, *w_pieces, summed)
    return (
        grad_input,
        weight_grads[:, :cols],
        weight_grads[:, cols : 2 * cols],
        weight_grads[:, 2 * cols :],
    )


def solution(mesh):
    placed = (
        P(("seq", "head"), None),
        P(None, "head"),
        P(None, "head"),
        P(None, "head"),
        P(("seq", "head"), None),
        P("seq", None),
        P("seq"),
    )
    return jax.shard_map(
        shards,
        mesh=mesh,
        in_specs=placed,
        out_specs=(P(("seq", "head"), None), P("seq", "head"), P("seq", "head"), P("seq", "head")),
        check_vma=False,
    )
```

time: 342 us -> 280 us (0.82)
  local copies, waits for them, and re-layouts: 64.1 us -> 14.1 us
  Pallas kernels: 45.6 us -> 72.7 us
  matrix products: 29.3 us -> 8.11 us
  starting transfers between devices: 79.7 us -> 99.9 us
  waiting for transfers between devices: 91.4 us -> 75.1 us
  between operations: 14.6 us -> 1.21 us
  blocking collectives: 10.5 us -> 0 us
  other arithmetic: 4.67 us -> 8.43 us
    ppermute x14 -> x32, waiting for transfers between devices: 4.69 us -> 52.6 us  [the longest x2 17.5 us: head_gather(): up = lax.ppermute(up, 'head', head_pairs(1, 0))]
    all_to_all x5 -> x6, waiting for transfers between devices: 59.4 us -> 14.7 us  [seq_exchange(): return lax.all_to_all(x, 'seq', split_axis=0, concat_axis=0, tiled=True)]
    ppermute x14 -> x32, starting transfers between devices: 24.1 us -> 54.2 us  [the longest x14 27.6 us: head_send(): lax.ppermute(c, 'head', head_pairs(*place))]
    pallas_call x3 -> x6, Pallas kernels: 4.49 us -> 33.5 us  [the longest x1 9.91 us: shards(): pl.pallas_call(functools.partial(project_kernel, places), out_shape=(jax....]
    dot_general x6 -> x0, matrix products: 20.9 us -> none  [the longest x1 4.69 us: shards(): keys = jnp.dot(gathered, w_key, preferred_element_type=F32).astype(BF16)]
    slice x5 -> x4, local copies, waits for them, and re-layouts: 17.6 us -> 1.3 us  [the longest x2 1.23 us: head_gather(): down[half:]]
    all_gather x2 -> x0, waiting for transfers between devices: 15.9 us -> none  [the longest x1 15.9 us: shards(): gathered = lax.all_gather(node_input, 'head', axis=0, tiled=True)]
    unnamed x56 -> x94, local copies, waits for them, and re-layouts: 18.4 us -> 6.71 us
  transfers between devices with their start and end apart: 22 -> 39, of which waited for: 7 -> 17; matrix products, arithmetic and copies ran while one was open for 18% -> 6% of each run, Pallas kernels for 13% -> 16%
where the time goes in v2:
time: 280 us
  starting transfers between devices  99.9 us (36%)
  waiting for transfers between devices  75.1 us (27%)
  Pallas kernels  72.7 us (26%)
  local copies, waits for them, and re-layouts  14.1 us (5%)
  other arithmetic  8.43 us (3%)
  matrix products  8.11 us (3%)
    all_to_all x6, starting transfers between devices, seq_exchange(): return lax.all_to_all(x, 'seq', split_axis=0, concat_axis=0, tiled=True)  38.9 us
    ppermute x14, starting transfers between devices, head_send(): lax.ppermute(c, 'head', head_pairs(*place))  27.6 us
    ppermute x2, waiting for transfers between devices, head_gather(): up = lax.ppermute(up, 'head', head_pairs(1, 0))  17.5 us
    ppermute x10, starting transfers between devices, head_gather(): lax.ppermute(b, 'head', head_pairs(0, 1))  16.3 us
    ppermute x2, waiting for transfers between devices, head_gather(): down = lax.ppermute(down, 'head', head_pairs(-1, 0))  15.3 us
    all_to_all x6, waiting for transfers between devices, seq_exchange(): return lax.all_to_all(x, 'seq', split_axis=0, concat_axis=0, tiled=True)  14.7 us
    pallas_call x1, Pallas kernels, shards(): pl.pallas_call(functools.partial(key_value_kernel, per), out_shape=(jax.S...  14.5 us
    ppermute x14, waiting for transfers between devices, head_send(): lax.ppermute(c, 'head', head_pairs(*place))  13.7 us
  transfers between devices with their start and end apart: 39, of which 17 were waited for; matrix products, arithmetic and copies ran while one was open for 6% of the time, Pallas kernels for 16%

profile of v2, /device:TPU:1, one launch (start us, length us, event | category | flops | bytes accessed | tf_op | source)
XLA Modules:
  0.0 279.6 jit_solution(17127177549250724214)
XLA Ops:
  2.8 6.8 %all-to-all-start = ((bf16[384,8,128]{2,0,1:T(8,128)(2,1)}), bf16[384,8,128]{2,0,1:T(8,128)(2,1)S(1)}, u32[]{:S(2)}, u32[]{:S(2)}) async-start(bf16[384,8,128]{2,0,1:T(8,128)(2,1)} %copy_bitcast_fusion), calls=%async_computation | async-start | bytes 1572864 | tf_op jit(solution)/shard_map/all_to_all | solution.py:470
  14.2 7.7 %all-to-all-done = bf16[384,8,128]{2,0,1:T(8,128)(2,1)S(1)} async-done(((bf16[384,8,128]{2,0,1:T(8,128)(2,1)}), bf16[384,8,128]{2,0,1:T(8,128)(2,1)S(1)}, u32[]{:S(2)}, u32[]{:S(2)}) %all-to-all-start) | async-done | bytes 786464 | tf_op jit(solution)/shard_map/all_to_all | solution.py:470
  22.8 4.6 %shard_map.120 = bf16[16,912,128]{2,1,0:T(8,128)(2,1)} custom-call(s32[112]{0:T(128)} %get-tuple-element.85.source_ref, bf16[24,128,128]{2,1,0:T(8,128)(2,1)} %bitcast.26, bf16[16,16,128]{2,1,0:T(8,128)(2,1)} %broadcast_in_dim.77.rest_0_), custom_call_target="tpu_custom_call" | custom-call | bytes 7471104 | tf_op jit(solution)/shard_map/pallas_call | solution.py:379
  27.4 6.9 %all-to-all-start.1 = ((bf16[16,912,128]{2,1,0:T(8,128)(2,1)}), bf16[16,912,128]{2,1,0:T(8,128)(2,1)}, u32[]{:S(2)}, u32[]{:S(2)}) async-start(bf16[16,912,128]{2,1,0:T(8,128)(2,1)} %shard_map.120), calls=%async_computation.1 | async-start | bytes 7471104 | tf_op jit(solution)/shard_map/all_to_all | solution.py:394
  37.1 16.7 %collective-permute-done.1.refs_2_ = bf16[384,1024]{1,0:T(8,128)(2,1)S(1)} collective-permute-done((bf16[384,1024]{1,0:T(8,128)(2,1)}, bf16[384,1024]{1,0:T(8,128)(2,1)S(1)}, u32[]{:S(2)}, u32[]{:S(2)}) %collective-permute-start.1) | collective-permute-done | bytes 786464 | tf_op jit(solution)/shard_map/ppermute | solution.py:414
  69.0 9.9 %shard_map.121 = (bf16[3072,128]{1,0:T(8,128)(2,1)}, bf16[3072,128]{1,0:T(8,128)(2,1)}, bf16[3072,128]{1,0:T(8,128)(2,1)}, bf16[3072,1024]{1,0:T(8,128)(2,1)}) custom-call(s32[8]{0:T(128)} %get-tuple-element.86.source_ref, bf16[384,1024]{1,0:T(8,128)(2,1)} %refs_0_.1, bf16[384,1024]{1,0:T(8,128)(2,1)} %collective-permute-done.refs_1_, ...), custom_call_target="tpu_custom_call" | custom-call | flops 2415919104 | bytes 12582912 | tf_op jit(solution)/shard_map/pallas_call | solution.py:491
  78.9 4.2 %shard_map.122 = bf16[16,896,128]{2,1,0:T(8,128)(2,1)} custom-call(s32[112]{0:T(128)} %get-tuple-element.85.source_ref, bf16[24,128,128]{2,1,0:T(8,128)(2,1)} %bitcast.37), custom_call_target="tpu_custom_call" | custom-call | bytes 7340032 | tf_op jit(solution)/shard_map/pallas_call | solution.py:379
  83.0 10.0 %all-to-all-start.2 = ((bf16[16,896,128]{2,1,0:T(8,128)(2,1)}), bf16[16,896,128]{2,1,0:T(8,128)(2,1)}, u32[]{:S(2)}, u32[]{:S(2)}) async-start(bf16[16,896,128]{2,1,0:T(8,128)(2,1)} %shard_map.122), calls=%async_computation.2 | async-start | bytes 7340032 | tf_op jit(solution)/shard_map/all_to_all | solution.py:394
  94.6 15.3 %collective-permute-done.13.refs_16_ = bf16[1024,384]{1,0:T(8,128)(2,1)S(1)} collective-permute-done((bf16[1024,384]{1,0:T(8,128)(2,1)S(1)}, bf16[1024,384]{1,0:T(8,128)(2,1)S(1)}, u32[]{:S(2)}, u32[]{:S(2)}) %collective-permute-start.13) | collective-permute-done | bytes 786464 | tf_op jit(solution)/shard_map/ppermute | solution.py:415
  129.6 6.6 %all-to-all-done.2.query_ref.far_query_ref = bf16[16,896,128]{2,1,0:T(8,128)(2,1)} async-done(((bf16[16,896,128]{2,1,0:T(8,128)(2,1)}), bf16[16,896,128]{2,1,0:T(8,128)(2,1)}, u32[]{:S(2)}, u32[]{:S(2)}) %all-to-all-start.2) | async-done | bytes 3670048 | tf_op jit(solution)/shard_map/all_to_all | solution.py:394
  136.2 8.2 %shard_map.124 = f32[112,4,128]{2,1,0:T(4,128)} custom-call(s32[1]{0:T(128)} %bitcast.3.count_ref, s32[112]{0:T(128)} %select_reduce_fusion.order_ref, s32[112]{0:T(128)} %copy-done.28, bf16[16,896,128]{2,1,0:T(8,128)(2,1)} %all-to-all-done.2.query_ref.far_query_ref, bf16[16,912,128]{2,1,0:T(8,128)(2,1)} %all-to-all-done.1.grad_ref.far_grad_ref, ...), custom_call_target="tpu_custom_call" | custom-call | flops 1879048192 | bytes 7340032 | tf_op jit(solution)/shard_map/pallas_call | solution.py:524
  144.4 6.7 %all-to-all-start.3 = ((f32[112,4,128]{2,1,0:T(4,128)}), f32[112,4,128]{2,1,0:T(4,128)S(1)}, u32[]{:S(2)}, u32[]{:S(2)}) async-start(f32[112,4,128]{2,1,0:T(4,128)} %shard_map.124), calls=%async_computation.3 | async-start | bytes 458752 | tf_op jit(solution)/shard_map/all_to_all | solution.py:394
  151.1 4.2 %shard_map.123.own_ref = f32[24,4,128]{2,1,0:T(4,128)} custom-call(bf16[24,128,128]{2,1,0:T(8,128)(2,1)} %bitcast.38, bf16[24,128,128]{2,1,0:T(8,128)(2,1)} %bitcast.27, bf16[24,128,128]{2,1,0:T(8,128)(2,1)} %bitcast.22, bf16[24,128,128]{2,1,0:T(8,128)(2,1)} %bitcast.30, bf16[256,128]{1,0:T(8,128)(2,1)} %get-tuple-element.94.key_mask_ref, ...), custom_call_target="tpu_custom_call" | custom-call | flops 402653184 | bytes 3145728 | tf_op jit(solution)/shard_map/pallas_call | solution.py:516
  166.6 5.2 %all-to-all-done.4.far_stats_ref.stats_ref = f32[112,4,128]{2,1,0:T(4,128)S(1)} async-done(((f32[112,4,128]{2,1,0:T(4,128)}), f32[112,4,128]{2,1,0:T(4,128)S(1)}, u32[]{:S(2)}, u32[]{:S(2)}) %all-to-all-start.4) | async-done | bytes 229408 | tf_op jit(solution)/shard_map/all_to_all | solution.py:394
  172.5 10.2 %shard_map.127 = bf16[112,128,128]{2,1,0:T(8,128)(2,1)} custom-call(s32[1]{0:T(128)} %bitcast.3.count_ref, s32[112]{0:T(128)} %select_reduce_fusion.order_ref, s32[112]{0:T(128)} %copy-done.28, bf16[16,896,128]{2,1,0:T(8,128)(2,1)} %all-to-all-done.2.query_ref.far_query_ref, bf16[16,912,128]{2,1,0:T(8,128)(2,1)} %all-to-all-done.1.grad_ref.far_grad_ref, ...), custom_call_target="tpu_custom_call" | custom-call | flops 2818572288 | bytes 11010048 | tf_op jit(solution)/shard_map/pallas_call | solution.py:543
  182.7 5.0 %all-to-all-start.5 = ((bf16[112,128,128]{2,1,0:T(8,128)(2,1)}), bf16[112,128,128]{2,1,0:T(8,128)(2,1)}, u32[]{:S(2)}, u32[]{:S(2)}) async-start(bf16[112,128,128]{2,1,0:T(8,128)(2,1)} %shard_map.127), calls=%async_computation.5 | async-start | bytes 7340032 | tf_op jit(solution)/shard_map/all_to_all | solution.py:394
  188.2 14.5 %shard_map.126 = (f32[24,128,128]{2,1,0:T(8,128)}, bf16[3072,256]{1,0:T(8,128)(2,1)}, bf16[384,256]{1,0:T(8,128)(2,1)}, bf16[384,256]{1,0:T(8,128)(2,1)}, bf16[3...) custom-call(s32[8]{0:T(128)} %fusion.9.target_ref, ...), custom_call_target="tpu_custom_call" | custom-call | flops 4697620480 | bytes 11010048 | tf_op jit(solution)/shard_map/pallas_call | solution.py:566
  202.7 7.1 %collective-permute-start.18 = (bf16[384,256]{1,0:T(8,128)(2,1)}, bf16[384,256]{1,0:T(8,128)(2,1)S(1)}, u32[]{:S(2)}, u32[]{:S(2)}) collective-permute-start(bf16[384,256]{1,0:T(8,128)(2,1)} %get-tuple-element.52), channel_id=1, source_target_pairs={{0,1},{1,0},{2,3},{3,2},{4,5},{5,4},{6,7},{7,6},{8,9},{9,8},{10,11... | collective-permute-start | bytes 589832 | tf_op jit(solution)/shard_map/ppermute | solution.py:432
  210.1 4.9 %collective-permute-start.20 = (bf16[384,256]{1,0:T(8,128)(2,1)}, bf16[384,256]{1,0:T(8,128)(2,1)S(1)}, u32[]{:S(2)}, u32[]{:S(2)}) collective-permute-start(bf16[384,256]{1,0:T(8,128)(2,1)} %get-tuple-element.54), channel_id=1, source_target_pairs={{0,3},{1,2},{2,5},{3,4},{4,7},{5,6},{6,1},{7,0},{8,11},{9,10},{10,... | collective-permute-start | bytes 589832 | tf_op jit(solution)/shard_map/ppermute | solution.py:432
  235.5 6.3 %shard_map.128.refs_18_ = f32[384,1024]{1,0:T(8,128)} custom-call(bf16[384,256]{1,0:T(8,128)(2,1)} %get-tuple-element.51.refs_0_, bf16[384,256]{1,0:T(8,128)(2,1)} %copy-done.14, bf16[384,256]{1,0:T(8,128)(2,1)} %copy-done.15, bf16[384,256]{1,0:T(8,128)(2,1)} %copy-done.16, bf16[384,256]{1,0:T(8,128)(2,1)} %copy-done.17, bf16[384,256]{1,0:T(8,128)(2,1)} %copy-done.18, ...), custom_call_target="tpu_custom_call" | custom-call | flops 1610612736 | bytes 6291456 | tf_op jit(solution)/shard_map/pallas_call | solution.py:602
  241.9 4.3 %shard_map.129 = (bf16[3072,128]{1,0:T(8,128)(2,1)}, bf16[384,128]{1,0:T(8,128)(2,1)}, bf16[384,128]{1,0:T(8,128)(2,1)}, bf16[384,128]{1,0:T(8,128)(2,1)}, bf16[...) custom-call(s32[8]{0:T(128)} %fusion.9.target_ref, ...), custom_call_target="tpu_custom_call" | custom-call | bytes 3670016 | tf_op jit(solution)/shard_map/pallas_call | solution.py:612
  246.2 4.9 %convolution_convert_fusion.1 = bf16[1024,128]{1,0:T(8,128)(2,1)S(1)} fusion(bf16[3072,1024]{1,0:T(8,128)(2,1)} %get-tuple-element.79, bf16[3072,128]{1,0:T(8,128)(2,1)} %get-tuple-element.80), kind=kOutput, calls=%fused_computation.3 | convolution fusion | flops 805437440 | bytes 7340032 | tf_op jit(solution)/shard_map/dot_general | solution.py:621
  252.1 6.5 %all-to-all-start.6 = ((bf16[16,64,384]{2,1,0:T(8,128)(2,1)}), bf16[16,64,384]{2,1,0:T(8,128)(2,1)S(1)}, u32[]{:S(2)}, u32[]{:S(2)}) async-start(bf16[16,64,384]{2,1,0:T(8,128)(2,1)} %pad_maximum_fusion), calls=%async_computation.6 | async-start | bytes 1572864 | tf_op jit(solution)/shard_map/all_to_all | solution.py:394
  274.5 4.3 %shard_map.130 = bf16[384,1024]{1,0:T(8,128)(2,1)} custom-call(bf16[384,128]{1,0:T(8,128)(2,1)} %get-tuple-element.70.refs_0_, bf16[384,128]{1,0:T(8,128)(2,1)} %copy-done.21, bf16[384,128]{1,0:T(8,128)(2,1)} %copy-done.22, bf16[384,128]{1,0:T(8,128)(2,1)} %copy-done.23, bf16[384,128]{1,0:T(8,128)(2,1)} %copy-done.24, bf16[384,128]{1,0:T(8,128)(2,1)} %copy-done.25, ...), custom_call_target="tpu_custom_call" | custom-call | flops 805306368 | bytes 2097152 | tf_op jit(solution)/shard_map/pallas_call | solution.py:626
  (204 shorter events, 97.3 us)
Async XLA Ops:
  2.8 19.1 %all-to-all-start = ((bf16[384,8,128]{2,0,1:T(8,128)(2,1)}), bf16[384,8,128]{2,0,1:T(8,128)(2,1)S(1)}, u32[]{:S(2)}, u32[]{:S(2)}) async-start(bf16[384,8,128]{2,0,1:T(8,128)(2,1)} %copy_bitcast_fusion), calls=%async_computation | async-start | bytes 1572864 | tf_op jit(solution)/shard_map/all_to_all | solution.py:470
  27.4 55.6 %all-to-all-start.1 = ((bf16[16,912,128]{2,1,0:T(8,128)(2,1)}), bf16[16,912,128]{2,1,0:T(8,128)(2,1)}, u32[]{:S(2)}, u32[]{:S(2)}) async-start(bf16[16,912,128]{2,1,0:T(8,128)(2,1)} %shard_map.120), calls=%async_computation.1 | async-start | bytes 7471104 | tf_op jit(solution)/shard_map/all_to_all | solution.py:394
  34.4 19.5 %collective-permute-start.1 = (bf16[384,1024]{1,0:T(8,128)(2,1)}, bf16[384,1024]{1,0:T(8,128)(2,1)S(1)}, u32[]{:S(2)}, u32[]{:S(2)}) collective-permute-start(bf16[384,1024]{1,0:T(8,128)(2,1)} %refs_0_.1), channel_id=1, source_target_pairs={{0,2},{1,3},{2,4},{3,5},{4,6},{5,7},{6,0},{7,1},{8,10},{9,11},{10,... | collective-permute-start | bytes 2359304 | tf_op jit(solution)/shard_map/ppermute | solution.py:414
  34.7 19.2 %collective-permute-start.4 = (bf16[384,1024]{1,0:T(8,128)(2,1)}, bf16[384,1024]{1,0:T(8,128)(2,1)}, u32[]{:S(2)}, u32[]{:S(2)}) collective-permute-start(bf16[384,1024]{1,0:T(8,128)(2,1)} %refs_0_.1), channel_id=1, source_target_pairs={{0,6},{1,7},{2,0},{3,1},{4,2},{5,3},{6,4},{7,5},{8,14},{9,15},{10,... | collective-permute-start | bytes 2359304 | tf_op jit(solution)/shard_map/ppermute | solution.py:415
  53.9 10.0 %collective-permute-start.3 = (bf16[192,1024]{1,0:T(8,128)(2,1)S(1)}, bf16[192,1024]{1,0:T(8,128)(2,1)S(1)}, u32[]{:S(2)}, u32[]{:S(2)}) collective-permute-start(bf16[192,1024]{1,0:T(8,128)(2,1)S(1)} %slice.39), channel_id=1, source_target_pairs={{0,2},{1,3},{2,4},{3,5},{4,6},{5,7},{6,0},{7,1},{8,10},{9,11},{10,... | collective-permute-start | bytes 1179656 | tf_op jit(solution)/shard_map/ppermute | solution.py:419
  55.2 11.5 %collective-permute-start.5 = (bf16[192,1024]{1,0:T(8,128)(2,1)S(1)}, bf16[192,1024]{1,0:T(8,128)(2,1)}, u32[]{:S(2)}, u32[]{:S(2)}) collective-permute-start(bf16[192,1024]{1,0:T(8,128)(2,1)S(1)} %slice.40), channel_id=1, source_target_pairs={{0,6},{1,7},{2,0},{3,1},{4,2},{5,3},{6,4},{7,5},{8,14},{9,15},{10,... | collective-permute-start | bytes 1179656 | tf_op jit(solution)/shard_map/ppermute | solution.py:420
  57.7 10.1 %collective-permute-start = (bf16[384,1024]{1,0:T(8,128)(2,1)}, bf16[384,1024]{1,0:T(8,128)(2,1)}, u32[]{:S(2)}, u32[]{:S(2)}) collective-permute-start(bf16[384,1024]{1,0:T(8,128)(2,1)} %refs_0_.1), channel_id=1, source_target_pairs={{0,1},{1,0},{2,3},{3,2},{4,5},{5,4},{6,7},{7,6},{8,9},{9,8},{10,11... | collective-permute-start | bytes 2359304 | tf_op jit(solution)/shard_map/ppermute | solution.py:425
  83.0 53.1 %all-to-all-start.2 = ((bf16[16,896,128]{2,1,0:T(8,128)(2,1)}), bf16[16,896,128]{2,1,0:T(8,128)(2,1)}, u32[]{:S(2)}, u32[]{:S(2)}) async-start(bf16[16,896,128]{2,1,0:T(8,128)(2,1)} %shard_map.122), calls=%async_computation.2 | async-start | bytes 7340032 | tf_op jit(solution)/shard_map/all_to_all | solution.py:394
  93.1 16.8 %collective-permute-start.13 = (bf16[1024,384]{1,0:T(8,128)(2,1)S(1)}, bf16[1024,384]{1,0:T(8,128)(2,1)S(1)}, u32[]{:S(2)}, u32[]{:S(2)}) collective-permute-start(bf16[1024,384]{1,0:T(8,128)(2,1)S(1)} %copy-done.6), channel_id=1, source_target_pairs={{0,6},{1,7},{2,0},{3,1},{4,2},{5,3},{6,4},{7,5},{8,14},{9,15},{10,... | collective-permute-start | bytes 2359304 | tf_op jit(solution)/shard_map/ppermute | solution.py:415
  94.1 19.9 %collective-permute-start.10 = (bf16[1024,384]{1,0:T(8,128)(2,1)S(1)}, bf16[1024,384]{1,0:T(8,128)(2,1)S(1)}, u32[]{:S(2)}, u32[]{:S(2)}) collective-permute-start(bf16[1024,384]{1,0:T(8,128)(2,1)S(1)} %copy-done.6), channel_id=1, source_target_pairs={{0,2},{1,3},{2,4},{3,5},{4,6},{5,7},{6,0},{7,1},{8,10},{9,11},{10,... | collective-permute-start | bytes 2359304 | tf_op jit(solution)/shard_map/ppermute | solution.py:414
  110.0 10.5 %collective-permute-start.14 = (bf16[512,384]{1,0:T(8,128)(2,1)S(1)}, bf16[512,384]{1,0:T(8,128)(2,1)S(1)}, u32[]{:S(2)}, u32[]{:S(2)}) collective-permute-start(bf16[512,384]{1,0:T(8,128)(2,1)S(1)} %slice.42), channel_id=1, source_target_pairs={{0,6},{1,7},{2,0},{3,1},{4,2},{5,3},{6,4},{7,5},{8,14},{9,15},{10,... | collective-permute-start | bytes 1179656 | tf_op jit(solution)/shard_map/ppermute | solution.py:420
  114.9 14.6 %collective-permute-start.9 = (bf16[1024,384]{1,0:T(8,128)(2,1)S(1)}, bf16[1024,384]{1,0:T(8,128)(2,1)}, u32[]{:S(2)}, u32[]{:S(2)}) collective-permute-start(bf16[1024,384]{1,0:T(8,128)(2,1)S(1)} %copy-done.6), channel_id=1, source_target_pairs={{0,1},{1,0},{2,3},{3,2},{4,5},{5,4},{6,7},{7,6},{8,9},{9,8},{10,11... | collective-permute-start | bytes 2359304 | tf_op jit(solution)/shard_map/ppermute | solution.py:425
  118.1 11.5 %collective-permute-start.17 = (bf16[1024,384]{1,0:T(8,128)(2,1)S(1)}, bf16[1024,384]{1,0:T(8,128)(2,1)}, u32[]{:S(2)}, u32[]{:S(2)}) collective-permute-start(bf16[1024,384]{1,0:T(8,128)(2,1)S(1)} %collective-permute-done.13.refs_16_), channel_id=1, source_target_pairs={{0,1},{1,0},{2,3},{3,2},{4,5},{5,4},{6,7},{7,6},{8,9},{9,8},{10,11... | collective-permute-start | bytes 2359304 | tf_op jit(solution)/shard_map/ppermute | solution.py:425
  118.1 11.5 %collective-permute-start.11 = (bf16[1024,384]{1,0:T(8,128)(2,1)S(1)}, bf16[1024,384]{1,0:T(8,128)(2,1)}, u32[]{:S(2)}, u32[]{:S(2)}) collective-permute-start(bf16[1024,384]{1,0:T(8,128)(2,1)S(1)} %collective-permute-done.10.refs_10_), channel_id=1, source_target_pairs={{0,1},{1,0},{2,3},{3,2},{4,5},{5,4},{6,7},{7,6},{8,9},{9,8},{10,11... | collective-permute-start | bytes 2359304 | tf_op jit(solution)/shard_map/ppermute | solution.py:425
  144.4 13.8 %all-to-all-start.3 = ((f32[112,4,128]{2,1,0:T(4,128)}), f32[112,4,128]{2,1,0:T(4,128)S(1)}, u32[]{:S(2)}, u32[]{:S(2)}) async-start(f32[112,4,128]{2,1,0:T(4,128)} %shard_map.124), calls=%async_computation.3 | async-start | bytes 458752 | tf_op jit(solution)/shard_map/all_to_all | solution.py:394
  160.9 10.9 %all-to-all-start.4 = ((f32[112,4,128]{2,1,0:T(4,128)}), f32[112,4,128]{2,1,0:T(4,128)S(1)}, u32[]{:S(2)}, u32[]{:S(2)}) async-start(f32[112,4,128]{2,1,0:T(4,128)} %get-tuple-element.48), calls=%async_computation.4 | async-start | bytes 458752 | tf_op jit(solution)/shard_map/all_to_all | solution.py:394
  182.7 59.2 %all-to-all-start.5 = ((bf16[112,128,128]{2,1,0:T(8,128)(2,1)}), bf16[112,128,128]{2,1,0:T(8,128)(2,1)}, u32[]{:S(2)}, u32[]{:S(2)}) async-start(bf16[112,128,128]{2,1,0:T(8,128)(2,1)} %shard_map.127), calls=%async_computation.5 | async-start | bytes 7340032 | tf_op jit(solution)/shard_map/all_to_all | solution.py:394
  202.7 15.6 %collective-permute-start.18 = (bf16[384,256]{1,0:T(8,128)(2,1)}, bf16[384,256]{1,0:T(8,128)(2,1)S(1)}, u32[]{:S(2)}, u32[]{:S(2)}) collective-permute-start(bf16[384,256]{1,0:T(8,128)(2,1)} %get-tuple-element.52), channel_id=1, source_target_pairs={{0,1},{1,0},{2,3},{3,2},{4,5},{5,4},{6,7},{7,6},{8,9},{9,8},{10,11... | collective-permute-start | bytes 589832 | tf_op jit(solution)/shard_map/ppermute | solution.py:432
  210.1 14.8 %collective-permute-start.20 = (bf16[384,256]{1,0:T(8,128)(2,1)}, bf16[384,256]{1,0:T(8,128)(2,1)S(1)}, u32[]{:S(2)}, u32[]{:S(2)}) collective-permute-start(bf16[384,256]{1,0:T(8,128)(2,1)} %get-tuple-element.54), channel_id=1, source_target_pairs={{0,3},{1,2},{2,5},{3,4},{4,7},{5,6},{6,1},{7,0},{8,11},{9,10},{10,... | collective-permute-start | bytes 589832 | tf_op jit(solution)/shard_map/ppermute | solution.py:432
  215.0 14.0 %collective-permute-start.21 = (bf16[384,256]{1,0:T(8,128)(2,1)}, bf16[384,256]{1,0:T(8,128)(2,1)S(1)}, u32[]{:S(2)}, u32[]{:S(2)}) collective-permute-start(bf16[384,256]{1,0:T(8,128)(2,1)} %get-tuple-element.55), channel_id=1, source_target_pairs={{0,4},{1,5},{2,6},{3,7},{4,0},{5,1},{6,2},{7,3},{8,12},{9,13},{10,... | collective-permute-start | bytes 589832 | tf_op jit(solution)/shard_map/ppermute | solution.py:432
  215.1 18.4 %collective-permute-start.22 = (bf16[384,256]{1,0:T(8,128)(2,1)}, bf16[384,256]{1,0:T(8,128)(2,1)S(1)}, u32[]{:S(2)}, u32[]{:S(2)}) collective-permute-start(bf16[384,256]{1,0:T(8,128)(2,1)} %get-tuple-element.56), channel_id=1, source_target_pairs={{0,5},{1,4},{2,7},{3,6},{4,1},{5,0},{6,3},{7,2},{8,13},{9,12},{10,... | collective-permute-start | bytes 589832 | tf_op jit(solution)/shard_map/ppermute | solution.py:432
  218.3 15.9 %collective-permute-start.23 = (bf16[384,256]{1,0:T(8,128)(2,1)}, bf16[384,256]{1,0:T(8,128)(2,1)S(1)}, u32[]{:S(2)}, u32[]{:S(2)}) collective-permute-start(bf16[384,256]{1,0:T(8,128)(2,1)} %get-tuple-element.57), channel_id=1, source_target_pairs={{0,6},{1,7},{2,0},{3,1},{4,2},{5,3},{6,4},{7,5},{8,14},{9,15},{10,... | collective-permute-start | bytes 589832 | tf_op jit(solution)/shard_map/ppermute | solution.py:432
  218.4 16.5 %collective-permute-start.24 = (bf16[384,256]{1,0:T(8,128)(2,1)}, bf16[384,256]{1,0:T(8,128)(2,1)S(1)}, u32[]{:S(2)}, u32[]{:S(2)}) collective-permute-start(bf16[384,256]{1,0:T(8,128)(2,1)} %get-tuple-element.58), channel_id=1, source_target_pairs={{0,7},{1,6},{2,1},{3,0},{4,3},{5,2},{6,5},{7,4},{8,15},{9,14},{10,... | collective-permute-start | bytes 589832 | tf_op jit(solution)/shard_map/ppermute | solution.py:432
  252.1 26.7 %all-to-all-start.6 = ((bf16[16,64,384]{2,1,0:T(8,128)(2,1)}), bf16[16,64,384]{2,1,0:T(8,128)(2,1)S(1)}, u32[]{:S(2)}, u32[]{:S(2)}) async-start(bf16[16,64,384]{2,1,0:T(8,128)(2,1)} %pad_maximum_fusion), calls=%async_computation.6 | async-start | bytes 1572864 | tf_op jit(solution)/shard_map/all_to_all | solution.py:394
  (61 other events, 730.4 us)

commit v3 on v2

--- a/solution.py
+++ b/solution.py
@@ -13,16 +13,20 @@
 BF16 = jnp.bfloat16
 F32 = jnp.float32
 SCALE = HDIM ** (-0.5)
-GROUP = 6
-VMEM_LIMIT = 56 * 1024 * 1024
+GROUP = 8
+MIB = 1024 * 1024
+PACK_LIMIT = 8 * MIB
+ROWS_LIMIT = 24 * MIB
+ATTEND_LIMIT = 28 * MIB
+TAIL_LIMIT = 24 * MIB
 VMEM = pl.BlockSpec(memory_space=pltpu.VMEM)
 SMEM = pl.BlockSpec(memory_space=pltpu.SMEM)
 NT = (((1,), (1,)), ((), ()))
 TN = (((0,), (0,)), ((), ()))
 
 
-def params():
-    return pltpu.CompilerParams(vmem_limit_bytes=VMEM_LIMIT)
+def params(limit):
+    return pltpu.CompilerParams(vmem_limit_bytes=limit)
 
 
 def cost(flops, moved):
@@ -66,6 +70,10 @@
 
 def group_of(blocks):
     return GROUP if blocks % GROUP == 0 else 1
+
+
+def tile_rows(ref, block, part, width):
+    return ref[pl.ds(pl.multiple_of(block * BLOCK, BLOCK), BLOCK), part * width : (part + 1) * width]
 
 
 def slot_rows(ref, slot, per):
@@ -79,13 +87,13 @@
     meta_ref,
     query_ref,
     grad_ref,
-    key_ref,
-    value_ref,
+    kv_ref,
     key_mask_ref,
     mask_ref,
     out_ref,
 ):
     heads = mask_ref.shape[0] // BLOCK
+    width = mask_ref.shape[1]
     out_ref[...] = jnp.zeros_like(out_ref)
     n = count_ref[0]
 
@@ -93,8 +101,8 @@
         picked = [order_ref[jnp.minimum(g * GROUP + u, n - 1)] for u in range(GROUP)]
         pairs = [
             products(
-                by_head(key_ref[meta_ref[slot]], key_mask_ref),
-                by_head(value_ref[meta_ref[slot]], mask_ref),
+                by_head(tile_rows(kv_ref, meta_ref[slot], 0, width), key_mask_ref),
+                by_head(tile_rows(kv_ref, meta_ref[slot], 1, width), mask_ref),
                 slot_rows(query_ref, slot, per),
                 slot_rows(grad_ref, slot, per),
             )
@@ -109,8 +117,9 @@
     lax.fori_loop(0, pl.cdiv(n, GROUP), step, 0)
 
 
-def own_stats_kernel(query_ref, grad_ref, key_ref, value_ref, key_mask_ref, mask_ref, out_ref):
+def own_stats_kernel(query_ref, grad_ref, kv_ref, key_mask_ref, mask_ref, out_ref):
     heads = mask_ref.shape[0] // BLOCK
+    width = mask_ref.shape[1]
     blocks = query_ref.shape[0]
     group = group_of(blocks)
 
@@ -118,8 +127,8 @@
         picked = [g * group + u for u in range(group)]
         pairs = [
             products(
-                by_head(key_ref[b], key_mask_ref),
-                by_head(value_ref[b], mask_ref),
+                by_head(tile_rows(kv_ref, b, 0, width), key_mask_ref),
+                by_head(tile_rows(kv_ref, b, 1, width), mask_ref),
                 query_ref[b],
                 grad_ref[b],
             )
@@ -167,11 +176,6 @@
     return picked
 
 
-def across_heads(tile, mask_ref):
-    heads = mask_ref.shape[1] // BLOCK
-    return jnp.concatenate([tile] * heads, axis=1) * mask_ref[...]
-
-
 def far_query_kernel(
     per,
     count_ref,
@@ -180,22 +184,20 @@
     query_ref,
     grad_ref,
     stats_ref,
-    key_ref,
-    value_ref,
-    key_across_ref,
+    kv_ref,
     key_mask_ref,
     mask_ref,
-    across_mask_ref,
     out_ref,
 ):
     n = count_ref[0]
+    width = mask_ref.shape[1]
 
     def step(g, carry):
         picked = [order_ref[jnp.minimum(g * GROUP + u, n - 1)] for u in range(GROUP)]
         pairs = [
             products(
-                by_head(key_ref[meta_ref[slot]], key_mask_ref),
-                by_head(value_ref[meta_ref[slot]], mask_ref),
+                by_head(tile_rows(kv_ref, meta_ref[slot], 0, width), key_mask_ref),
+                by_head(tile_rows(kv_ref, meta_ref[slot], 1, width), mask_ref),
                 slot_rows(query_ref, slot, per),
                 slot_rows(grad_ref, slot, per),
             )
@@ -203,8 +205,8 @@
         ]
         grads = [entry_grads(*pair, stats_ref[slot])[1] for slot, pair in zip(picked, pairs)]
         for slot, grad_scores in zip(picked, grads):
-            key_across = across_heads(key_across_ref[meta_ref[slot]], across_mask_ref)
-            term = jnp.dot(key_across, grad_scores, preferred_element_type=F32)
+            key_heads = by_head(tile_rows(kv_ref, meta_ref[slot], 0, width), key_mask_ref)
+            term = lax.dot_general(grad_scores, key_heads, TN, preferred_element_type=F32)
             out_ref[slot] = term.astype(BF16)
         return carry
 
@@ -223,12 +225,9 @@
     query_ref,
     grad_ref,
     stats_ref,
-    key_ref,
-    value_ref,
-    key_across_ref,
+    kv_ref,
     key_mask_ref,
     mask_ref,
-    across_mask_ref,
     own_term_ref,
     out_ref,
     *rest,
@@ -242,8 +241,8 @@
         picked = [g * group + u for u in range(group)]
         pairs = [
             products(
-                by_head(key_ref[b], key_mask_ref),
-                by_head(value_ref[b], mask_ref),
+                by_head(tile_rows(kv_ref, b, 0, width), key_mask_ref),
+                by_head(tile_rows(kv_ref, b, 1, width), mask_ref),
                 query_ref[b],
                 grad_ref[b],
             )
@@ -251,8 +250,8 @@
         ]
         grads = [entry_grads(*pair, stats_ref[b]) for b, pair in zip(picked, pairs)]
         for b, (probs, grad_scores) in zip(picked, grads):
-            key_across = across_heads(key_across_ref[b], across_mask_ref)
-            own_term_ref[b] = jnp.dot(key_across, grad_scores, preferred_element_type=F32)
+            key_heads = by_head(tile_rows(kv_ref, b, 0, width), key_mask_ref)
+            own_term_ref[b] = lax.dot_general(grad_scores, key_heads, TN, preferred_element_type=F32)
             key_sum[b] = pick_heads(jnp.dot(grad_scores, query_ref[b], preferred_element_type=F32))
             value_sum[b] = pick_heads(jnp.dot(probs, grad_ref[b], preferred_element_type=F32))
         return carry
@@ -268,8 +267,8 @@
         ]
         pairs = [
             products(
-                by_head(key_ref[meta_ref[slot]], key_mask_ref),
-                by_head(value_ref[meta_ref[slot]], mask_ref),
+                by_head(tile_rows(kv_ref, meta_ref[slot], 0, width), key_mask_ref),
+                by_head(tile_rows(kv_ref, meta_ref[slot], 1, width), mask_ref),
                 *tile,
             )
             for slot, tile in zip(picked, tiles)
@@ -310,84 +309,87 @@
         for j in range(KB - 1):
             term = far_ref[slot_ref[b * (KB - 1) + j]].astype(F32)
             total = total + jnp.where(count_ref[b] > j + 1, term, 0.0)
-        out_ref[b * BLOCK : (b + 1) * BLOCK, :] = total.T.astype(BF16)
+        out_ref[b * BLOCK : (b + 1) * BLOCK, :] = total.astype(BF16)
     copy_chunks(target_ref, out_ref, chunk_refs)
 
 
-def rows_kernel(halves, first, width, *refs):
-    n = len(halves)
+def rows_kernel(n, *refs):
     chunks = jnp.concatenate([ref[...] for ref in refs[:n]], axis=1)
-    weight_refs = list(refs[n : n + sum(halves)])
-    start_ref, out_ref = refs[-2:]
-    depth = out_ref.shape[1] // 2
-    sides = ([], [])
-    for count in halves:
-        pieces = [weight_refs.pop(0) for _ in range(count)]
-        for half in range(2):
-            if count == 2:
-                sides[half].append(pieces[half][:, first : first + width])
-            else:
-                sides[half].append(pieces[0][half * depth : (half + 1) * depth, first : first + width])
-    for half in range(2):
-        columns = slice(half * depth, (half + 1) * depth)
-        total = lax.dot_general(
-            chunks, jnp.concatenate(sides[half], axis=1), NT, preferred_element_type=F32
-        )
-        if start_ref is not None:
-            total = total + start_ref[:, columns]
-        out_ref[:, columns] = total.astype(out_ref.dtype)
-
-
-def first_rows_kernel(halves, first, width, *refs):
-    rows_kernel(halves, first, width, *refs[:-1], None, refs[-1])
-
-
-def project_kernel(places, source_ref, *refs):
-    n = len(places)
-    weight_ref, query_ref, key_ref, value_ref, out_ref = refs[n:]
-    cols = query_ref.shape[1]
+    weight_ref, out_ref = refs[n], refs[-1]
+    total = lax.dot_general(chunks, weight_ref[...], NT, preferred_element_type=F32)
+    if len(refs) == n + 3:
+        total = total + refs[n + 1][...]
+    out_ref[...] = total.astype(out_ref.dtype)
+
+
+def weights_kernel(halves, *refs):
+    query_ref, kv_ref = refs[-2:]
+    piece_refs = list(refs[:-2])
+    width = query_ref.shape[1] // len(halves)
+    for i, count in enumerate(halves):
+        start = 0
+        for _ in range(count):
+            piece = piece_refs.pop(0)
+            rows = slice(start, start + piece.shape[0])
+            start += piece.shape[0]
+            query_ref[rows, i * width : (i + 1) * width] = piece[:, :width]
+            kv_ref[rows, 2 * i * width : 2 * (i + 1) * width] = piece[:, width:]
+
+
+def spans(places, source_ref, refs):
     for i, (index, half) in enumerate(places):
         rows = refs[i].shape[0]
         start = source_ref[index] * (rows if half is None else 2 * rows) + (half or 0) * rows
-        span = pl.ds(pl.multiple_of(start, 64), rows)
-        out_ref[span, :] = refs[i][...]
-        result = jnp.dot(refs[i][...], weight_ref[...], preferred_element_type=F32)
-        for j, ref in enumerate((query_ref, key_ref, value_ref)):
-            ref[span, :] = result[:, j * cols : (j + 1) * cols].astype(BF16)
-
-
-def pack_kernel(per, peers_step, source_ref, tile_ref, *rest):
-    out_ref = rest[-1]
+        yield refs[i], pl.ds(pl.multiple_of(start, 64), rows)
+
+
+def query_kernel(places, source_ref, *refs):
+    weight_ref, out_ref = refs[len(places) :]
+    for ref, span in spans(places, source_ref, refs):
+        out_ref[span, :] = jnp.dot(
+            ref[...], weight_ref[...], preferred_element_type=F32
+        ).astype(BF16)
+
+
+def project_kernel(places, source_ref, *refs):
+    weight_ref, kv_ref, out_ref = refs[len(places) :]
+    for ref, span in spans(places, source_ref, refs):
+        out_ref[span, :] = ref[...]
+        kv_ref[span, :] = jnp.dot(
+            ref[...], weight_ref[...], preferred_element_type=F32
+        ).astype(BF16)
+
+
+def pack_kernel(per, peers_step, extra, source_ref, asked_ref, tile_ref, out_ref):
     first = pl.program_id(0) * peers_step
     for p in range(peers_step):
+        at = (first + p) * per
         for r in range(per):
-            out_ref[p, r * BLOCK : (r + 1) * BLOCK, :] = tile_ref[source_ref[(first + p) * per + r]]
-    if len(rest) == 2:
-        out_ref[:, per * BLOCK :, :] = rest[0][...]
-
-
-def pack(tiles, source, meta, n_seq, per):
+            out_ref[p, r * BLOCK : (r + 1) * BLOCK, :] = tile_ref[source_ref[at + r]]
+        if extra:
+            row = lax.broadcasted_iota(jnp.int32, (extra, out_ref.shape[2]), 0)
+            meta = jnp.zeros(row.shape, F32)
+            for r in range(per):
+                meta = jnp.where(row == r, asked_ref[at + r].astype(F32), meta)
+            out_ref[p, per * BLOCK :, :] = meta.astype(BF16)
+
+
+def pack(tiles, source, asked, n_seq, per, extra):
     blocks, _, cols = tiles.shape
     peers_step = 4 if n_seq % 4 == 0 else 1
-    extra = 0 if meta is None else meta.shape[1]
     rows = per * BLOCK + extra
-    in_specs = [pl.BlockSpec((blocks, BLOCK, cols), lambda i, s: (0, 0, 0))]
-    operands = [tiles]
-    if meta is not None:
-        in_specs.append(pl.BlockSpec((peers_step, extra, cols), lambda i, s: (i, 0, 0)))
-        operands.append(meta)
     return pl.pallas_call(
-        functools.partial(pack_kernel, per, peers_step),
+        functools.partial(pack_kernel, per, peers_step, extra),
         grid_spec=pltpu.PrefetchScalarGridSpec(
-            num_scalar_prefetch=1,
+            num_scalar_prefetch=2,
             grid=(n_seq // peers_step,),
-            in_specs=in_specs,
-            out_specs=pl.BlockSpec((peers_step, rows, cols), lambda i, s: (i, 0, 0)),
+            in_specs=[pl.BlockSpec((blocks, BLOCK, cols), lambda i, s, a: (0, 0, 0))],
+            out_specs=pl.BlockSpec((peers_step, rows, cols), lambda i, s, a: (i, 0, 0)),
         ),
         out_shape=jax.ShapeDtypeStruct((n_seq, rows, cols), BF16),
-        compiler_params=params(),
+        compiler_params=params(PACK_LIMIT),
         cost_estimate=cost(0, 2 * 2 * n_seq * rows * cols),
-    )(source, *operands)
+    )(source, asked, tiles)
 
 
 def seq_exchange(x):
@@ -463,13 +465,9 @@
     taken = slot_of[None, :] == jnp.arange(slots, dtype=jnp.int32)[:, None]
     source = jnp.sum(jnp.where(taken, numbers[None, :] // (KB - 1), 0), axis=1)
     asked = jnp.sum(jnp.where(taken & live[None, :], inner[None, :] + 1, 0), axis=1) - 1
-    meta = jnp.broadcast_to(
-        jnp.pad(asked.reshape(n_seq, per), ((0, 0), (0, 16 - per)))[:, :, None], (n_seq, 16, cols)
-    ).astype(BF16)
-
     upstream = lax.all_to_all(grad_context, "head", split_axis=1, concat_axis=0, tiled=True)
     grad_tiles = upstream.reshape(blocks, BLOCK, cols)
-    far_grads = seq_exchange(pack(grad_tiles, source, meta, n_seq, per))
+    far_grads = seq_exchange(pack(grad_tiles, source, asked, n_seq, per, 16))
     far_meta = far_grads[:, per * BLOCK : per * BLOCK + per, 0].astype(jnp.int32).reshape(-1)
     slot_numbers = jnp.arange(slots, dtype=jnp.int32)
     wanted = far_meta >= 0
@@ -481,34 +479,55 @@
     far_count = jnp.sum(wanted.astype(jnp.int32)).reshape(1)
     far_list = (far_count, far_order, far_meta)
 
+    width = node_input.shape[1]
     found = head_gather(node_input)
     places, pieces = [], []
     for i, place in enumerate(order):
         for half, piece in enumerate(found[place]):
             places.append((i, None if len(found[place]) == 1 else half))
             pieces.append(piece)
+    queries = pl.pallas_call(
+        functools.partial(query_kernel, places),
+        out_shape=jax.ShapeDtypeStruct((nodes, cols), BF16),
+        in_specs=[SMEM] + [VMEM] * (len(pieces) + 1),
+        out_specs=VMEM,
+        compiler_params=params(ROWS_LIMIT),
+        cost_estimate=cost(2 * nodes * width * cols, 2 * nodes * width),
+    )(sources, *pieces, w_query)
+    query_tiles = queries.reshape(blocks, BLOCK, cols)
+    packed = pack(query_tiles, source, asked, n_seq, per, 0)
+    far_queries = seq_exchange(packed)
+    w_kv = jnp.concatenate([w_key, w_value], axis=1)
+    packed, *pieces = lax.optimization_barrier((packed, *pieces))
+    kv, gathered = pl.pallas_call(
+        functools.partial(project_kernel, places),
+        out_shape=(
+            jax.ShapeDtypeStruct((nodes, 2 * cols), BF16),
+            jax.ShapeDtypeStruct((nodes, width), BF16),
+        ),
+        in_specs=[SMEM] + [VMEM] * (len(pieces) + 1),
+        out_specs=(VMEM,) * 2,
+        compiler_params=params(ROWS_LIMIT),
+        cost_estimate=cost(4 * nodes * width * cols, 4 * nodes * width),
+    )(sources, *pieces, w_kv)
+
     w_all = jnp.concatenate([w_query, w_key, w_value], axis=1)
-    queries, keys, values, gathered = pl.pallas_call(
-        functools.partial(project_kernel, places),
-        out_shape=(jax.ShapeDtypeStruct((nodes, cols), BF16),) * 3
-        + (jax.ShapeDtypeStruct((nodes, node_input.shape[1]), BF16),),
-        in_specs=[SMEM] + [VMEM] * (len(pieces) + 1),
-        out_specs=(VMEM,) * 4,
-        compiler_params=params(),
-        cost_estimate=cost(6 * nodes * node_input.shape[1] * cols, 4 * nodes * node_input.shape[1]),
-    )(sources, *pieces, w_all)
-    query_tiles = queries.reshape(blocks, BLOCK, cols)
-    far_queries = seq_exchange(pack(query_tiles, source, None, n_seq, per))
-    key_tiles = keys.reshape(blocks, BLOCK, cols)
-    value_tiles = values.reshape(blocks, BLOCK, cols)
-
-    w_all, _ = lax.optimization_barrier((w_all, queries))
+    w_all, _ = lax.optimization_barrier((w_all, packed))
     found = head_gather(w_all)
     halves = [len(found[place]) for place in order]
     w_pieces = [piece for place in order for piece in found[place]]
-    far_queries, *w_pieces = lax.optimization_barrier((far_queries, *w_pieces))
-    key_across = keys.reshape(blocks, BLOCK, cols).transpose(0, 2, 1)
-    across_mask = key_mask.T
+    w_rows, w_kv_rows = pl.pallas_call(
+        functools.partial(weights_kernel, halves),
+        out_shape=(
+            jax.ShapeDtypeStruct((width, n_head * cols), BF16),
+            jax.ShapeDtypeStruct((width, n_head * 2 * cols), BF16),
+        ),
+        in_specs=[VMEM] * len(w_pieces),
+        out_specs=(VMEM,) * 2,
+        compiler_params=params(ROWS_LIMIT),
+        cost_estimate=cost(0, 12 * width * n_head * cols),
+    )(*w_pieces)
+    far_queries, w_rows, w_kv_rows = lax.optimization_barrier((far_queries, w_rows, w_kv_rows))
 
     unit_flops = 2 * heads * BLOCK * BLOCK * cols
     tile_bytes = 2 * BLOCK * cols
@@ -516,48 +535,45 @@
     own_stats = pl.pallas_call(
         own_stats_kernel,
         out_shape=jax.ShapeDtypeStruct((blocks, 2 * heads, BLOCK), F32),
-        in_specs=[VMEM] * 6,
+        in_specs=[VMEM] * 5,
         out_specs=VMEM,
-        compiler_params=params(),
+        compiler_params=params(ATTEND_LIMIT),
         cost_estimate=cost(2 * blocks * unit_flops, 4 * blocks * tile_bytes),
-    )(query_tiles, grad_tiles, key_tiles, value_tiles, key_mask, mask)
+    )(query_tiles, grad_tiles, kv, key_mask, mask)
     far_stats = pl.pallas_call(
         functools.partial(remote_stats_kernel, per),
         out_shape=stats_shape,
-        in_specs=[SMEM] * 3 + [VMEM] * 6,
+        in_specs=[SMEM] * 3 + [VMEM] * 5,
         out_specs=VMEM,
-        compiler_params=params(),
+        compiler_params=params(ATTEND_LIMIT),
         cost_estimate=cost(2 * slots * unit_flops, 2 * slots * tile_bytes),
-    )(*far_list, far_queries, far_grads, key_tiles, value_tiles, key_mask, mask)
+    )(*far_list, far_queries, far_grads, kv, key_mask, mask)
     row_stats_all, back = pl.pallas_call(
         merge_kernel,
         out_shape=(jax.ShapeDtypeStruct((blocks, 2 * heads, BLOCK), F32), stats_shape),
         in_specs=[SMEM, SMEM, VMEM, VMEM],
         out_specs=(VMEM, VMEM),
         scratch_shapes=[pltpu.VMEM((KB - 1, blocks, heads, BLOCK), F32)] * 2,
-        compiler_params=params(),
+        compiler_params=params(ATTEND_LIMIT),
         cost_estimate=cost(0, 2 * 2 * slots * 4 * heads * BLOCK),
     )(slot_of, counts, own_stats, seq_exchange(far_stats))
     back = seq_exchange(back)
 
     far_terms = pl.pallas_call(
         functools.partial(far_query_kernel, per),
-        out_shape=jax.ShapeDtypeStruct((slots, cols, BLOCK), BF16),
-        in_specs=[SMEM] * 3 + [VMEM] * 9,
+        out_shape=jax.ShapeDtypeStruct((slots, BLOCK, cols), BF16),
+        in_specs=[SMEM] * 3 + [VMEM] * 6,
         out_specs=VMEM,
-        compiler_params=params(),
+        compiler_params=params(ATTEND_LIMIT),
         cost_estimate=cost(3 * slots * unit_flops, 3 * slots * tile_bytes),
     )(
         *far_list,
         far_queries,
         far_grads,
         back,
-        key_tiles,
-        value_tiles,
-        key_across,
+        kv,
         key_mask,
         mask,
-        across_mask,
     )
     back_terms = seq_exchange(far_terms)
 
@@ -566,17 +582,17 @@
     own_terms, grad_key_value, *chunks = pl.pallas_call(
         functools.partial(key_value_kernel, per),
         out_shape=(
-            jax.ShapeDtypeStruct((blocks, cols, BLOCK), F32),
+            jax.ShapeDtypeStruct(tile_shape, F32),
             jax.ShapeDtypeStruct((nodes, 2 * cols), BF16),
         )
         + (jax.ShapeDtypeStruct((rows, 2 * cols), BF16),) * n_head,
-        in_specs=[SMEM] * 4 + [VMEM] * 12,
+        in_specs=[SMEM] * 4 + [VMEM] * 9,
         out_specs=(VMEM,) * (2 + n_head),
         scratch_shapes=[
             pltpu.VMEM(tile_shape, F32),
             pltpu.VMEM(tile_shape, F32),
         ],
-        compiler_params=params(),
+        compiler_params=params(ATTEND_LIMIT),
         cost_estimate=cost(5 * slots * unit_flops, 3 * slots * tile_bytes),
     )(
         targets,
@@ -587,53 +603,46 @@
         query_tiles,
         grad_tiles,
         row_stats_all,
-        key_tiles,
-        value_tiles,
-        key_across,
+        kv,
         key_mask,
         mask,
-        across_mask,
     )
 
     contract_rows = (((0,), (0,)), ((), ()))
     chunks = head_send(chunks)
     term_key_value = lax.dot_general(gathered, grad_key_value, contract_rows, preferred_element_type=F32)
-    width = w_query.shape[0]
+    back_terms, *chunks = lax.optimization_barrier((back_terms, *chunks))
     summed = pl.pallas_call(
-        functools.partial(first_rows_kernel, halves, cols, 2 * cols),
+        functools.partial(rows_kernel, n_head),
         out_shape=jax.ShapeDtypeStruct((rows, width), F32),
-        in_specs=[VMEM] * (len(chunks) + len(w_pieces)),
+        in_specs=[VMEM] * (n_head + 1),
         out_specs=VMEM,
-        compiler_params=params(),
-        cost_estimate=cost(2 * rows * width * 2 * cols * n_head, 2 * width * 3 * cols * n_head),
-    )(*chunks, *w_pieces)
-
-    back_terms, summed = lax.optimization_barrier((back_terms, summed))
+        compiler_params=params(TAIL_LIMIT),
+        cost_estimate=cost(2 * rows * width * 2 * cols * n_head, 2 * width * 2 * cols * n_head),
+    )(*chunks, w_kv_rows)
+
     grad_query, *chunks = pl.pallas_call(
         query_sum_kernel,
         out_shape=(jax.ShapeDtypeStruct((nodes, cols), BF16),)
         + (jax.ShapeDtypeStruct((rows, cols), BF16),) * n_head,
         in_specs=[SMEM] * 3 + [VMEM] * 2,
         out_specs=(VMEM,) * (1 + n_head),
-        compiler_params=params(),
+        compiler_params=params(TAIL_LIMIT),
         cost_estimate=cost(0, slots * tile_bytes),
     )(targets, slot_of, counts, own_terms, back_terms)
     term_query = lax.dot_general(gathered, grad_query, contract_rows, preferred_element_type=F32)
     weight_terms = jnp.concatenate([term_query, term_key_value], axis=1).astype(BF16)
-    weight_terms = seq_exchange(weight_terms.reshape(n_seq, -1, 3 * cols))
+    weight_terms = seq_exchange(weight_terms.reshape(n_seq, width // n_seq, 3 * cols))
     weight_grads = jnp.sum(weight_terms.astype(F32), axis=0)
     chunks = head_send(chunks)
     grad_input = pl.pallas_call(
-        functools.partial(rows_kernel, halves, 0, cols),
-        grid=(1,),
+        functools.partial(rows_kernel, n_head),
         out_shape=jax.ShapeDtypeStruct((rows, width), BF16),
-        in_specs=[VMEM] * n_head
-        + [pl.BlockSpec((p.shape[0], cols), lambda i: (0, 0)) for p in w_pieces]
-        + [VMEM],
+        in_specs=[VMEM] * (n_head + 2),
         out_specs=VMEM,
-        compiler_params=params(),
+        compiler_params=params(TAIL_LIMIT),
         cost_estimate=cost(2 * rows * width * cols * n_head, 2 * width * cols * n_head),
-    )(*chunks, *w_pieces, summed)
+    )(*chunks, w_rows, summed)
     return (
         grad_input,
         weight_grads[:, :cols],

time: 280 us -> 271 us (0.968)
  Pallas kernels: 72.7 us -> 46.9 us
  local copies, waits for them, and re-layouts: 14.1 us -> 26 us
  blocking collectives: 0 us -> 10.5 us
    ppermute x2, waiting for transfers between devices: 17.5 us -> 0.73 us  [head_gather(): up = lax.ppermute(up, 'head', head_pairs(1, 0))]
    unnamed x94 -> x74, local copies, waits for them, and re-layouts: 6.71 us -> 22.3 us
    ppermute x2, waiting for transfers between devices: 15.3 us -> 30.1 us  [head_gather(): down = lax.ppermute(down, 'head', head_pairs(-1, 0))]
    all_to_all x0 -> x1, blocking collectives: none -> 10.5 us  [seq_exchange(): return lax.all_to_all(x, 'seq', split_axis=0, concat_axis=0, tiled=True)]
    pallas_call x4 -> x6, Pallas kernels: 19.3 us -> 10.5 us  [the longest x1 3.88 us: shards(): pl.pallas_call(functools.partial(query_kernel, places), out_shape=jax.Sha...]
    pallas_call x1, Pallas kernels: 9.91 us -> 4.29 us  [shards(): pl.pallas_call(functools.partial(project_kernel, places), out_shape=(jax....]
    ppermute x2, waiting for transfers between devices: 1.93 us -> 6.75 us  [head_gather(): lax.ppermute(down[half:], 'head', head_pairs(-1, 0))]
    ppermute x10, starting transfers between devices: 16.3 us -> 20.2 us  [head_gather(): lax.ppermute(b, 'head', head_pairs(0, 1))]
  transfers between devices with their start and end apart: 39 -> 38, of which waited for: 17 -> 17; matrix products, arithmetic and copies ran while one was open for 6% -> 4% of each run, Pallas kernels for 16% -> 10%
where the time goes in v3:
time: 271 us
  starting transfers between devices  98 us (36%)
  waiting for transfers between devices  72.7 us (27%)
  Pallas kernels  46.9 us (17%)
  local copies, waits for them, and re-layouts  26 us (10%)
  blocking collectives  10.5 us (4%)
  matrix products  9.27 us (3%)
  other arithmetic  6.72 us (2%)
    all_to_all x5, starting transfers between devices, seq_exchange(): return lax.all_to_all(x, 'seq', split_axis=0, concat_axis=0, tiled=True)  37.2 us
    ppermute x2, waiting for transfers between devices, head_gather(): down = lax.ppermute(down, 'head', head_pairs(-1, 0))  30.1 us
    ppermute x14, starting transfers between devices, head_send(): lax.ppermute(c, 'head', head_pairs(*place))  25.2 us
    unnamed x74, local copies, waits for them, and re-layouts  22.3 us
    ppermute x10, starting transfers between devices, head_gather(): lax.ppermute(b, 'head', head_pairs(0, 1))  20.2 us
    all_to_all x5, waiting for transfers between devices, seq_exchange(): return lax.all_to_all(x, 'seq', split_axis=0, concat_axis=0, tiled=True)  12.7 us
    pallas_call x1, Pallas kernels, shards(): pl.pallas_call(functools.partial(key_value_kernel, per), out_shape=(jax.S...  11.3 us
    ppermute x14, waiting for transfers between devices, head_send(): lax.ppermute(c, 'head', head_pairs(*place))  11 us
  transfers between devices with their start and end apart: 38, of which 17 were waited for; matrix products, arithmetic and copies ran while one was open for 4% of the time, Pallas kernels for 10%

profile of v3, /device:TPU:1, one launch (start us, length us, event | category | flops | bytes accessed | tf_op | source)
XLA Modules:
  0.0 271.4 jit_solution(3633700977965250038)
XLA Ops:
  2.8 6.8 %all-to-all-start = ((bf16[384,8,128]{2,0,1:T(8,128)(2,1)}), bf16[384,8,128]{2,0,1:T(8,128)(2,1)S(1)}, u32[]{:S(2)}, u32[]{:S(2)}) async-start(bf16[384,8,128]{2,0,1:T(8,128)(2,1)} %copy_bitcast_fusion), calls=%async_computation | async-start | bytes 1572864 | tf_op jit(solution)/shard_map/all_to_all | solution.py:468
  11.9 10.0 %all-to-all-done = bf16[384,8,128]{2,0,1:T(8,128)(2,1)S(1)} async-done(((bf16[384,8,128]{2,0,1:T(8,128)(2,1)}), bf16[384,8,128]{2,0,1:T(8,128)(2,1)S(1)}, u32[]{:S(2)}, u32[]{:S(2)}) %all-to-all-start) | async-done | bytes 786464 | tf_op jit(solution)/shard_map/all_to_all | solution.py:468
  24.6 6.9 %all-to-all-start.1 = ((bf16[16,912,128]{2,1,0:T(8,128)(2,1)}), bf16[16,912,128]{2,1,0:T(8,128)(2,1)}, u32[]{:S(2)}, u32[]{:S(2)}) async-start(bf16[16,912,128]{2,1,0:T(8,128)(2,1)} %copy-done.3), calls=%async_computation.1 | async-start | bytes 7471104 | tf_op jit(solution)/shard_map/all_to_all | solution.py:396
  34.8 14.8 %collective-permute-done.4.refs_8_ = bf16[384,1024]{1,0:T(8,128)(2,1)S(1)} collective-permute-done((bf16[384,1024]{1,0:T(8,128)(2,1)S(1)}, bf16[384,1024]{1,0:T(8,128)(2,1)S(1)}, u32[]{:S(2)}, u32[]{:S(2)}) %collective-permute-start.4) | collective-permute-done | bytes 786464 | tf_op jit(solution)/shard_map/ppermute | solution.py:417
  54.4 4.1 %collective-permute-done.5.refs_5_ = bf16[192,1024]{1,0:T(8,128)(2,1)S(1)} collective-permute-done((bf16[192,1024]{1,0:T(8,128)(2,1)S(1)}, bf16[192,1024]{1,0:T(8,128)(2,1)S(1)}, u32[]{:S(2)}, u32[]{:S(2)}) %collective-permute-start.5) | collective-permute-done | bytes 393248 | tf_op jit(solution)/shard_map/ppermute | solution.py:422
  67.4 3.9 %shard_map.121 = bf16[3072,128]{1,0:T(8,128)(2,1)S(1)} custom-call(s32[8]{0:T(128)S(1)} %get-tuple-element.102.source_ref, bf16[384,1024]{1,0:T(8,128)(2,1)S(1)} %copy-done.14, bf16[384,1024]{1,0:T(8,128)(2,1)} %collective-permute-done.refs_1_, bf16[384,1024]{1,0:T(8,128)(2,1)S(1)} %collective-permute-done.1.refs_2_, ...), custom_call_target="tpu_custom_call" | custom-call | flops 805306368 | bytes 6291456 | tf_op jit(solution)/shard_map/pallas_call | solution.py:489
  74.9 3.5 %all-to-all-done.1.grad_ref.far_grad_ref = bf16[16,912,128]{2,1,0:T(8,128)(2,1)} async-done(((bf16[16,912,128]{2,1,0:T(8,128)(2,1)}), bf16[16,912,128]{2,1,0:T(8,128)(2,1)}, u32[]{:S(2)}, u32[]{:S(2)}) %all-to-all-start.1) | async-done | bytes 3735584 | tf_op jit(solution)/shard_map/all_to_all | solution.py:396
  78.5 11.8 %all-to-all-start.2 = ((bf16[16,896,128]{2,1,0:T(8,128)(2,1)}), bf16[16,896,128]{2,1,0:T(8,128)(2,1)}, u32[]{:S(2)}, u32[]{:S(2)}) async-start(bf16[16,896,128]{2,1,0:T(8,128)(2,1)} %copy-done.4), calls=%async_computation.2 | async-start | bytes 7340032 | tf_op jit(solution)/shard_map/all_to_all | solution.py:396
  92.0 15.3 %collective-permute-done.13.refs_8_ = bf16[1024,384]{1,0:T(8,128)(2,1)S(1)} collective-permute-done((bf16[1024,384]{1,0:T(8,128)(2,1)S(1)}, bf16[1024,384]{1,0:T(8,128)(2,1)S(1)}, u32[]{:S(2)}, u32[]{:S(2)}) %collective-permute-start.13) | collective-permute-done | bytes 786464 | tf_op jit(solution)/shard_map/ppermute | solution.py:417
  130.1 4.3 %shard_map.124 = (bf16[3072,256]{1,0:T(8,128)(2,1)S(1)}, bf16[3072,1024]{1,0:T(8,128)(2,1)S(1)}) custom-call(s32[8]{0:T(128)S(1)} %get-tuple-element.102.source_ref, bf16[384,1024]{1,0:T(8,128)(2,1)S(1)} %copy-done.15, bf16[384,1024]{1,0:T(8,128)(2,1)} %collective-permute-done.refs_1_, bf16[384,1024]{1,0:T(8,128)(2,1)S(1)} %copy-done.11, ...), custom_call_target="tpu_custom_call" | custom-call | flops 1610612736 | bytes 12582912 | tf_op jit(solution)/shard_map/pallas_call | solution.py:502
  140.8 7.9 %shard_map.126 = f32[112,4,128]{2,1,0:T(4,128)} custom-call(s32[1]{0:T(128)} %bitcast.3.count_ref, s32[112]{0:T(128)S(1)} %select_reduce_fusion.order_ref, s32[112]{0:T(128)S(1)} %reshape.259.meta_ref, bf16[16,896,128]{2,1,0:T(8,128)(2,1)} %all-to-all-done.2.query_ref.far_query_ref, bf16[16,912,128]{2,1,0:T(8,128)(2,1)} %all-to-all-done.1.grad_ref.far_grad_ref, ...), custom_call_target="tpu_custom_call" | custom-call | flops 1879048192 | bytes 7340032 | tf_op jit(solution)/shard_map/pallas_call | solution.py:543
  148.7 5.8 %all-to-all-start.3 = ((f32[112,4,128]{2,1,0:T(4,128)}), f32[112,4,128]{2,1,0:T(4,128)S(1)}, u32[]{:S(2)}, u32[]{:S(2)}) async-start(f32[112,4,128]{2,1,0:T(4,128)} %shard_map.126), calls=%async_computation.3 | async-start | bytes 458752 | tf_op jit(solution)/shard_map/all_to_all | solution.py:396
  157.4 4.5 %all-to-all-done.3.far_ref = f32[112,4,128]{2,1,0:T(4,128)S(1)} async-done(((f32[112,4,128]{2,1,0:T(4,128)}), f32[112,4,128]{2,1,0:T(4,128)S(1)}, u32[]{:S(2)}, u32[]{:S(2)}) %all-to-all-start.3) | async-done | bytes 229408 | tf_op jit(solution)/shard_map/all_to_all | solution.py:396
  163.4 10.5 %all_to_all.46.far_stats_ref.stats_ref = f32[112,4,128]{2,1,0:T(4,128)S(1)} all-to-all(f32[112,4,128]{2,1,0:T(4,128)S(1)} %get-tuple-element.65), channel_id=1, replica_groups=mesh['seq'=16,'head'=8] {'seq'}, dimensions={0} | all-to-all | bytes 458752 | tf_op jit(solution)/shard_map/all_to_all | solution.py:396
  173.9 7.8 %shard_map.129 = bf16[112,128,128]{2,1,0:T(8,128)(2,1)S(1)} custom-call(s32[1]{0:T(128)} %bitcast.3.count_ref, s32[112]{0:T(128)S(1)} %select_reduce_fusion.order_ref, s32[112]{0:T(128)S(1)} %reshape.259.meta_ref, bf16[16,896,128]{2,1,0:T(8,128)(2,1)} %all-to-all-done.2.query_ref.far_query_ref, bf16[16,912,128]{2,1,0:T(8,128)(2,1)} %all-to-all-done.1.grad_ref.far_grad_ref, ...), custom_call_target="tpu_custom_call" | custom-call | flops 2818572288 | bytes 11010048 | tf_op jit(solution)/shard_map/pallas_call | solution.py:562
  183.5 4.6 %all-to-all-start.5 = ((bf16[112,128,128]{2,1,0:T(8,128)(2,1)}), bf16[112,128,128]{2,1,0:T(8,128)(2,1)}, u32[]{:S(2)}, u32[]{:S(2)}) async-start(bf16[112,128,128]{2,1,0:T(8,128)(2,1)} %copy-done.5), calls=%async_computation.5 | async-start | bytes 7340032 | tf_op jit(solution)/shard_map/all_to_all | solution.py:396
  189.0 11.3 %shard_map.128 = (f32[24,128,128]{2,1,0:T(8,128)S(1)}, bf16[3072,256]{1,0:T(8,128)(2,1)S(1)}, bf16[384,256]{1,0:T(8,128)(2,1)S(1)}, bf16[384,256]{1,0:T(8,128)(2...) custom-call(s32[8]{0:T(128)S(1)} %fusion.9.target_ref, ...), custom_call_target="tpu_custom_call" | custom-call | flops 4697620480 | bytes 11010048 | tf_op jit(solution)/shard_map/pallas_call | solution.py:582
  213.0 4.7 %convolution_convert_fusion = bf16[1024,256]{1,0:T(8,128)(2,1)S(1)} fusion(bf16[3072,1024]{1,0:T(8,128)(2,1)} %copy-done.9, bf16[3072,256]{1,0:T(8,128)(2,1)S(1)} %get-tuple-element.97), kind=kOutput, calls=%fused_computation.2 | convolution fusion | flops 1610874880 | bytes 8388608 | tf_op jit(solution)/shard_map/dot_general | solution.py:613
  220.5 4.5 %collective-permute-done.22.refs_5_ = bf16[384,256]{1,0:T(8,128)(2,1)S(1)} collective-permute-done((bf16[384,256]{1,0:T(8,128)(2,1)S(1)}, bf16[384,256]{1,0:T(8,128)(2,1)S(1)}, u32[]{:S(2)}, u32[]{:S(2)}) %collective-permute-start.22) | collective-permute-done | bytes 196640 | tf_op jit(solution)/shard_map/ppermute | solution.py:434
  225.0 4.6 %all-to-all-done.5.far_ref = bf16[112,128,128]{2,1,0:T(8,128)(2,1)} async-done(((bf16[112,128,128]{2,1,0:T(8,128)(2,1)}), bf16[112,128,128]{2,1,0:T(8,128)(2,1)}, u32[]{:S(2)}, u32[]{:S(2)}) %all-to-all-start.5) | async-done | bytes 3670048 | tf_op jit(solution)/shard_map/all_to_all | solution.py:396
  233.6 4.6 %convolution_convert_fusion.1 = bf16[1024,128]{1,0:T(8,128)(2,1)S(1)} fusion(bf16[3072,1024]{1,0:T(8,128)(2,1)} %copy-done.9, bf16[3072,128]{1,0:T(8,128)(2,1)S(1)} %get-tuple-element.96), kind=kOutput, calls=%fused_computation.3 | convolution fusion | flops 805437440 | bytes 7340032 | tf_op jit(solution)/shard_map/dot_general | solution.py:633
  239.3 8.0 %all-to-all-start.6 = ((bf16[16,64,384]{2,1,0:T(8,128)(2,1)}), bf16[16,64,384]{2,1,0:T(8,128)(2,1)}, u32[]{:S(2)}, u32[]{:S(2)}) async-start(bf16[16,64,384]{2,1,0:T(8,128)(2,1)} %pad_maximum_fusion.1), calls=%async_computation.6 | async-start | bytes 1572864 | tf_op jit(solution)/shard_map/all_to_all | solution.py:396
  247.3 4.9 %collective-permute-start.25 = (bf16[384,128]{1,0:T(8,128)(2,1)S(1)}, bf16[384,128]{1,0:T(8,128)(2,1)S(1)}, u32[]{:S(2)}, u32[]{:S(2)}) collective-permute-start(bf16[384,128]{1,0:T(8,128)(2,1)S(1)} %get-tuple-element.78), channel_id=1, source_target_pairs={{0,1},{1,0},{2,3},{3,2},{4,5},{5,4},{6,7},{7,6},{8,9},{9,8},{10,11... | collective-permute-start | bytes 294920 | tf_op jit(solution)/shard_map/ppermute | solution.py:434
  252.2 4.6 %collective-permute-start.27 = (bf16[384,128]{1,0:T(8,128)(2,1)S(1)}, bf16[384,128]{1,0:T(8,128)(2,1)S(1)}, u32[]{:S(2)}, u32[]{:S(2)}) collective-permute-start(bf16[384,128]{1,0:T(8,128)(2,1)S(1)} %get-tuple-element.80), channel_id=1, source_target_pairs={{0,3},{1,2},{2,5},{3,4},{4,7},{5,6},{6,1},{7,0},{8,11},{9,10},{10,... | collective-permute-start | bytes 294920 | tf_op jit(solution)/shard_map/ppermute | solution.py:434
  (180 shorter events, 100.3 us)
Async XLA Ops:
  2.8 19.1 %all-to-all-start = ((bf16[384,8,128]{2,0,1:T(8,128)(2,1)}), bf16[384,8,128]{2,0,1:T(8,128)(2,1)S(1)}, u32[]{:S(2)}, u32[]{:S(2)}) async-start(bf16[384,8,128]{2,0,1:T(8,128)(2,1)} %copy_bitcast_fusion), calls=%async_computation | async-start | bytes 1572864 | tf_op jit(solution)/shard_map/all_to_all | solution.py:468
  24.6 53.8 %all-to-all-start.1 = ((bf16[16,912,128]{2,1,0:T(8,128)(2,1)}), bf16[16,912,128]{2,1,0:T(8,128)(2,1)}, u32[]{:S(2)}, u32[]{:S(2)}) async-start(bf16[16,912,128]{2,1,0:T(8,128)(2,1)} %copy-done.3), calls=%async_computation.1 | async-start | bytes 7471104 | tf_op jit(solution)/shard_map/all_to_all | solution.py:396
  31.6 18.1 %collective-permute-start.4 = (bf16[384,1024]{1,0:T(8,128)(2,1)S(1)}, bf16[384,1024]{1,0:T(8,128)(2,1)S(1)}, u32[]{:S(2)}, u32[]{:S(2)}) collective-permute-start(bf16[384,1024]{1,0:T(8,128)(2,1)S(1)} %copy-done.14), channel_id=1, source_target_pairs={{0,6},{1,7},{2,0},{3,1},{4,2},{5,3},{6,4},{7,5},{8,14},{9,15},{10,... | collective-permute-start | bytes 2359304 | tf_op jit(solution)/shard_map/ppermute | solution.py:417
  32.5 19.3 %collective-permute-start.1 = (bf16[384,1024]{1,0:T(8,128)(2,1)S(1)}, bf16[384,1024]{1,0:T(8,128)(2,1)S(1)}, u32[]{:S(2)}, u32[]{:S(2)}) collective-permute-start(bf16[384,1024]{1,0:T(8,128)(2,1)S(1)} %copy-done.14), channel_id=1, source_target_pairs={{0,2},{1,3},{2,4},{3,5},{4,6},{5,7},{6,0},{7,1},{8,10},{9,11},{10,... | collective-permute-start | bytes 2359304 | tf_op jit(solution)/shard_map/ppermute | solution.py:416
  33.1 32.9 %collective-permute-start = (bf16[384,1024]{1,0:T(8,128)(2,1)S(1)}, bf16[384,1024]{1,0:T(8,128)(2,1)}, u32[]{:S(2)}, u32[]{:S(2)}) collective-permute-start(bf16[384,1024]{1,0:T(8,128)(2,1)S(1)} %copy-done.14), channel_id=1, source_target_pairs={{0,1},{1,0},{2,3},{3,2},{4,5},{5,4},{6,7},{7,6},{8,9},{9,8},{10,11... | collective-permute-start | bytes 2359304 | tf_op jit(solution)/shard_map/ppermute | solution.py:427
  52.0 14.0 %collective-permute-start.8 = (bf16[384,1024]{1,0:T(8,128)(2,1)S(1)}, bf16[384,1024]{1,0:T(8,128)(2,1)}, u32[]{:S(2)}, u32[]{:S(2)}) collective-permute-start(bf16[384,1024]{1,0:T(8,128)(2,1)S(1)} %collective-permute-done.4.refs_8_), channel_id=1, source_target_pairs={{0,1},{1,0},{2,3},{3,2},{4,5},{5,4},{6,7},{7,6},{8,9},{9,8},{10,11... | collective-permute-start | bytes 2359304 | tf_op jit(solution)/shard_map/ppermute | solution.py:427
  54.3 12.2 %collective-permute-start.2 = (bf16[384,1024]{1,0:T(8,128)(2,1)S(1)}, bf16[384,1024]{1,0:T(8,128)(2,1)}, u32[]{:S(2)}, u32[]{:S(2)}) collective-permute-start(bf16[384,1024]{1,0:T(8,128)(2,1)S(1)} %collective-permute-done.1.refs_2_), channel_id=1, source_target_pairs={{0,1},{1,0},{2,3},{3,2},{4,5},{5,4},{6,7},{7,6},{8,9},{9,8},{10,11... | collective-permute-start | bytes 2359304 | tf_op jit(solution)/shard_map/ppermute | solution.py:427
  78.5 60.7 %all-to-all-start.2 = ((bf16[16,896,128]{2,1,0:T(8,128)(2,1)}), bf16[16,896,128]{2,1,0:T(8,128)(2,1)}, u32[]{:S(2)}, u32[]{:S(2)}) async-start(bf16[16,896,128]{2,1,0:T(8,128)(2,1)} %copy-done.4), calls=%async_computation.2 | async-start | bytes 7340032 | tf_op jit(solution)/shard_map/all_to_all | solution.py:396
  90.4 16.8 %collective-permute-start.13 = (bf16[1024,384]{1,0:T(8,128)(2,1)S(1)}, bf16[1024,384]{1,0:T(8,128)(2,1)S(1)}, u32[]{:S(2)}, u32[]{:S(2)}) collective-permute-start(bf16[1024,384]{1,0:T(8,128)(2,1)S(1)} %pad_maximum_fusion.refs_0_), channel_id=1, source_target_pairs={{0,6},{1,7},{2,0},{3,1},{4,2},{5,3},{6,4},{7,5},{8,14},{9,15},{10,... | collective-permute-start | bytes 2359304 | tf_op jit(solution)/shard_map/ppermute | solution.py:417
  91.4 19.9 %collective-permute-start.10 = (bf16[1024,384]{1,0:T(8,128)(2,1)S(1)}, bf16[1024,384]{1,0:T(8,128)(2,1)S(1)}, u32[]{:S(2)}, u32[]{:S(2)}) collective-permute-start(bf16[1024,384]{1,0:T(8,128)(2,1)S(1)} %pad_maximum_fusion.refs_0_), channel_id=1, source_target_pairs={{0,2},{1,3},{2,4},{3,5},{4,6},{5,7},{6,0},{7,1},{8,10},{9,11},{10,... | collective-permute-start | bytes 2359304 | tf_op jit(solution)/shard_map/ppermute | solution.py:416
  107.3 10.5 %collective-permute-start.14 = (bf16[512,384]{1,0:T(8,128)(2,1)S(1)}, bf16[512,384]{1,0:T(8,128)(2,1)S(1)}, u32[]{:S(2)}, u32[]{:S(2)}) collective-permute-start(bf16[512,384]{1,0:T(8,128)(2,1)S(1)} %slice.42), channel_id=1, source_target_pairs={{0,6},{1,7},{2,0},{3,1},{4,2},{5,3},{6,4},{7,5},{8,14},{9,15},{10,... | collective-permute-start | bytes 1179656 | tf_op jit(solution)/shard_map/ppermute | solution.py:422
  111.5 13.6 %collective-permute-start.9 = (bf16[1024,384]{1,0:T(8,128)(2,1)S(1)}, bf16[1024,384]{1,0:T(8,128)(2,1)S(1)}, u32[]{:S(2)}, u32[]{:S(2)}) collective-permute-start(bf16[1024,384]{1,0:T(8,128)(2,1)S(1)} %pad_maximum_fusion.refs_0_), channel_id=1, source_target_pairs={{0,1},{1,0},{2,3},{3,2},{4,5},{5,4},{6,7},{7,6},{8,9},{9,8},{10,11... | collective-permute-start | bytes 2359304 | tf_op jit(solution)/shard_map/ppermute | solution.py:427
  114.7 10.4 %collective-permute-start.17 = (bf16[1024,384]{1,0:T(8,128)(2,1)S(1)}, bf16[1024,384]{1,0:T(8,128)(2,1)S(1)}, u32[]{:S(2)}, u32[]{:S(2)}) collective-permute-start(bf16[1024,384]{1,0:T(8,128)(2,1)S(1)} %collective-permute-done.13.refs_8_), channel_id=1, source_target_pairs={{0,1},{1,0},{2,3},{3,2},{4,5},{5,4},{6,7},{7,6},{8,9},{9,8},{10,11... | collective-permute-start | bytes 2359304 | tf_op jit(solution)/shard_map/ppermute | solution.py:427
  114.8 10.8 %collective-permute-start.11 = (bf16[1024,384]{1,0:T(8,128)(2,1)S(1)}, bf16[1024,384]{1,0:T(8,128)(2,1)S(1)}, u32[]{:S(2)}, u32[]{:S(2)}) collective-permute-start(bf16[1024,384]{1,0:T(8,128)(2,1)S(1)} %collective-permute-done.10.refs_2_), channel_id=1, source_target_pairs={{0,1},{1,0},{2,3},{3,2},{4,5},{5,4},{6,7},{7,6},{8,9},{9,8},{10,11... | collective-permute-start | bytes 2359304 | tf_op jit(solution)/shard_map/ppermute | solution.py:427
  148.7 13.1 %all-to-all-start.3 = ((f32[112,4,128]{2,1,0:T(4,128)}), f32[112,4,128]{2,1,0:T(4,128)S(1)}, u32[]{:S(2)}, u32[]{:S(2)}) async-start(f32[112,4,128]{2,1,0:T(4,128)} %shard_map.126), calls=%async_computation.3 | async-start | bytes 458752 | tf_op jit(solution)/shard_map/all_to_all | solution.py:396
  183.5 46.1 %all-to-all-start.5 = ((bf16[112,128,128]{2,1,0:T(8,128)(2,1)}), bf16[112,128,128]{2,1,0:T(8,128)(2,1)}, u32[]{:S(2)}, u32[]{:S(2)}) async-start(bf16[112,128,128]{2,1,0:T(8,128)(2,1)} %copy-done.5), calls=%async_computation.5 | async-start | bytes 7340032 | tf_op jit(solution)/shard_map/all_to_all | solution.py:396
  203.4 14.4 %collective-permute-start.20 = (bf16[384,256]{1,0:T(8,128)(2,1)S(1)}, bf16[384,256]{1,0:T(8,128)(2,1)S(1)}, u32[]{:S(2)}, u32[]{:S(2)}) collective-permute-start(bf16[384,256]{1,0:T(8,128)(2,1)S(1)} %get-tuple-element.71), channel_id=1, source_target_pairs={{0,3},{1,2},{2,5},{3,4},{4,7},{5,6},{6,1},{7,0},{8,11},{9,10},{10,... | collective-permute-start | bytes 589832 | tf_op jit(solution)/shard_map/ppermute | solution.py:434
  206.7 13.8 %collective-permute-start.21 = (bf16[384,256]{1,0:T(8,128)(2,1)S(1)}, bf16[384,256]{1,0:T(8,128)(2,1)S(1)}, u32[]{:S(2)}, u32[]{:S(2)}) collective-permute-start(bf16[384,256]{1,0:T(8,128)(2,1)S(1)} %get-tuple-element.72), channel_id=1, source_target_pairs={{0,4},{1,5},{2,6},{3,7},{4,0},{5,1},{6,2},{7,3},{8,12},{9,13},{10,... | collective-permute-start | bytes 589832 | tf_op jit(solution)/shard_map/ppermute | solution.py:434
  207.5 17.5 %collective-permute-start.22 = (bf16[384,256]{1,0:T(8,128)(2,1)S(1)}, bf16[384,256]{1,0:T(8,128)(2,1)S(1)}, u32[]{:S(2)}, u32[]{:S(2)}) collective-permute-start(bf16[384,256]{1,0:T(8,128)(2,1)S(1)} %get-tuple-element.73), channel_id=1, source_target_pairs={{0,5},{1,4},{2,7},{3,6},{4,1},{5,0},{6,3},{7,2},{8,13},{9,12},{10,... | collective-permute-start | bytes 589832 | tf_op jit(solution)/shard_map/ppermute | solution.py:434
  210.0 15.0 %collective-permute-start.23 = (bf16[384,256]{1,0:T(8,128)(2,1)S(1)}, bf16[384,256]{1,0:T(8,128)(2,1)S(1)}, u32[]{:S(2)}, u32[]{:S(2)}) collective-permute-start(bf16[384,256]{1,0:T(8,128)(2,1)S(1)} %get-tuple-element.74), channel_id=1, source_target_pairs={{0,6},{1,7},{2,0},{3,1},{4,2},{5,3},{6,4},{7,5},{8,14},{9,15},{10,... | collective-permute-start | bytes 589832 | tf_op jit(solution)/shard_map/ppermute | solution.py:434
  211.2 13.8 %collective-permute-start.24 = (bf16[384,256]{1,0:T(8,128)(2,1)S(1)}, bf16[384,256]{1,0:T(8,128)(2,1)S(1)}, u32[]{:S(2)}, u32[]{:S(2)}) collective-permute-start(bf16[384,256]{1,0:T(8,128)(2,1)S(1)} %get-tuple-element.75), channel_id=1, source_target_pairs={{0,7},{1,6},{2,1},{3,0},{4,3},{5,2},{6,5},{7,4},{8,15},{9,14},{10,... | collective-permute-start | bytes 589832 | tf_op jit(solution)/shard_map/ppermute | solution.py:434
  239.3 30.3 %all-to-all-start.6 = ((bf16[16,64,384]{2,1,0:T(8,128)(2,1)}), bf16[16,64,384]{2,1,0:T(8,128)(2,1)}, u32[]{:S(2)}, u32[]{:S(2)}) async-start(bf16[16,64,384]{2,1,0:T(8,128)(2,1)} %pad_maximum_fusion.1), calls=%async_computation.6 | async-start | bytes 1572864 | tf_op jit(solution)/shard_map/all_to_all | solution.py:396
  247.3 12.8 %collective-permute-start.25 = (bf16[384,128]{1,0:T(8,128)(2,1)S(1)}, bf16[384,128]{1,0:T(8,128)(2,1)S(1)}, u32[]{:S(2)}, u32[]{:S(2)}) collective-permute-start(bf16[384,128]{1,0:T(8,128)(2,1)S(1)} %get-tuple-element.78), channel_id=1, source_target_pairs={{0,1},{1,0},{2,3},{3,2},{4,5},{5,4},{6,7},{7,6},{8,9},{9,8},{10,11... | collective-permute-start | bytes 294920 | tf_op jit(solution)/shard_map/ppermute | solution.py:434
  252.2 12.9 %collective-permute-start.27 = (bf16[384,128]{1,0:T(8,128)(2,1)S(1)}, bf16[384,128]{1,0:T(8,128)(2,1)S(1)}, u32[]{:S(2)}, u32[]{:S(2)}) collective-permute-start(bf16[384,128]{1,0:T(8,128)(2,1)S(1)} %get-tuple-element.80), channel_id=1, source_target_pairs={{0,3},{1,2},{2,5},{3,4},{4,7},{5,6},{6,1},{7,0},{8,11},{9,10},{10,... | collective-permute-start | bytes 294920 | tf_op jit(solution)/shard_map/ppermute | solution.py:434
  (51 other events, 354.7 us)

commit v4 on v3

--- a/solution.py
+++ b/solution.py
@@ -512,23 +512,11 @@
     )(sources, *pieces, w_kv)
 
     w_all = jnp.concatenate([w_query, w_key, w_value], axis=1)
-    w_all, _ = lax.optimization_barrier((w_all, packed))
+    w_all, _ = lax.optimization_barrier((w_all, kv))
     found = head_gather(w_all)
     halves = [len(found[place]) for place in order]
     w_pieces = [piece for place in order for piece in found[place]]
-    w_rows, w_kv_rows = pl.pallas_call(
-        functools.partial(weights_kernel, halves),
-        out_shape=(
-            jax.ShapeDtypeStruct((width, n_head * cols), BF16),
-            jax.ShapeDtypeStruct((width, n_head * 2 * cols), BF16),
-        ),
-        in_specs=[VMEM] * len(w_pieces),
-        out_specs=(VMEM,) * 2,
-        compiler_params=params(ROWS_LIMIT),
-        cost_estimate=cost(0, 12 * width * n_head * cols),
-    )(*w_pieces)
-    far_queries, w_rows, w_kv_rows = lax.optimization_barrier((far_queries, w_rows, w_kv_rows))
-
+    far_queries, *w_pieces = lax.optimization_barrier((far_queries, *w_pieces))
     unit_flops = 2 * heads * BLOCK * BLOCK * cols
     tile_bytes = 2 * BLOCK * cols
     stats_shape = jax.ShapeDtypeStruct((slots, 2 * heads, BLOCK), F32)
@@ -608,10 +596,24 @@
         mask,
     )
 
+    grad_key_value, *w_pieces = lax.optimization_barrier((grad_key_value, *w_pieces))
+    w_rows, w_kv_rows = pl.pallas_call(
+        functools.partial(weights_kernel, halves),
+        out_shape=(
+            jax.ShapeDtypeStruct((width, n_head * cols), BF16),
+            jax.ShapeDtypeStruct((width, n_head * 2 * cols), BF16),
+        ),
+        in_specs=[VMEM] * len(w_pieces),
+        out_specs=(VMEM,) * 2,
+        compiler_params=params(ROWS_LIMIT),
+        cost_estimate=cost(0, 12 * width * n_head * cols),
+    )(*w_pieces)
     contract_rows = (((0,), (0,)), ((), ()))
     chunks = head_send(chunks)
     term_key_value = lax.dot_general(gathered, grad_key_value, contract_rows, preferred_element_type=F32)
-    back_terms, *chunks = lax.optimization_barrier((back_terms, *chunks))
+    back_terms, w_rows, w_kv_rows, *chunks = lax.optimization_barrier(
+        (back_terms, w_rows, w_kv_rows, *chunks)
+    )
     summed = pl.pallas_call(
         functools.partial(rows_kernel, n_head),
         out_shape=jax.ShapeDtypeStruct((rows, width), F32),

time: 271 us -> 270 us (level)
  waiting for transfers between devices: 72.7 us -> 56.9 us
  Pallas kernels: 46.9 us -> 51.6 us
  starting transfers between devices: 98 us -> 102 us
  local copies, waits for them, and re-layouts: 26 us -> 29.4 us
    ppermute x14, waiting for transfers between devices: 11 us -> 1.62 us  [head_send(): lax.ppermute(c, 'head', head_pairs(*place))]
    all_to_all x5, waiting for transfers between devices: 12.7 us -> 7.95 us  [seq_exchange(): return lax.all_to_all(x, 'seq', split_axis=0, concat_axis=0, tiled=True)]
    ppermute x14, starting transfers between devices: 25.2 us -> 28.5 us  [head_send(): lax.ppermute(c, 'head', head_pairs(*place))]
    unnamed x74 -> x102, local copies, waits for them, and re-layouts: 22.3 us -> 24.8 us
  transfers between devices with their start and end apart: 38 -> 38, of which waited for: 17 -> 12; matrix products, arithmetic and copies ran while one was open for 4% -> 5% of each run, Pallas kernels for 10% -> 11%
where the time goes in v4:
time: 270 us; the launch traced here: 269 us
  starting transfers between devices  102 us (38%)
  waiting for transfers between devices  56.9 us (21%)
  Pallas kernels  51.6 us (19%)
  local copies, waits for them, and re-layouts  29.4 us (11%)
  blocking collectives  10.6 us (4%)
  matrix products  10.4 us (4%)
  other arithmetic  6.97 us (3%)
    all_to_all x5, starting transfers between devices, seq_exchange(): return lax.all_to_all(x, 'seq', split_axis=0, concat_axis=0, tiled=True)  36.3 us
    ppermute x2, waiting for transfers between devices, head_gather(): down = lax.ppermute(down, 'head', head_pairs(-1, 0))  30.3 us
    ppermute x14, starting transfers between devices, head_send(): lax.ppermute(c, 'head', head_pairs(*place))  28.5 us
    unnamed x102, local copies, waits for them, and re-layouts  24.8 us
    ppermute x10, starting transfers between devices, head_gather(): lax.ppermute(b, 'head', head_pairs(0, 1))  21.4 us
    pallas_call x1, Pallas kernels, shards(): pl.pallas_call(functools.partial(key_value_kernel, per), out_shape=(jax.S...  12.1 us
    all_to_all x1, blocking collectives, seq_exchange(): return lax.all_to_all(x, 'seq', split_axis=0, concat_axis=0, tiled=True)  10.6 us
    all_to_all x1, waiting for transfers between devices, shards(): lax.all_to_all(grad_context, 'head', split_axis=1, concat_axis=0, tiled=T...  10 us
  transfers between devices with their start and end apart: 38, of which 12 were waited for; matrix products, arithmetic and copies ran while one was open for 5% of the time, Pallas kernels for 11%

profile of v4, /device:TPU:1, one launch (start us, length us, event | category | flops | bytes accessed | tf_op | source)
XLA Modules:
  0.0 269.1 jit_solution(13820899077890528151)
XLA Ops:
  2.8 6.8 %all-to-all-start = ((bf16[384,8,128]{2,0,1:T(8,128)(2,1)}), bf16[384,8,128]{2,0,1:T(8,128)(2,1)S(1)}, u32[]{:S(2)}, u32[]{:S(2)}) async-start(bf16[384,8,128]{2,0,1:T(8,128)(2,1)} %copy_bitcast_fusion), calls=%async_computation | async-start | bytes 1572864 | tf_op jit(solution)/shard_map/all_to_all | solution.py:468
  11.9 10.0 %all-to-all-done = bf16[384,8,128]{2,0,1:T(8,128)(2,1)S(1)} async-done(((bf16[384,8,128]{2,0,1:T(8,128)(2,1)}), bf16[384,8,128]{2,0,1:T(8,128)(2,1)S(1)}, u32[]{:S(2)}, u32[]{:S(2)}) %all-to-all-start) | async-done | bytes 786464 | tf_op jit(solution)/shard_map/all_to_all | solution.py:468
  24.7 6.9 %all-to-all-start.1 = ((bf16[16,912,128]{2,1,0:T(8,128)(2,1)}), bf16[16,912,128]{2,1,0:T(8,128)(2,1)}, u32[]{:S(2)}, u32[]{:S(2)}) async-start(bf16[16,912,128]{2,1,0:T(8,128)(2,1)} %copy-done.3), calls=%async_computation.1 | async-start | bytes 7471104 | tf_op jit(solution)/shard_map/all_to_all | solution.py:396
  34.8 14.8 %collective-permute-done.4.refs_8_ = bf16[384,1024]{1,0:T(8,128)(2,1)S(1)} collective-permute-done((bf16[384,1024]{1,0:T(8,128)(2,1)S(1)}, bf16[384,1024]{1,0:T(8,128)(2,1)S(1)}, u32[]{:S(2)}, u32[]{:S(2)}) %collective-permute-start.4) | collective-permute-done | bytes 786464 | tf_op jit(solution)/shard_map/ppermute | solution.py:417
  54.4 4.1 %collective-permute-done.5.refs_5_ = bf16[192,1024]{1,0:T(8,128)(2,1)S(1)} collective-permute-done((bf16[192,1024]{1,0:T(8,128)(2,1)S(1)}, bf16[192,1024]{1,0:T(8,128)(2,1)S(1)}, u32[]{:S(2)}, u32[]{:S(2)}) %collective-permute-start.5) | collective-permute-done | bytes 393248 | tf_op jit(solution)/shard_map/ppermute | solution.py:422
  67.5 3.9 %shard_map.121 = bf16[3072,128]{1,0:T(8,128)(2,1)S(1)} custom-call(s32[8]{0:T(128)S(1)} %get-tuple-element.146.source_ref, bf16[384,1024]{1,0:T(8,128)(2,1)S(1)} %copy-done.14, bf16[384,1024]{1,0:T(8,128)(2,1)} %collective-permute-done.refs_1_, bf16[384,1024]{1,0:T(8,128)(2,1)S(1)} %collective-permute-done.1.refs_2_, ...), custom_call_target="tpu_custom_call" | custom-call | flops 805306368 | bytes 6291456 | tf_op jit(solution)/shard_map/pallas_call | solution.py:489
  74.9 3.6 %all-to-all-done.1.grad_ref.far_grad_ref = bf16[16,912,128]{2,1,0:T(8,128)(2,1)} async-done(((bf16[16,912,128]{2,1,0:T(8,128)(2,1)}), bf16[16,912,128]{2,1,0:T(8,128)(2,1)}, u32[]{:S(2)}, u32[]{:S(2)}) %all-to-all-start.1) | async-done | bytes 3735584 | tf_op jit(solution)/shard_map/all_to_all | solution.py:396
  78.5 11.8 %all-to-all-start.2 = ((bf16[16,896,128]{2,1,0:T(8,128)(2,1)}), bf16[16,896,128]{2,1,0:T(8,128)(2,1)}, u32[]{:S(2)}, u32[]{:S(2)}) async-start(bf16[16,896,128]{2,1,0:T(8,128)(2,1)} %copy-done.4), calls=%async_computation.2 | async-start | bytes 7340032 | tf_op jit(solution)/shard_map/all_to_all | solution.py:396
  92.0 4.3 %shard_map.123 = (bf16[3072,256]{1,0:T(8,128)(2,1)S(1)}, bf16[3072,1024]{1,0:T(8,128)(2,1)S(1)}) custom-call(s32[8]{0:T(128)S(1)} %get-tuple-element.146.source_ref, bf16[384,1024]{1,0:T(8,128)(2,1)S(1)} %copy-done.15, bf16[384,1024]{1,0:T(8,128)(2,1)} %collective-permute-done.refs_1_, bf16[384,1024]{1,0:T(8,128)(2,1)S(1)} %copy-done.11, ...), custom_call_target="tpu_custom_call" | custom-call | flops 1610612736 | bytes 12582912 | tf_op jit(solution)/shard_map/pallas_call | solution.py:502
  100.4 15.5 %collective-permute-done.13.refs_8_ = bf16[1024,384]{1,0:T(8,128)(2,1)S(1)} collective-permute-done((bf16[1024,384]{1,0:T(8,128)(2,1)}, bf16[1024,384]{1,0:T(8,128)(2,1)S(1)}, u32[]{:S(2)}, u32[]{:S(2)}) %collective-permute-start.13) | collective-permute-done | bytes 786464 | tf_op jit(solution)/shard_map/ppermute | solution.py:417
  129.9 4.0 %collective-permute-start.15 = (bf16[512,384]{1,0:T(8,128)(2,1)}, bf16[512,384]{1,0:T(8,128)(2,1)}, u32[]{:S(2)}, u32[]{:S(2)}) collective-permute-start(bf16[512,384]{1,0:T(8,128)(2,1)} %collective-permute-done.12.refs_4_), channel_id=1, source_target_pairs={{0,1},{1,0},{2,3},{3,2},{4,5},{5,4},{6,7},{7,6},{8,9},{9,8},{10,11... | collective-permute-start | bytes 1179656 | tf_op jit(solution)/shard_map/ppermute | solution.py:427
  136.1 8.6 %shard_map.125 = f32[112,4,128]{2,1,0:T(4,128)} custom-call(s32[1]{0:T(128)} %bitcast.3.count_ref, s32[112]{0:T(128)S(1)} %select_reduce_fusion.order_ref, s32[112]{0:T(128)S(1)} %reshape.259.meta_ref, bf16[16,896,128]{2,1,0:T(8,128)(2,1)} %all-to-all-done.2.query_ref.far_query_ref, bf16[16,912,128]{2,1,0:T(8,128)(2,1)} %all-to-all-done.1.grad_ref.far_grad_ref, ...), custom_call_target="tpu_custom_call" | custom-call | flops 1879048192 | bytes 7340032 | tf_op jit(solution)/shard_map/pallas_call | solution.py:531
  144.7 5.8 %all-to-all-start.3 = ((f32[112,4,128]{2,1,0:T(4,128)}), f32[112,4,128]{2,1,0:T(4,128)S(1)}, u32[]{:S(2)}, u32[]{:S(2)}) async-start(f32[112,4,128]{2,1,0:T(4,128)} %shard_map.125), calls=%async_computation.3 | async-start | bytes 458752 | tf_op jit(solution)/shard_map/all_to_all | solution.py:396
  153.3 4.4 %all-to-all-done.3.far_ref = f32[112,4,128]{2,1,0:T(4,128)S(1)} async-done(((f32[112,4,128]{2,1,0:T(4,128)}), f32[112,4,128]{2,1,0:T(4,128)S(1)}, u32[]{:S(2)}, u32[]{:S(2)}) %all-to-all-start.3) | async-done | bytes 229408 | tf_op jit(solution)/shard_map/all_to_all | solution.py:396
  159.1 10.6 %all_to_all.46.far_stats_ref.stats_ref = f32[112,4,128]{2,1,0:T(4,128)S(1)} all-to-all(f32[112,4,128]{2,1,0:T(4,128)S(1)} %get-tuple-element.86), channel_id=1, replica_groups=mesh['seq'=16,'head'=8] {'seq'}, dimensions={0} | all-to-all | bytes 458752 | tf_op jit(solution)/shard_map/all_to_all | solution.py:396
  169.7 8.4 %shard_map.128 = bf16[112,128,128]{2,1,0:T(8,128)(2,1)S(1)} custom-call(s32[1]{0:T(128)} %bitcast.3.count_ref, s32[112]{0:T(128)S(1)} %select_reduce_fusion.order_ref, s32[112]{0:T(128)S(1)} %reshape.259.meta_ref, bf16[16,896,128]{2,1,0:T(8,128)(2,1)} %all-to-all-done.2.query_ref.far_query_ref, bf16[16,912,128]{2,1,0:T(8,128)(2,1)} %all-to-all-done.1.grad_ref.far_grad_ref, ...), custom_call_target="tpu_custom_call" | custom-call | flops 2818572288 | bytes 11010048 | tf_op jit(solution)/shard_map/pallas_call | solution.py:550
  180.0 4.6 %all-to-all-start.5 = ((bf16[112,128,128]{2,1,0:T(8,128)(2,1)}), bf16[112,128,128]{2,1,0:T(8,128)(2,1)}, u32[]{:S(2)}, u32[]{:S(2)}) async-start(bf16[112,128,128]{2,1,0:T(8,128)(2,1)} %copy-done.5), calls=%async_computation.5 | async-start | bytes 7340032 | tf_op jit(solution)/shard_map/all_to_all | solution.py:396
  185.5 12.1 %shard_map.127 = (f32[24,128,128]{2,1,0:T(8,128)S(1)}, bf16[3072,256]{1,0:T(8,128)(2,1)S(1)}, bf16[384,256]{1,0:T(8,128)(2,1)S(1)}, bf16[384,256]{1,0:T(8,128)(2...) custom-call(s32[8]{0:T(128)S(1)} %fusion.9.target_ref, ...), custom_call_target="tpu_custom_call" | custom-call | flops 4697620480 | bytes 11010048 | tf_op jit(solution)/shard_map/pallas_call | solution.py:570
  198.9 4.3 %collective-permute-start.18 = (bf16[384,256]{1,0:T(8,128)(2,1)S(1)}, bf16[384,256]{1,0:T(8,128)(2,1)S(1)}, u32[]{:S(2)}, u32[]{:S(2)}) collective-permute-start(bf16[384,256]{1,0:T(8,128)(2,1)S(1)} %get-tuple-element.113), channel_id=1, source_target_pairs={{0,1},{1,0},{2,3},{3,2},{4,5},{5,4},{6,7},{7,6},{8,9},{9,8},{10,11... | collective-permute-start | bytes 589832 | tf_op jit(solution)/shard_map/ppermute | solution.py:434
  203.4 4.8 %collective-permute-start.20 = (bf16[384,256]{1,0:T(8,128)(2,1)S(1)}, bf16[384,256]{1,0:T(8,128)(2,1)S(1)}, u32[]{:S(2)}, u32[]{:S(2)}) collective-permute-start(bf16[384,256]{1,0:T(8,128)(2,1)S(1)} %get-tuple-element.115), channel_id=1, source_target_pairs={{0,3},{1,2},{2,5},{3,4},{4,7},{5,6},{6,1},{7,0},{8,11},{9,10},{10,... | collective-permute-start | bytes 589832 | tf_op jit(solution)/shard_map/ppermute | solution.py:434
  214.6 5.5 %convolution_convert_fusion = bf16[1024,256]{1,0:T(8,128)(2,1)} fusion(bf16[3072,1024]{1,0:T(8,128)(2,1)} %copy-done.9, bf16[3072,256]{1,0:T(8,128)(2,1)S(1)} %get-tuple-element.141), kind=kOutput, calls=%fused_computation.2 | convolution fusion | flops 1610874880 | bytes 8388608 | tf_op jit(solution)/shard_map/dot_general | solution.py:613
  220.1 3.7 %shard_map.129 = (bf16[1024,1024]{1,0:T(8,128)(2,1)S(1)}, bf16[1024,2048]{1,0:T(8,128)(2,1)S(1)}) custom-call(bf16[1024,384]{1,0:T(8,128)(2,1)} %pad_maximum_fusion.refs_0_, bf16[1024,384]{1,0:T(8,128)(2,1)} %collective-permute-done.9.refs_1_, bf16[1024,384]{1,0:T(8,128)(2,1)} %collective-permute-done.10.refs_2_, ...), custom_call_target="tpu_custom_call" | custom-call | bytes 12582912 | tf_op jit(solution)/shard_map/pallas_call | solution.py:600
  232.7 4.8 %convolution_convert_fusion.1 = bf16[1024,128]{1,0:T(8,128)(2,1)S(1)} fusion(bf16[3072,1024]{1,0:T(8,128)(2,1)} %copy-done.9, bf16[3072,128]{1,0:T(8,128)(2,1)S(1)} %get-tuple-element.140), kind=kOutput, calls=%fused_computation.3 | convolution fusion | flops 805437440 | bytes 7340032 | tf_op jit(solution)/shard_map/dot_general | solution.py:635
  238.7 7.1 %all-to-all-start.6 = ((bf16[16,64,384]{2,1,0:T(8,128)(2,1)}), bf16[16,64,384]{2,1,0:T(8,128)(2,1)}, u32[]{:S(2)}, u32[]{:S(2)}) async-start(bf16[16,64,384]{2,1,0:T(8,128)(2,1)} %pad_maximum_fusion.1), calls=%async_computation.6 | async-start | bytes 1572864 | tf_op jit(solution)/shard_map/all_to_all | solution.py:396
  (208 shorter events, 97.1 us)
Async XLA Ops:
  2.8 19.1 %all-to-all-start = ((bf16[384,8,128]{2,0,1:T(8,128)(2,1)}), bf16[384,8,128]{2,0,1:T(8,128)(2,1)S(1)}, u32[]{:S(2)}, u32[]{:S(2)}) async-start(bf16[384,8,128]{2,0,1:T(8,128)(2,1)} %copy_bitcast_fusion), calls=%async_computation | async-start | bytes 1572864 | tf_op jit(solution)/shard_map/all_to_all | solution.py:468
  24.7 53.8 %all-to-all-start.1 = ((bf16[16,912,128]{2,1,0:T(8,128)(2,1)}), bf16[16,912,128]{2,1,0:T(8,128)(2,1)}, u32[]{:S(2)}, u32[]{:S(2)}) async-start(bf16[16,912,128]{2,1,0:T(8,128)(2,1)} %copy-done.3), calls=%async_computation.1 | async-start | bytes 7471104 | tf_op jit(solution)/shard_map/all_to_all | solution.py:396
  31.6 18.1 %collective-permute-start.4 = (bf16[384,1024]{1,0:T(8,128)(2,1)S(1)}, bf16[384,1024]{1,0:T(8,128)(2,1)S(1)}, u32[]{:S(2)}, u32[]{:S(2)}) collective-permute-start(bf16[384,1024]{1,0:T(8,128)(2,1)S(1)} %copy-done.14), channel_id=1, source_target_pairs={{0,6},{1,7},{2,0},{3,1},{4,2},{5,3},{6,4},{7,5},{8,14},{9,15},{10,... | collective-permute-start | bytes 2359304 | tf_op jit(solution)/shard_map/ppermute | solution.py:417
  32.6 19.3 %collective-permute-start.1 = (bf16[384,1024]{1,0:T(8,128)(2,1)S(1)}, bf16[384,1024]{1,0:T(8,128)(2,1)S(1)}, u32[]{:S(2)}, u32[]{:S(2)}) collective-permute-start(bf16[384,1024]{1,0:T(8,128)(2,1)S(1)} %copy-done.14), channel_id=1, source_target_pairs={{0,2},{1,3},{2,4},{3,5},{4,6},{5,7},{6,0},{7,1},{8,10},{9,11},{10,... | collective-permute-start | bytes 2359304 | tf_op jit(solution)/shard_map/ppermute | solution.py:416
  33.1 32.9 %collective-permute-start = (bf16[384,1024]{1,0:T(8,128)(2,1)S(1)}, bf16[384,1024]{1,0:T(8,128)(2,1)}, u32[]{:S(2)}, u32[]{:S(2)}) collective-permute-start(bf16[384,1024]{1,0:T(8,128)(2,1)S(1)} %copy-done.14), channel_id=1, source_target_pairs={{0,1},{1,0},{2,3},{3,2},{4,5},{5,4},{6,7},{7,6},{8,9},{9,8},{10,11... | collective-permute-start | bytes 2359304 | tf_op jit(solution)/shard_map/ppermute | solution.py:427
  52.0 14.0 %collective-permute-start.8 = (bf16[384,1024]{1,0:T(8,128)(2,1)S(1)}, bf16[384,1024]{1,0:T(8,128)(2,1)}, u32[]{:S(2)}, u32[]{:S(2)}) collective-permute-start(bf16[384,1024]{1,0:T(8,128)(2,1)S(1)} %collective-permute-done.4.refs_8_), channel_id=1, source_target_pairs={{0,1},{1,0},{2,3},{3,2},{4,5},{5,4},{6,7},{7,6},{8,9},{9,8},{10,11... | collective-permute-start | bytes 2359304 | tf_op jit(solution)/shard_map/ppermute | solution.py:427
  54.3 12.2 %collective-permute-start.2 = (bf16[384,1024]{1,0:T(8,128)(2,1)S(1)}, bf16[384,1024]{1,0:T(8,128)(2,1)}, u32[]{:S(2)}, u32[]{:S(2)}) collective-permute-start(bf16[384,1024]{1,0:T(8,128)(2,1)S(1)} %collective-permute-done.1.refs_2_), channel_id=1, source_target_pairs={{0,1},{1,0},{2,3},{3,2},{4,5},{5,4},{6,7},{7,6},{8,9},{9,8},{10,11... | collective-permute-start | bytes 2359304 | tf_op jit(solution)/shard_map/ppermute | solution.py:427
  78.5 57.6 %all-to-all-start.2 = ((bf16[16,896,128]{2,1,0:T(8,128)(2,1)}), bf16[16,896,128]{2,1,0:T(8,128)(2,1)}, u32[]{:S(2)}, u32[]{:S(2)}) async-start(bf16[16,896,128]{2,1,0:T(8,128)(2,1)} %copy-done.4), calls=%async_computation.2 | async-start | bytes 7340032 | tf_op jit(solution)/shard_map/all_to_all | solution.py:396
  98.9 17.0 %collective-permute-start.13 = (bf16[1024,384]{1,0:T(8,128)(2,1)}, bf16[1024,384]{1,0:T(8,128)(2,1)S(1)}, u32[]{:S(2)}, u32[]{:S(2)}) collective-permute-start(bf16[1024,384]{1,0:T(8,128)(2,1)} %pad_maximum_fusion.refs_0_), channel_id=1, source_target_pairs={{0,6},{1,7},{2,0},{3,1},{4,2},{5,3},{6,4},{7,5},{8,14},{9,15},{10,... | collective-permute-start | bytes 2359304 | tf_op jit(solution)/shard_map/ppermute | solution.py:417
  99.8 20.2 %collective-permute-start.10 = (bf16[1024,384]{1,0:T(8,128)(2,1)}, bf16[1024,384]{1,0:T(8,128)(2,1)}, u32[]{:S(2)}, u32[]{:S(2)}) collective-permute-start(bf16[1024,384]{1,0:T(8,128)(2,1)} %pad_maximum_fusion.refs_0_), channel_id=1, source_target_pairs={{0,2},{1,3},{2,4},{3,5},{4,6},{5,7},{6,0},{7,1},{8,10},{9,11},{10,... | collective-permute-start | bytes 2359304 | tf_op jit(solution)/shard_map/ppermute | solution.py:416
  121.3 14.8 %collective-permute-start.9 = (bf16[1024,384]{1,0:T(8,128)(2,1)}, bf16[1024,384]{1,0:T(8,128)(2,1)}, u32[]{:S(2)}, u32[]{:S(2)}) collective-permute-start(bf16[1024,384]{1,0:T(8,128)(2,1)} %pad_maximum_fusion.refs_0_), channel_id=1, source_target_pairs={{0,1},{1,0},{2,3},{3,2},{4,5},{5,4},{6,7},{7,6},{8,9},{9,8},{10,11... | collective-permute-start | bytes 2359304 | tf_op jit(solution)/shard_map/ppermute | solution.py:427
  124.5 11.5 %collective-permute-start.17 = (bf16[1024,384]{1,0:T(8,128)(2,1)S(1)}, bf16[1024,384]{1,0:T(8,128)(2,1)}, u32[]{:S(2)}, u32[]{:S(2)}) collective-permute-start(bf16[1024,384]{1,0:T(8,128)(2,1)S(1)} %collective-permute-done.13.refs_8_), channel_id=1, source_target_pairs={{0,1},{1,0},{2,3},{3,2},{4,5},{5,4},{6,7},{7,6},{8,9},{9,8},{10,11... | collective-permute-start | bytes 2359304 | tf_op jit(solution)/shard_map/ppermute | solution.py:427
  124.6 11.4 %collective-permute-start.11 = (bf16[1024,384]{1,0:T(8,128)(2,1)}, bf16[1024,384]{1,0:T(8,128)(2,1)}, u32[]{:S(2)}, u32[]{:S(2)}) collective-permute-start(bf16[1024,384]{1,0:T(8,128)(2,1)} %collective-permute-done.10.refs_2_), channel_id=1, source_target_pairs={{0,1},{1,0},{2,3},{3,2},{4,5},{5,4},{6,7},{7,6},{8,9},{9,8},{10,11... | collective-permute-start | bytes 2359304 | tf_op jit(solution)/shard_map/ppermute | solution.py:427
  144.7 12.9 %all-to-all-start.3 = ((f32[112,4,128]{2,1,0:T(4,128)}), f32[112,4,128]{2,1,0:T(4,128)S(1)}, u32[]{:S(2)}, u32[]{:S(2)}) async-start(f32[112,4,128]{2,1,0:T(4,128)} %shard_map.125), calls=%async_computation.3 | async-start | bytes 458752 | tf_op jit(solution)/shard_map/all_to_all | solution.py:396
  180.0 48.6 %all-to-all-start.5 = ((bf16[112,128,128]{2,1,0:T(8,128)(2,1)}), bf16[112,128,128]{2,1,0:T(8,128)(2,1)}, u32[]{:S(2)}, u32[]{:S(2)}) async-start(bf16[112,128,128]{2,1,0:T(8,128)(2,1)} %copy-done.5), calls=%async_computation.5 | async-start | bytes 7340032 | tf_op jit(solution)/shard_map/all_to_all | solution.py:396
  198.9 12.7 %collective-permute-start.18 = (bf16[384,256]{1,0:T(8,128)(2,1)S(1)}, bf16[384,256]{1,0:T(8,128)(2,1)S(1)}, u32[]{:S(2)}, u32[]{:S(2)}) collective-permute-start(bf16[384,256]{1,0:T(8,128)(2,1)S(1)} %get-tuple-element.113), channel_id=1, source_target_pairs={{0,1},{1,0},{2,3},{3,2},{4,5},{5,4},{6,7},{7,6},{8,9},{9,8},{10,11... | collective-permute-start | bytes 589832 | tf_op jit(solution)/shard_map/ppermute | solution.py:434
  203.4 22.5 %collective-permute-start.20 = (bf16[384,256]{1,0:T(8,128)(2,1)S(1)}, bf16[384,256]{1,0:T(8,128)(2,1)S(1)}, u32[]{:S(2)}, u32[]{:S(2)}) collective-permute-start(bf16[384,256]{1,0:T(8,128)(2,1)S(1)} %get-tuple-element.115), channel_id=1, source_target_pairs={{0,3},{1,2},{2,5},{3,4},{4,7},{5,6},{6,1},{7,0},{8,11},{9,10},{10,... | collective-permute-start | bytes 589832 | tf_op jit(solution)/shard_map/ppermute | solution.py:434
  208.2 17.7 %collective-permute-start.21 = (bf16[384,256]{1,0:T(8,128)(2,1)S(1)}, bf16[384,256]{1,0:T(8,128)(2,1)S(1)}, u32[]{:S(2)}, u32[]{:S(2)}) collective-permute-start(bf16[384,256]{1,0:T(8,128)(2,1)S(1)} %get-tuple-element.116), channel_id=1, source_target_pairs={{0,4},{1,5},{2,6},{3,7},{4,0},{5,1},{6,2},{7,3},{8,12},{9,13},{10,... | collective-permute-start | bytes 589832 | tf_op jit(solution)/shard_map/ppermute | solution.py:434
  208.4 18.2 %collective-permute-start.22 = (bf16[384,256]{1,0:T(8,128)(2,1)S(1)}, bf16[384,256]{1,0:T(8,128)(2,1)S(1)}, u32[]{:S(2)}, u32[]{:S(2)}) collective-permute-start(bf16[384,256]{1,0:T(8,128)(2,1)S(1)} %get-tuple-element.117), channel_id=1, source_target_pairs={{0,5},{1,4},{2,7},{3,6},{4,1},{5,0},{6,3},{7,2},{8,13},{9,12},{10,... | collective-permute-start | bytes 589832 | tf_op jit(solution)/shard_map/ppermute | solution.py:434
  211.6 15.7 %collective-permute-start.23 = (bf16[384,256]{1,0:T(8,128)(2,1)S(1)}, bf16[384,256]{1,0:T(8,128)(2,1)S(1)}, u32[]{:S(2)}, u32[]{:S(2)}) collective-permute-start(bf16[384,256]{1,0:T(8,128)(2,1)S(1)} %get-tuple-element.118), channel_id=1, source_target_pairs={{0,6},{1,7},{2,0},{3,1},{4,2},{5,3},{6,4},{7,5},{8,14},{9,15},{10,... | collective-permute-start | bytes 589832 | tf_op jit(solution)/shard_map/ppermute | solution.py:434
  211.6 16.3 %collective-permute-start.24 = (bf16[384,256]{1,0:T(8,128)(2,1)S(1)}, bf16[384,256]{1,0:T(8,128)(2,1)S(1)}, u32[]{:S(2)}, u32[]{:S(2)}) collective-permute-start(bf16[384,256]{1,0:T(8,128)(2,1)S(1)} %get-tuple-element.119), channel_id=1, source_target_pairs={{0,7},{1,6},{2,1},{3,0},{4,3},{5,2},{6,5},{7,4},{8,15},{9,14},{10,... | collective-permute-start | bytes 589832 | tf_op jit(solution)/shard_map/ppermute | solution.py:434
  238.7 28.4 %all-to-all-start.6 = ((bf16[16,64,384]{2,1,0:T(8,128)(2,1)}), bf16[16,64,384]{2,1,0:T(8,128)(2,1)}, u32[]{:S(2)}, u32[]{:S(2)}) async-start(bf16[16,64,384]{2,1,0:T(8,128)(2,1)} %pad_maximum_fusion.1), calls=%async_computation.6 | async-start | bytes 1572864 | tf_op jit(solution)/shard_map/all_to_all | solution.py:396
  245.9 11.6 %collective-permute-start.25 = (bf16[384,128]{1,0:T(8,128)(2,1)}, bf16[384,128]{1,0:T(8,128)(2,1)S(1)}, u32[]{:S(2)}, u32[]{:S(2)}) collective-permute-start(bf16[384,128]{1,0:T(8,128)(2,1)} %copy-done.42), channel_id=1, source_target_pairs={{0,1},{1,0},{2,3},{3,2},{4,5},{5,4},{6,7},{7,6},{8,9},{9,8},{10,11... | collective-permute-start | bytes 294920 | tf_op jit(solution)/shard_map/ppermute | solution.py:434
  251.9 11.7 %collective-permute-start.27 = (bf16[384,128]{1,0:T(8,128)(2,1)}, bf16[384,128]{1,0:T(8,128)(2,1)S(1)}, u32[]{:S(2)}, u32[]{:S(2)}) collective-permute-start(bf16[384,128]{1,0:T(8,128)(2,1)} %copy-done.40), channel_id=1, source_target_pairs={{0,3},{1,2},{2,5},{3,4},{4,7},{5,6},{6,1},{7,0},{8,11},{9,10},{10,... | collective-permute-start | bytes 294920 | tf_op jit(solution)/shard_map/ppermute | solution.py:434
  (65 other events, 454.5 us)

commit v5 on v4

--- a/solution.py
+++ b/solution.py
@@ -18,7 +18,7 @@
 PACK_LIMIT = 8 * MIB
 ROWS_LIMIT = 24 * MIB
 ATTEND_LIMIT = 28 * MIB
-TAIL_LIMIT = 24 * MIB
+TAIL_LIMIT = 36 * MIB
 VMEM = pl.BlockSpec(memory_space=pltpu.VMEM)
 SMEM = pl.BlockSpec(memory_space=pltpu.SMEM)
 NT = (((1,), (1,)), ((), ()))
@@ -629,13 +629,15 @@
         + (jax.ShapeDtypeStruct((rows, cols), BF16),) * n_head,
         in_specs=[SMEM] * 3 + [VMEM] * 2,
         out_specs=(VMEM,) * (1 + n_head),
-        compiler_params=params(TAIL_LIMIT),
+        compiler_params=params(ATTEND_LIMIT * 2),
         cost_estimate=cost(0, slots * tile_bytes),
     )(targets, slot_of, counts, own_terms, back_terms)
     term_query = lax.dot_general(gathered, grad_query, contract_rows, preferred_element_type=F32)
     weight_terms = jnp.concatenate([term_query, term_key_value], axis=1).astype(BF16)
     weight_terms = seq_exchange(weight_terms.reshape(n_seq, width // n_seq, 3 * cols))
-    weight_grads = jnp.sum(weight_terms.astype(F32), axis=0)
+    weight_grads = [
+        jnp.sum(weight_terms[:, :, i * cols : (i + 1) * cols].astype(F32), axis=0) for i in range(3)
+    ]
     chunks = head_send(chunks)
     grad_input = pl.pallas_call(
         functools.partial(rows_kernel, n_head),
@@ -647,9 +649,7 @@
     )(*chunks, w_rows, summed)
     return (
         grad_input,
-        weight_grads[:, :cols],
-        weight_grads[:, cols : 2 * cols],
-        weight_grads[:, 2 * cols :],
+        *weight_grads,
     )
 
 

time: 270 us -> 268 us (level)
    unnamed x102 -> x88, local copies, waits for them, and re-layouts: 24.8 us -> 23.3 us
where the time goes in v5:
time: 268 us
  starting transfers between devices  104 us (39%)
  waiting for transfers between devices  56.8 us (21%)
  Pallas kernels  49.2 us (18%)
  local copies, waits for them, and re-layouts  27.4 us (10%)
  blocking collectives  10.6 us (4%)
  matrix products  10.4 us (4%)
  other arithmetic  7.61 us (3%)
    all_to_all x5, starting transfers between devices, seq_exchange(): return lax.all_to_all(x, 'seq', split_axis=0, concat_axis=0, tiled=True)  38.7 us
    ppermute x2, waiting for transfers between devices, head_gather(): down = lax.ppermute(down, 'head', head_pairs(-1, 0))  30.3 us
    ppermute x14, starting transfers between devices, head_send(): lax.ppermute(c, 'head', head_pairs(*place))  28.8 us
    unnamed x88, local copies, waits for them, and re-layouts  23.3 us
    ppermute x10, starting transfers between devices, head_gather(): lax.ppermute(b, 'head', head_pairs(0, 1))  21.4 us
    all_to_all x1, blocking collectives, seq_exchange(): return lax.all_to_all(x, 'seq', split_axis=0, concat_axis=0, tiled=True)  10.6 us
    pallas_call x1, Pallas kernels, shards(): pl.pallas_call(functools.partial(key_value_kernel, per), out_shape=(jax.S...  10.6 us
    all_to_all x1, waiting for transfers between devices, shards(): lax.all_to_all(grad_context, 'head', split_axis=1, concat_axis=0, tiled=T...  10 us
  transfers between devices with their start and end apart: 38, of which 12 were waited for; matrix products, arithmetic and copies ran while one was open for 5% of the time, Pallas kernels for 11%

profile of v5, /device:TPU:1, one launch (start us, length us, event | category | flops | bytes accessed | tf_op | source)
XLA Modules:
  0.0 267.8 jit_solution(1137707022183401499)
XLA Ops:
  2.8 6.8 %all-to-all-start = ((bf16[384,8,128]{2,0,1:T(8,128)(2,1)}), bf16[384,8,128]{2,0,1:T(8,128)(2,1)S(1)}, u32[]{:S(2)}, u32[]{:S(2)}) async-start(bf16[384,8,128]{2,0,1:T(8,128)(2,1)} %copy_bitcast_fusion), calls=%async_computation | async-start | bytes 1572864 | tf_op jit(solution)/shard_map/all_to_all | solution.py:468
  11.9 10.0 %all-to-all-done = bf16[384,8,128]{2,0,1:T(8,128)(2,1)S(1)} async-done(((bf16[384,8,128]{2,0,1:T(8,128)(2,1)}), bf16[384,8,128]{2,0,1:T(8,128)(2,1)S(1)}, u32[]{:S(2)}, u32[]{:S(2)}) %all-to-all-start) | async-done | bytes 786464 | tf_op jit(solution)/shard_map/all_to_all | solution.py:468
  24.6 6.9 %all-to-all-start.1 = ((bf16[16,912,128]{2,1,0:T(8,128)(2,1)}), bf16[16,912,128]{2,1,0:T(8,128)(2,1)}, u32[]{:S(2)}, u32[]{:S(2)}) async-start(bf16[16,912,128]{2,1,0:T(8,128)(2,1)} %copy-done.3), calls=%async_computation.1 | async-start | bytes 7471104 | tf_op jit(solution)/shard_map/all_to_all | solution.py:396
  34.8 14.8 %collective-permute-done.4.refs_8_ = bf16[384,1024]{1,0:T(8,128)(2,1)S(1)} collective-permute-done((bf16[384,1024]{1,0:T(8,128)(2,1)S(1)}, bf16[384,1024]{1,0:T(8,128)(2,1)S(1)}, u32[]{:S(2)}, u32[]{:S(2)}) %collective-permute-start.4) | collective-permute-done | bytes 786464 | tf_op jit(solution)/shard_map/ppermute | solution.py:417
  54.4 4.1 %collective-permute-done.5.refs_5_ = bf16[192,1024]{1,0:T(8,128)(2,1)S(1)} collective-permute-done((bf16[192,1024]{1,0:T(8,128)(2,1)S(1)}, bf16[192,1024]{1,0:T(8,128)(2,1)S(1)}, u32[]{:S(2)}, u32[]{:S(2)}) %collective-permute-start.5) | collective-permute-done | bytes 393248 | tf_op jit(solution)/shard_map/ppermute | solution.py:422
  78.5 11.8 %all-to-all-start.2 = ((bf16[16,896,128]{2,1,0:T(8,128)(2,1)}), bf16[16,896,128]{2,1,0:T(8,128)(2,1)}, u32[]{:S(2)}, u32[]{:S(2)}) async-start(bf16[16,896,128]{2,1,0:T(8,128)(2,1)} %copy-done.4), calls=%async_computation.2 | async-start | bytes 7340032 | tf_op jit(solution)/shard_map/all_to_all | solution.py:396
  92.0 4.3 %shard_map.123 = (bf16[3072,256]{1,0:T(8,128)(2,1)S(1)}, bf16[3072,1024]{1,0:T(8,128)(2,1)S(1)}) custom-call(s32[8]{0:T(128)S(1)} %get-tuple-element.149.source_ref, bf16[384,1024]{1,0:T(8,128)(2,1)S(1)} %copy-done.15, bf16[384,1024]{1,0:T(8,128)(2,1)} %collective-permute-done.refs_1_, bf16[384,1024]{1,0:T(8,128)(2,1)S(1)} %copy-done.11, ...), custom_call_target="tpu_custom_call" | custom-call | flops 1610612736 | bytes 12582912 | tf_op jit(solution)/shard_map/pallas_call | solution.py:502
  100.4 15.5 %collective-permute-done.13.refs_8_ = bf16[1024,384]{1,0:T(8,128)(2,1)S(1)} collective-permute-done((bf16[1024,384]{1,0:T(8,128)(2,1)}, bf16[1024,384]{1,0:T(8,128)(2,1)S(1)}, u32[]{:S(2)}, u32[]{:S(2)}) %collective-permute-start.13) | collective-permute-done | bytes 786464 | tf_op jit(solution)/shard_map/ppermute | solution.py:417
  129.9 4.0 %collective-permute-start.15 = (bf16[512,384]{1,0:T(8,128)(2,1)}, bf16[512,384]{1,0:T(8,128)(2,1)}, u32[]{:S(2)}, u32[]{:S(2)}) collective-permute-start(bf16[512,384]{1,0:T(8,128)(2,1)} %collective-permute-done.12.refs_4_), channel_id=1, source_target_pairs={{0,1},{1,0},{2,3},{3,2},{4,5},{5,4},{6,7},{7,6},{8,9},{9,8},{10,11... | collective-permute-start | bytes 1179656 | tf_op jit(solution)/shard_map/ppermute | solution.py:427
  136.1 7.5 %shard_map.125 = f32[112,4,128]{2,1,0:T(4,128)} custom-call(s32[1]{0:T(128)} %bitcast.3.count_ref, s32[112]{0:T(128)S(1)} %select_reduce_fusion.order_ref, s32[112]{0:T(128)S(1)} %reshape.259.meta_ref, bf16[16,896,128]{2,1,0:T(8,128)(2,1)} %all-to-all-done.2.query_ref.far_query_ref, bf16[16,912,128]{2,1,0:T(8,128)(2,1)} %all-to-all-done.1.grad_ref.far_grad_ref, ...), custom_call_target="tpu_custom_call" | custom-call | flops 1879048192 | bytes 7340032 | tf_op jit(solution)/shard_map/pallas_call | solution.py:531
  143.6 6.6 %all-to-all-start.3 = ((f32[112,4,128]{2,1,0:T(4,128)}), f32[112,4,128]{2,1,0:T(4,128)S(1)}, u32[]{:S(2)}, u32[]{:S(2)}) async-start(f32[112,4,128]{2,1,0:T(4,128)} %shard_map.125), calls=%async_computation.3 | async-start | bytes 458752 | tf_op jit(solution)/shard_map/all_to_all | solution.py:396
  153.0 4.3 %all-to-all-done.3.far_ref = f32[112,4,128]{2,1,0:T(4,128)S(1)} async-done(((f32[112,4,128]{2,1,0:T(4,128)}), f32[112,4,128]{2,1,0:T(4,128)S(1)}, u32[]{:S(2)}, u32[]{:S(2)}) %all-to-all-start.3) | async-done | bytes 229408 | tf_op jit(solution)/shard_map/all_to_all | solution.py:396
  158.8 10.6 %all_to_all.46.far_stats_ref.stats_ref = f32[112,4,128]{2,1,0:T(4,128)S(1)} all-to-all(f32[112,4,128]{2,1,0:T(4,128)S(1)} %get-tuple-element.86), channel_id=1, replica_groups=mesh['seq'=16,'head'=8] {'seq'}, dimensions={0} | all-to-all | bytes 458752 | tf_op jit(solution)/shard_map/all_to_all | solution.py:396
  169.4 7.1 %shard_map.128 = bf16[112,128,128]{2,1,0:T(8,128)(2,1)S(1)} custom-call(s32[1]{0:T(128)} %bitcast.3.count_ref, s32[112]{0:T(128)S(1)} %select_reduce_fusion.order_ref, s32[112]{0:T(128)S(1)} %reshape.259.meta_ref, bf16[16,896,128]{2,1,0:T(8,128)(2,1)} %all-to-all-done.2.query_ref.far_query_ref, bf16[16,912,128]{2,1,0:T(8,128)(2,1)} %all-to-all-done.1.grad_ref.far_grad_ref, ...), custom_call_target="tpu_custom_call" | custom-call | flops 2818572288 | bytes 11010048 | tf_op jit(solution)/shard_map/pallas_call | solution.py:550
  178.4 4.6 %all-to-all-start.5 = ((bf16[112,128,128]{2,1,0:T(8,128)(2,1)}), bf16[112,128,128]{2,1,0:T(8,128)(2,1)}, u32[]{:S(2)}, u32[]{:S(2)}) async-start(bf16[112,128,128]{2,1,0:T(8,128)(2,1)} %copy-done.5), calls=%async_computation.5 | async-start | bytes 7340032 | tf_op jit(solution)/shard_map/all_to_all | solution.py:396
  183.9 10.6 %shard_map.127 = (f32[24,128,128]{2,1,0:T(8,128)S(1)}, bf16[3072,256]{1,0:T(8,128)(2,1)S(1)}, bf16[384,256]{1,0:T(8,128)(2,1)S(1)}, bf16[384,256]{1,0:T(8,128)(2...) custom-call(s32[8]{0:T(128)S(1)} %fusion.9.target_ref, ...), custom_call_target="tpu_custom_call" | custom-call | flops 4697620480 | bytes 11010048 | tf_op jit(solution)/shard_map/pallas_call | solution.py:570
  195.8 3.9 %collective-permute-start.18 = (bf16[384,256]{1,0:T(8,128)(2,1)S(1)}, bf16[384,256]{1,0:T(8,128)(2,1)S(1)}, u32[]{:S(2)}, u32[]{:S(2)}) collective-permute-start(bf16[384,256]{1,0:T(8,128)(2,1)S(1)} %get-tuple-element.113), channel_id=1, source_target_pairs={{0,1},{1,0},{2,3},{3,2},{4,5},{5,4},{6,7},{7,6},{8,9},{9,8},{10,11... | collective-permute-start | bytes 589832 | tf_op jit(solution)/shard_map/ppermute | solution.py:434
  199.9 4.7 %collective-permute-start.20 = (bf16[384,256]{1,0:T(8,128)(2,1)S(1)}, bf16[384,256]{1,0:T(8,128)(2,1)S(1)}, u32[]{:S(2)}, u32[]{:S(2)}) collective-permute-start(bf16[384,256]{1,0:T(8,128)(2,1)S(1)} %get-tuple-element.115), channel_id=1, source_target_pairs={{0,3},{1,2},{2,5},{3,4},{4,7},{5,6},{6,1},{7,0},{8,11},{9,10},{10,... | collective-permute-start | bytes 589832 | tf_op jit(solution)/shard_map/ppermute | solution.py:434
  211.0 5.5 %convolution_convert_fusion = bf16[1024,256]{1,0:T(8,128)(2,1)} fusion(bf16[3072,1024]{1,0:T(8,128)(2,1)} %copy-done.9, bf16[3072,256]{1,0:T(8,128)(2,1)S(1)} %get-tuple-element.141), kind=kOutput, calls=%fused_computation.1 | convolution fusion | flops 1610874880 | bytes 8388608 | tf_op jit(solution)/shard_map/dot_general | solution.py:613
  225.1 4.2 %shard_map.130 = (bf16[3072,128]{1,0:T(8,128)(2,1)}, bf16[384,128]{1,0:T(8,128)(2,1)}, bf16[384,128]{1,0:T(8,128)(2,1)}, bf16[384,128]{1,0:T(8,128)(2,1)}, bf16[...) custom-call(s32[8]{0:T(128)} %copy-done.35, ...), custom_call_target="tpu_custom_call" | custom-call | bytes 3670016 | tf_op jit(solution)/shard_map/pallas_call | solution.py:626
  229.2 4.8 %convolution_convert_fusion.1 = bf16[1024,128]{1,0:T(8,128)(2,1)S(1)} fusion(bf16[3072,1024]{1,0:T(8,128)(2,1)} %copy-done.9, bf16[3072,128]{1,0:T(8,128)(2,1)} %get-tuple-element.140), kind=kOutput, calls=%fused_computation.2 | convolution fusion | flops 805437440 | bytes 7340032 | tf_op jit(solution)/shard_map/dot_general | solution.py:635
  235.2 8.7 %all-to-all-start.6 = ((bf16[16,64,384]{2,1,0:T(8,128)(2,1)}), bf16[16,64,384]{2,1,0:T(8,128)(2,1)}, u32[]{:S(2)}, u32[]{:S(2)}) async-start(bf16[16,64,384]{2,1,0:T(8,128)(2,1)} %pad_maximum_fusion.1), calls=%async_computation.6 | async-start | bytes 1572864 | tf_op jit(solution)/shard_map/all_to_all | solution.py:396
  243.9 4.0 %collective-permute-start.25 = (bf16[384,128]{1,0:T(8,128)(2,1)}, bf16[384,128]{1,0:T(8,128)(2,1)S(1)}, u32[]{:S(2)}, u32[]{:S(2)}) collective-permute-start(bf16[384,128]{1,0:T(8,128)(2,1)} %get-tuple-element.122), channel_id=1, source_target_pairs={{0,1},{1,0},{2,3},{3,2},{4,5},{5,4},{6,7},{7,6},{8,9},{9,8},{10,11... | collective-permute-start | bytes 294920 | tf_op jit(solution)/shard_map/ppermute | solution.py:434
  248.6 4.4 %collective-permute-start.27 = (bf16[384,128]{1,0:T(8,128)(2,1)}, bf16[384,128]{1,0:T(8,128)(2,1)S(1)}, u32[]{:S(2)}, u32[]{:S(2)}) collective-permute-start(bf16[384,128]{1,0:T(8,128)(2,1)} %get-tuple-element.124), channel_id=1, source_target_pairs={{0,3},{1,2},{2,5},{3,4},{4,7},{5,6},{6,1},{7,0},{8,11},{9,10},{10,... | collective-permute-start | bytes 294920 | tf_op jit(solution)/shard_map/ppermute | solution.py:434
  (193 shorter events, 96.5 us)
Async XLA Ops:
  2.8 19.1 %all-to-all-start = ((bf16[384,8,128]{2,0,1:T(8,128)(2,1)}), bf16[384,8,128]{2,0,1:T(8,128)(2,1)S(1)}, u32[]{:S(2)}, u32[]{:S(2)}) async-start(bf16[384,8,128]{2,0,1:T(8,128)(2,1)} %copy_bitcast_fusion), calls=%async_computation | async-start | bytes 1572864 | tf_op jit(solution)/shard_map/all_to_all | solution.py:468
  24.6 53.8 %all-to-all-start.1 = ((bf16[16,912,128]{2,1,0:T(8,128)(2,1)}), bf16[16,912,128]{2,1,0:T(8,128)(2,1)}, u32[]{:S(2)}, u32[]{:S(2)}) async-start(bf16[16,912,128]{2,1,0:T(8,128)(2,1)} %copy-done.3), calls=%async_computation.1 | async-start | bytes 7471104 | tf_op jit(solution)/shard_map/all_to_all | solution.py:396
  31.6 18.1 %collective-permute-start.4 = (bf16[384,1024]{1,0:T(8,128)(2,1)S(1)}, bf16[384,1024]{1,0:T(8,128)(2,1)S(1)}, u32[]{:S(2)}, u32[]{:S(2)}) collective-permute-start(bf16[384,1024]{1,0:T(8,128)(2,1)S(1)} %copy-done.14), channel_id=1, source_target_pairs={{0,6},{1,7},{2,0},{3,1},{4,2},{5,3},{6,4},{7,5},{8,14},{9,15},{10,... | collective-permute-start | bytes 2359304 | tf_op jit(solution)/shard_map/ppermute | solution.py:417
  32.5 19.3 %collective-permute-start.1 = (bf16[384,1024]{1,0:T(8,128)(2,1)S(1)}, bf16[384,1024]{1,0:T(8,128)(2,1)S(1)}, u32[]{:S(2)}, u32[]{:S(2)}) collective-permute-start(bf16[384,1024]{1,0:T(8,128)(2,1)S(1)} %copy-done.14), channel_id=1, source_target_pairs={{0,2},{1,3},{2,4},{3,5},{4,6},{5,7},{6,0},{7,1},{8,10},{9,11},{10,... | collective-permute-start | bytes 2359304 | tf_op jit(solution)/shard_map/ppermute | solution.py:416
  33.1 32.9 %collective-permute-start = (bf16[384,1024]{1,0:T(8,128)(2,1)S(1)}, bf16[384,1024]{1,0:T(8,128)(2,1)}, u32[]{:S(2)}, u32[]{:S(2)}) collective-permute-start(bf16[384,1024]{1,0:T(8,128)(2,1)S(1)} %copy-done.14), channel_id=1, source_target_pairs={{0,1},{1,0},{2,3},{3,2},{4,5},{5,4},{6,7},{7,6},{8,9},{9,8},{10,11... | collective-permute-start | bytes 2359304 | tf_op jit(solution)/shard_map/ppermute | solution.py:427
  52.0 14.0 %collective-permute-start.8 = (bf16[384,1024]{1,0:T(8,128)(2,1)S(1)}, bf16[384,1024]{1,0:T(8,128)(2,1)}, u32[]{:S(2)}, u32[]{:S(2)}) collective-permute-start(bf16[384,1024]{1,0:T(8,128)(2,1)S(1)} %collective-permute-done.4.refs_8_), channel_id=1, source_target_pairs={{0,1},{1,0},{2,3},{3,2},{4,5},{5,4},{6,7},{7,6},{8,9},{9,8},{10,11... | collective-permute-start | bytes 2359304 | tf_op jit(solution)/shard_map/ppermute | solution.py:427
  54.3 12.2 %collective-permute-start.2 = (bf16[384,1024]{1,0:T(8,128)(2,1)S(1)}, bf16[384,1024]{1,0:T(8,128)(2,1)}, u32[]{:S(2)}, u32[]{:S(2)}) collective-permute-start(bf16[384,1024]{1,0:T(8,128)(2,1)S(1)} %collective-permute-done.1.refs_2_), channel_id=1, source_target_pairs={{0,1},{1,0},{2,3},{3,2},{4,5},{5,4},{6,7},{7,6},{8,9},{9,8},{10,11... | collective-permute-start | bytes 2359304 | tf_op jit(solution)/shard_map/ppermute | solution.py:427
  78.5 57.6 %all-to-all-start.2 = ((bf16[16,896,128]{2,1,0:T(8,128)(2,1)}), bf16[16,896,128]{2,1,0:T(8,128)(2,1)}, u32[]{:S(2)}, u32[]{:S(2)}) async-start(bf16[16,896,128]{2,1,0:T(8,128)(2,1)} %copy-done.4), calls=%async_computation.2 | async-start | bytes 7340032 | tf_op jit(solution)/shard_map/all_to_all | solution.py:396
  98.9 17.0 %collective-permute-start.13 = (bf16[1024,384]{1,0:T(8,128)(2,1)}, bf16[1024,384]{1,0:T(8,128)(2,1)S(1)}, u32[]{:S(2)}, u32[]{:S(2)}) collective-permute-start(bf16[1024,384]{1,0:T(8,128)(2,1)} %pad_maximum_fusion.refs_0_), channel_id=1, source_target_pairs={{0,6},{1,7},{2,0},{3,1},{4,2},{5,3},{6,4},{7,5},{8,14},{9,15},{10,... | collective-permute-start | bytes 2359304 | tf_op jit(solution)/shard_map/ppermute | solution.py:417
  99.8 20.2 %collective-permute-start.10 = (bf16[1024,384]{1,0:T(8,128)(2,1)}, bf16[1024,384]{1,0:T(8,128)(2,1)}, u32[]{:S(2)}, u32[]{:S(2)}) collective-permute-start(bf16[1024,384]{1,0:T(8,128)(2,1)} %pad_maximum_fusion.refs_0_), channel_id=1, source_target_pairs={{0,2},{1,3},{2,4},{3,5},{4,6},{5,7},{6,0},{7,1},{8,10},{9,11},{10,... | collective-permute-start | bytes 2359304 | tf_op jit(solution)/shard_map/ppermute | solution.py:416
  121.2 14.8 %collective-permute-start.9 = (bf16[1024,384]{1,0:T(8,128)(2,1)}, bf16[1024,384]{1,0:T(8,128)(2,1)}, u32[]{:S(2)}, u32[]{:S(2)}) collective-permute-start(bf16[1024,384]{1,0:T(8,128)(2,1)} %pad_maximum_fusion.refs_0_), channel_id=1, source_target_pairs={{0,1},{1,0},{2,3},{3,2},{4,5},{5,4},{6,7},{7,6},{8,9},{9,8},{10,11... | collective-permute-start | bytes 2359304 | tf_op jit(solution)/shard_map/ppermute | solution.py:427
  124.5 11.5 %collective-permute-start.17 = (bf16[1024,384]{1,0:T(8,128)(2,1)S(1)}, bf16[1024,384]{1,0:T(8,128)(2,1)}, u32[]{:S(2)}, u32[]{:S(2)}) collective-permute-start(bf16[1024,384]{1,0:T(8,128)(2,1)S(1)} %collective-permute-done.13.refs_8_), channel_id=1, source_target_pairs={{0,1},{1,0},{2,3},{3,2},{4,5},{5,4},{6,7},{7,6},{8,9},{9,8},{10,11... | collective-permute-start | bytes 2359304 | tf_op jit(solution)/shard_map/ppermute | solution.py:427
  124.6 11.4 %collective-permute-start.11 = (bf16[1024,384]{1,0:T(8,128)(2,1)}, bf16[1024,384]{1,0:T(8,128)(2,1)}, u32[]{:S(2)}, u32[]{:S(2)}) collective-permute-start(bf16[1024,384]{1,0:T(8,128)(2,1)} %collective-permute-done.10.refs_2_), channel_id=1, source_target_pairs={{0,1},{1,0},{2,3},{3,2},{4,5},{5,4},{6,7},{7,6},{8,9},{9,8},{10,11... | collective-permute-start | bytes 2359304 | tf_op jit(solution)/shard_map/ppermute | solution.py:427
  143.6 13.7 %all-to-all-start.3 = ((f32[112,4,128]{2,1,0:T(4,128)}), f32[112,4,128]{2,1,0:T(4,128)S(1)}, u32[]{:S(2)}, u32[]{:S(2)}) async-start(f32[112,4,128]{2,1,0:T(4,128)} %shard_map.125), calls=%async_computation.3 | async-start | bytes 458752 | tf_op jit(solution)/shard_map/all_to_all | solution.py:396
  178.4 46.7 %all-to-all-start.5 = ((bf16[112,128,128]{2,1,0:T(8,128)(2,1)}), bf16[112,128,128]{2,1,0:T(8,128)(2,1)}, u32[]{:S(2)}, u32[]{:S(2)}) async-start(bf16[112,128,128]{2,1,0:T(8,128)(2,1)} %copy-done.5), calls=%async_computation.5 | async-start | bytes 7340032 | tf_op jit(solution)/shard_map/all_to_all | solution.py:396
  195.8 12.3 %collective-permute-start.18 = (bf16[384,256]{1,0:T(8,128)(2,1)S(1)}, bf16[384,256]{1,0:T(8,128)(2,1)S(1)}, u32[]{:S(2)}, u32[]{:S(2)}) collective-permute-start(bf16[384,256]{1,0:T(8,128)(2,1)S(1)} %get-tuple-element.113), channel_id=1, source_target_pairs={{0,1},{1,0},{2,3},{3,2},{4,5},{5,4},{6,7},{7,6},{8,9},{9,8},{10,11... | collective-permute-start | bytes 589832 | tf_op jit(solution)/shard_map/ppermute | solution.py:434
  199.9 22.4 %collective-permute-start.20 = (bf16[384,256]{1,0:T(8,128)(2,1)S(1)}, bf16[384,256]{1,0:T(8,128)(2,1)S(1)}, u32[]{:S(2)}, u32[]{:S(2)}) collective-permute-start(bf16[384,256]{1,0:T(8,128)(2,1)S(1)} %get-tuple-element.115), channel_id=1, source_target_pairs={{0,3},{1,2},{2,5},{3,4},{4,7},{5,6},{6,1},{7,0},{8,11},{9,10},{10,... | collective-permute-start | bytes 589832 | tf_op jit(solution)/shard_map/ppermute | solution.py:434
  204.7 17.6 %collective-permute-start.21 = (bf16[384,256]{1,0:T(8,128)(2,1)S(1)}, bf16[384,256]{1,0:T(8,128)(2,1)S(1)}, u32[]{:S(2)}, u32[]{:S(2)}) collective-permute-start(bf16[384,256]{1,0:T(8,128)(2,1)S(1)} %get-tuple-element.116), channel_id=1, source_target_pairs={{0,4},{1,5},{2,6},{3,7},{4,0},{5,1},{6,2},{7,3},{8,12},{9,13},{10,... | collective-permute-start | bytes 589832 | tf_op jit(solution)/shard_map/ppermute | solution.py:434
  204.8 18.2 %collective-permute-start.22 = (bf16[384,256]{1,0:T(8,128)(2,1)S(1)}, bf16[384,256]{1,0:T(8,128)(2,1)S(1)}, u32[]{:S(2)}, u32[]{:S(2)}) collective-permute-start(bf16[384,256]{1,0:T(8,128)(2,1)S(1)} %get-tuple-element.117), channel_id=1, source_target_pairs={{0,5},{1,4},{2,7},{3,6},{4,1},{5,0},{6,3},{7,2},{8,13},{9,12},{10,... | collective-permute-start | bytes 589832 | tf_op jit(solution)/shard_map/ppermute | solution.py:434
  208.1 15.7 %collective-permute-start.23 = (bf16[384,256]{1,0:T(8,128)(2,1)S(1)}, bf16[384,256]{1,0:T(8,128)(2,1)S(1)}, u32[]{:S(2)}, u32[]{:S(2)}) collective-permute-start(bf16[384,256]{1,0:T(8,128)(2,1)S(1)} %get-tuple-element.118), channel_id=1, source_target_pairs={{0,6},{1,7},{2,0},{3,1},{4,2},{5,3},{6,4},{7,5},{8,14},{9,15},{10,... | collective-permute-start | bytes 589832 | tf_op jit(solution)/shard_map/ppermute | solution.py:434
  208.1 16.3 %collective-permute-start.24 = (bf16[384,256]{1,0:T(8,128)(2,1)S(1)}, bf16[384,256]{1,0:T(8,128)(2,1)S(1)}, u32[]{:S(2)}, u32[]{:S(2)}) collective-permute-start(bf16[384,256]{1,0:T(8,128)(2,1)S(1)} %get-tuple-element.119), channel_id=1, source_target_pairs={{0,7},{1,6},{2,1},{3,0},{4,3},{5,2},{6,5},{7,4},{8,15},{9,14},{10,... | collective-permute-start | bytes 589832 | tf_op jit(solution)/shard_map/ppermute | solution.py:434
  235.2 30.8 %all-to-all-start.6 = ((bf16[16,64,384]{2,1,0:T(8,128)(2,1)}), bf16[16,64,384]{2,1,0:T(8,128)(2,1)}, u32[]{:S(2)}, u32[]{:S(2)}) async-start(bf16[16,64,384]{2,1,0:T(8,128)(2,1)} %pad_maximum_fusion.1), calls=%async_computation.6 | async-start | bytes 1572864 | tf_op jit(solution)/shard_map/all_to_all | solution.py:396
  243.9 12.4 %collective-permute-start.25 = (bf16[384,128]{1,0:T(8,128)(2,1)}, bf16[384,128]{1,0:T(8,128)(2,1)S(1)}, u32[]{:S(2)}, u32[]{:S(2)}) collective-permute-start(bf16[384,128]{1,0:T(8,128)(2,1)} %get-tuple-element.122), channel_id=1, source_target_pairs={{0,1},{1,0},{2,3},{3,2},{4,5},{5,4},{6,7},{7,6},{8,9},{9,8},{10,11... | collective-permute-start | bytes 294920 | tf_op jit(solution)/shard_map/ppermute | solution.py:434
  248.6 13.8 %collective-permute-start.27 = (bf16[384,128]{1,0:T(8,128)(2,1)}, bf16[384,128]{1,0:T(8,128)(2,1)S(1)}, u32[]{:S(2)}, u32[]{:S(2)}) collective-permute-start(bf16[384,128]{1,0:T(8,128)(2,1)} %get-tuple-element.124), channel_id=1, source_target_pairs={{0,3},{1,2},{2,5},{3,4},{4,7},{5,6},{6,1},{7,0},{8,11},{9,10},{10,... | collective-permute-start | bytes 294920 | tf_op jit(solution)/shard_map/ppermute | solution.py:434
  (58 other events, 578.2 us)
